TPU v7x, 32 devices: a whole 2x2x4 slice. The times are simulated.
32 devices in a mesh: face: 4 (over y, x), tile: 8 (over z, core).
Axes of the slice: x: 2, y: 2, z: 4, core: 2. Of those that a mesh axis runs over, the one named last changes fastest.
Arguments:
- fields: bfloat16 [4, 64, 128, 256], P('face', 'tile'), may hold values from -6 to 6
- cotangent: bfloat16 [4, 64, 128, 256], P('face', 'tile'), may hold values from -6 to 6
- edge_match: int32 [4, 2, 3], replicated, may hold values from 0 to 3, as said below
- depth_kernel: bfloat16 [7, 7, 256], replicated, may hold values from -0.875 to 0.875
- depth_bias: float32 [256], replicated, may hold values from -3 to 3
- norm_gain: float32 [256], replicated, may hold values from 0.5 to 1.5
- norm_bias: float32 [256], replicated, may hold values from -3 to 3
- expand_weight: bfloat16 [256, 1024], replicated, may hold values from -0.375 to 0.375
- expand_bias: float32 [1024], replicated, may hold values from -3 to 3
- reduce_weight: bfloat16 [1024, 256], replicated, may hold values from -0.1875 to 0.1875
- reduce_bias: float32 [256], replicated, may hold values from -3 to 3
- layer_scale: float32 [256], replicated, may hold values from 0.5 to 1.5
Outputs:
- result: bfloat16 [4, 64, 128, 256], P('face', 'tile')
- grad_fields: bfloat16 [4, 64, 128, 256], P('face', 'tile')
- grad_kernel: float32 [7, 7, 256], replicated
- grad_expand: float32 [256, 1024], replicated
- grad_reduce: float32 [1024, 256], replicated
- grad_expand_bias: float32 [1024], replicated
- grad_vectors: float32 [5, 256], replicated
Inputs may be any that keep to these rules, and one draw needn't show every extreme that they name: edge_match[f, s] = (g, s2, r): side s of strip f is glued to side s2 of strip g, rows reversed where r is 1; the gluing is symmetric; one side of strip f is glued to strip f XOR 1, the other to strip (f + 2) mod 4; at least one glued pair has reversed rows and at least one has not.
All inputs are finite; a program needn't handle non-finite values.
Results may differ from a plain program's by a relative error of at most 0.0067.
Values may be sent and summed in bfloat16 or wider, within the bound.
No kernel may reach another device: no remote copies, remote signals or barrier semaphores. Data moves between devices by JAX's collectives and lax.ppermute only.
A program may use at most 64 MiB of HBM per device.

v0:
```python
import math

import jax
import jax.numpy as jnp
from jax import lax
from jax.sharding import PartitionSpec as P

EPSILON = 1e-06
ROOT_COEF = 0.7978845608028654
CUBIC_COEF = 0.044715


def swapped(x, axis, stride):
    return lax.ppermute(x, axis, [(i, i ^ 1 << stride) for i in range(lax.axis_size(axis))])


def padded_2(cells, sides, width):
    for axis, dim in sides:
        count = lax.axis_size(axis)
        ends = count - 1
        head = lax.slice_in_dim(cells, 0, width, axis=dim)
        tail = lax.slice_in_dim(cells, cells.shape[dim] - width, cells.shape[dim], axis=dim)
        cells = jnp.concatenate(
            [
                lax.ppermute(tail, axis, [(i, (i + 1) % count) for i in range(ends)]),
                cells,
                lax.ppermute(head, axis, [((i + 1) % count, i) for i in range(ends)]),
            ],
            axis=dim,
        )
    return cells


def gelu_pair(preact):
    argument = ROOT_COEF * (preact + CUBIC_COEF * preact * preact * preact)
    tanhed = jnp.tanh(argument)
    gelu_value = 0.5 * preact * (1.0 + tanhed)
    gelu_slope = 0.5 * (1.0 + tanhed) + 0.5 * preact * (1.0 - tanhed * tanhed) * ROOT_COEF * (
        1.0 + 3.0 * CUBIC_COEF * preact * preact
    )
    return (gelu_value, gelu_slope)


def contract_rows(left_side, right_side):
    return lax.dot_general(
        left_side, right_side, (((0,), (0,)), ((), ())), preferred_element_type=jnp.float32
    )


def contract_cols(left_side, right_side):
    return lax.dot_general(
        left_side, right_side, (((1,), (1,)), ((), ())), preferred_element_type=jnp.float32
    )


def block_pass(
    padded,
    face_grid,
    face_cot,
    kernel,
    depth_bias,
    norm_gain,
    norm_bias,
    expand_weight,
    expand_bias,
    reduce_weight,
    reduce_bias,
    layer_scale,
):
    row_count, col_count, channels = face_grid.shape
    kernel_size = kernel.shape[0]
    convolved = jnp.zeros((row_count, col_count, channels), jnp.float32) + depth_bias
    for row_off in range(kernel_size):
        for col_off in range(kernel_size):
            convolved = (
                convolved
                + kernel[row_off, col_off]
                * padded[row_off : row_off + row_count, col_off : col_off + col_count]
            )
    average = jnp.mean(convolved, axis=-1, keepdims=True)
    centred = convolved - average
    inverse = lax.rsqrt(jnp.mean(centred * centred, axis=-1, keepdims=True) + EPSILON)
    standard = centred * inverse
    normed = (
        (standard * norm_gain + norm_bias)
        .astype(jnp.bfloat16)
        .reshape(row_count * col_count, channels)
    )
    preact = jnp.dot(normed, expand_weight, preferred_element_type=jnp.float32) + expand_bias
    gelu_value, gelu_slope = gelu_pair(preact)
    activated = gelu_value.astype(jnp.bfloat16)
    branch = jnp.dot(activated, reduce_weight, preferred_element_type=jnp.float32) + reduce_bias
    residual = face_grid.reshape(row_count * col_count, channels).astype(jnp.float32)
    result = (
        (residual + layer_scale * branch)
        .astype(jnp.bfloat16)
        .reshape(row_count, col_count, channels)
    )
    upstream = face_cot.reshape(row_count * col_count, channels).astype(jnp.float32)
    grad_branch = (upstream * layer_scale).astype(jnp.bfloat16)
    grad_pre = (contract_cols(grad_branch, reduce_weight) * gelu_slope).astype(jnp.bfloat16)
    grad_normed = contract_cols(grad_pre, expand_weight).reshape(row_count, col_count, channels)
    scaled = grad_normed * norm_gain
    grad_conv = (
        scaled
        - jnp.mean(scaled, axis=-1, keepdims=True)
        - standard * jnp.mean(scaled * standard, axis=-1, keepdims=True)
    ) * inverse
    dz_padded = jnp.pad(grad_conv, ((6, 6), (6, 6), (0, 0)))
    grad_padded = jnp.zeros((row_count + 6, col_count + 6, channels), jnp.float32)
    kernel_terms = []
    for row_off in range(kernel_size):
        for col_off in range(kernel_size):
            grad_padded = (
                grad_padded
                + kernel[row_off, col_off]
                * dz_padded[
                    6 - row_off : 12 - row_off + row_count, 6 - col_off : 12 - col_off + col_count
                ]
            )
            kernel_terms.append(
                jnp.sum(
                    grad_conv
                    * padded[row_off : row_off + row_count, col_off : col_off + col_count],
                    axis=(0, 1),
                )
            )
    grad_kernel = jnp.stack(kernel_terms).reshape(kernel_size, kernel_size, channels)
    grad_expand = contract_rows(normed, grad_pre)
    grad_reduce = contract_rows(activated, grad_branch)
    grad_expand_bias = jnp.sum(grad_pre.astype(jnp.float32), axis=0)
    vectors = jnp.stack(
        [
            jnp.sum(grad_conv, axis=(0, 1)),
            jnp.sum(grad_normed * standard, axis=(0, 1)),
            jnp.sum(grad_normed, axis=(0, 1)),
            jnp.sum(upstream, axis=0) * layer_scale,
            jnp.sum(upstream * branch, axis=0),
        ]
    )
    return (result, grad_padded, (grad_kernel, grad_expand, grad_reduce, grad_expand_bias, vectors))


def mirrored(strips, backward):
    tile_count = lax.axis_size("tile")
    carried = strips
    for bit_index in range(tile_count.bit_length() - 1):
        if backward:
            carried = swapped(carried.astype(jnp.bfloat16), "tile", bit_index).astype(carried.dtype)
        else:
            carried = swapped(carried, "tile", bit_index)
    return carried


def partner_strips(strips, edge_match, backward):
    flipped = mirrored(strips, backward)
    both_kinds = jnp.stack([strips, flipped])
    own_index = lax.axis_index("face")
    own_match = lax.dynamic_index_in_dim(edge_match, own_index, 0, keepdims=False)
    received = []
    if backward:
        gathered = lax.all_gather(
            both_kinds[None].astype(jnp.bfloat16), "face", axis=0, tiled=True
        ).astype(jnp.float32)
    else:
        gathered = lax.all_gather(both_kinds[None], "face", axis=0, tiled=True)
    stacked_all = gathered.reshape((-1,) + gathered.shape[3:])
    for edge_side in range(2):
        partner = own_match[edge_side, 0]
        other_side = own_match[edge_side, 1]
        reverse_flag = own_match[edge_side, 2]
        picked_strip = lax.dynamic_index_in_dim(
            stacked_all, (partner * 2 + reverse_flag) * 2 + other_side, 0, keepdims=False
        )
        received.append(jnp.where(reverse_flag == 1, jnp.flip(picked_strip, 0), picked_strip))
    return received


def widen(tile_band, edge_match):
    col_count = tile_band.shape[1]
    strips = jnp.stack([tile_band[:, 0:3], jnp.flip(tile_band[:, col_count - 3 :], 1)])
    west_side, east_side = partner_strips(strips, edge_match, False)
    widened = jnp.concatenate([jnp.flip(west_side, 1), tile_band, east_side], axis=1)
    return padded_2(widened, (("tile", 0),), 3)


def fold_back(grad_padded, edge_match):
    row_count = grad_padded.shape[0] - 6
    col_count = grad_padded.shape[1] - 6
    rim_rows = jnp.concatenate([grad_padded[0:3], grad_padded[row_count + 3 :]], axis=0)
    arrived = padded_2(rim_rows.astype(jnp.bfloat16), (("tile", 0),), 3).astype(rim_rows.dtype)
    middle = grad_padded[3 : row_count + 3]
    middle = middle.at[0:3].add(arrived[0:3])
    middle = middle.at[row_count - 3 :].add(arrived[9:12])
    west_ghost = jnp.flip(middle[:, 0:3], 1)
    east_ghost = middle[:, col_count + 3 :]
    west_back, east_back = partner_strips(jnp.stack([west_ghost, east_ghost]), edge_match, True)
    interior = middle[:, 3 : col_count + 3]
    interior = interior.at[:, 0:3].add(west_back)
    interior = interior.at[:, col_count - 3 :].add(jnp.flip(east_back, 1))
    return interior


def shards(
    fields,
    cotangent,
    edge_match,
    depth_kernel,
    depth_bias,
    norm_gain,
    norm_bias,
    expand_weight,
    expand_bias,
    reduce_weight,
    reduce_bias,
    layer_scale,
):
    tile_band = fields[0]
    row_count, col_count, channels = tile_band.shape
    padded = widen(tile_band, edge_match).astype(jnp.float32)
    result, grad_padded, terms = block_pass(
        padded,
        tile_band,
        cotangent[0],
        depth_kernel.astype(jnp.float32),
        depth_bias,
        norm_gain,
        norm_bias,
        expand_weight,
        expand_bias,
        reduce_weight,
        reduce_bias,
        layer_scale,
    )
    interior = fold_back(grad_padded, edge_match)
    grad_fields = (cotangent[0].astype(jnp.float32) + interior).astype(jnp.bfloat16)
    grad_kernel, grad_expand, grad_reduce, grad_expand_bias, vectors = terms
    grad_kernel, grad_expand, grad_reduce, grad_expand_bias, vectors = lax.psum(
        (grad_kernel, grad_expand, grad_reduce, grad_expand_bias, vectors), ("face", "tile")
    )
    cell_total = lax.axis_size("face") * lax.axis_size("tile") * row_count * col_count
    factor = 1.0 / math.sqrt(cell_total)
    return (
        result[None],
        grad_fields[None],
        grad_kernel * factor,
        grad_expand * factor,
        grad_reduce * factor,
        grad_expand_bias * factor,
        vectors * factor,
    )


def solution(mesh):
    return jax.shard_map(
        shards,
        mesh=mesh,
        in_specs=(
            P("face", "tile", None, None),
            P("face", "tile", None, None),
            P(),
            P(),
            P(),
            P(),
            P(),
            P(),
            P(),
            P(),
            P(),
            P(),
        ),
        out_specs=(
            P("face", "tile", None, None),
            P("face", "tile", None, None),
            P(),
            P(),
            P(),
            P(),
            P(),
        ),
        check_vma=False,
    )
```

profile of v0, /device:TPU:0, one launch (start us, length us, event | category | flops | bytes accessed | tf_op | source)
XLA Modules:
  0.0 299.5 jit_solution(7611759808322394819)
XLA Ops:
  7.2 0.9 slice_bitcast_fusion.1
  8.3 0.5 collective-permute-start
  8.8 1.6 fusion.120
  10.5 1.7 fusion.121
  12.1 1.2 convert_reduce_fusion.1
  13.3 2.7 collective-permute-start.1
  16.0 0.8 constant_dynamic-slice_fusion.4
  16.8 1.2 collective-permute-done.1
  18.0 2.9 collective-permute-start.2
  20.9 0.6 fusion.123
  26.7 1.3 mul.1536
  28.1 8.7 %all-gather = bf16[8,2,8,3,256]{4,2,3,1,0:T(8,128)(2,1)S(1)} all-gather(bf16[2,2,8,3,256]{4,2,3,1,0:T(8,128)(2,1)S(1)} %copy.28), channel_id=2, replica_groups=mesh['face'=4,'tile'=8] {'face'}, dimensions={0}, use_global_device_ids=true | all-gather | bytes 245760 | tf_op jit(solution)/shard_map/all_gather | solution.py:166
  37.1 1.3 collective-permute-start.3
  38.4 1.3 collective-permute-start.4
  39.7 1.6 fusion.122
  41.3 2.3 collective-permute-done.4
  43.8 9.2 %fusion.117 = (f32[8,128]{1,0:T(8,128)S(1)}, f32[8,128,256]{2,1,0:T(8,128)S(1)}) fusion(f32[14,134,256]{2,1,0:T(8,128)S(1)} %maximum_convert_fusion, f32[256]{0:T(256)} %bitcast.286, f32[256]{0:T(256)} %bitcast.284, f32[256]{0:T(256)} %bitcast.282, f32[256]{0:T(256)} %bitcast.280, f32[256]{0:T(256)} %bitcast.278, f32[256]{0:T(256)} %bitcast.276, ...), kind=kLoop, calls=%fused_computation.271 | loop fusion | flops 25951232 | bytes 52484096 | tf_op jit(solution)/shard_map/reduce_sum | solution.py:80
  53.4 1.0 add_convert_fusion
  54.5 1.8 multiply_convert_fusion
  56.4 2.2 fusion.108
  58.6 1.7 fusion.125
  60.4 3.8 %convert_reduce_fusion = (f32[1024]{0:T(1024)}, bf16[1024,1024]{1,0:T(8,128)(2,1)S(1)}) fusion(f32[1024,1024]{1,0:T(8,128)S(1)} %get-tuple-element.199, f32[1024]{0:T(1024)S(1)} %copy-done.56, bf16[1024,256]{1,0:T(8,128)(2,1)S(1)} %get-tuple-element.134, bf16[1024,256]{1,0:T(8,128)(2,1)S(1)} %copy-done.55), kind=kOutput, calls=%fused_computation.58 | convolution fusion | flops 559938560 | bytes 7348224 | tf_op jit(solution)/shard_map/dot_general | solution.py:51
  64.2 1.3 copy-done.3
  65.5 1.7 fusion.124
  67.2 3.0 %fusion.114 = (f32[256]{0:T(256)}, f32[1024]{0:T(1024)S(1)}, f32[1024,256]{1,0:T(8,128)S(1)}) fusion(f32[256]{0:T(256)S(1)} %copy-done.7, bf16[1024,1024]{1,0:T(8,128)(2,1)} %copy-done.3, bf16[256,1024]{1,0:T(8,128)(2,1)S(1)} %copy-done), kind=kOutput, calls=%fused_computation.269 | convolution fusion | flops 537656064 | bytes 3676160 | tf_op jit(solution)/shard_map/dot_general | solution.py:51
  70.2 0.9 multiply_reduce_fusion
  71.2 3.6 %multiply_reduce_fusion.1 = (f32[256]{0:T(256)}, f32[256]{0:T(256)}, f32[256]{0:T(256)}, f32[256]{0:T(256)}, f32[256]{0:T(256)}, /*index=5*/f32[256]{0:T(256)}, ...) fusion(f32[14,134,256]{2,1,0:T(8,128)S(1)} %maximum_convert_fus, ...), kind=kLoop, calls=%fused_computation.169 | loop fusion | flops 11267584 | bytes 22055936 | tf_op jit(solution)/shard_map/reduce_sum | solution.py:122
  74.8 1.7 multiply_reduce_fusion.37
  76.9 2.5 multiply_reduce_fusion.19
  79.8 17.8 %fusion.115 = (bf16[14,134,256]{2,1,0:T(8,128)(2,1)S(1)}, f32[14,134,256]{2,1,0:T(8,128)}) fusion(f32[256]{0:T(256)} %bitcast.287, f32[256]{0:T(256)} %bitcast.285, f32[256]{0:T(256)} %bitcast.283, f32[256]{0:T(256)} %bitcast.281, f32[256]{0:T(256)S(1)} %bitcast.279, f32[256]{0:T(256)S(1)} %bitcast.277, f32[256]{0:T(256)S(1)} %bitcast.275, ...), kind=kLoop, calls=%fused_computation.270 | loop fusion | flops 47065088 | bytes 3980288 | tf_op jit(solution)/shard_map/convert.10
  97.7 2.8 stack.265
  100.5 1.3 slice.970
  101.9 6.2 %collective-permute-start.5 = (bf16[3,134,256]{2,1,0:T(8,128)(2,1)S(1)}, bf16[3,134,256]{2,1,0:T(8,128)(2,1)S(1)}, u32[]{:S(2)}, u32[]{:S(2)}) collective-permute-start(bf16[3,134,256]{2,1,0:T(8,128)(2,1)S(1)} %get-tuple-element.130), channel_id=1, source_target_pairs={{0,1},{1,2},{2,3},{3,4},{4,5},{5,6},{6,7},{8,9},{9,10},{10,11},{11... | collective-permute-start | bytes 617480 | tf_op jit(solution)/shard_map/ppermute | solution.py:25
  108.1 1.3 collective-permute-start.6
  109.4 41.1 %all-reduce.1 = (f32[7,7,256]{2,1,0:T(8,128)S(1)}, f32[1024]{0:T(1024)S(1)}, f32[5,256]{1,0:T(8,128)S(1)}) all-reduce(f32[7,7,256]{2,1,0:T(8,128)S(1)} %reshape.242, f32[1024]{0:T(1024)S(1)} %copy-done.50, f32[5,256]{1,0:T(8,128)S(1)} %stack.271), channel_id=1, replica_groups=mesh['face'=4,'tile'=8] {'face','tile'}, use_global_device_ids=true, to_apply=%region_53.54 | all-reduce | flops 14848 | bytes 118784 | tf_op jit(solution)/shard_map/psum | solution.py:238
  150.5 0.6 broadcast_multiply_fusion.2
  151.1 1.0 fusion.111
  152.6 0.6 broadcast_multiply_fusion.3
  153.2 0.6 collective-permute-done.7
  154.2 0.6 broadcast_multiply_fusion.4
  154.8 2.8 collective-permute-done.8
  157.7 0.5 collective-permute-start.9
  158.3 4.4 %collective-permute-done.9 = bf16[2,8,3,256]{3,2,1,0:T(4,128)(2,1)S(1)} collective-permute-done((bf16[2,8,3,256]{3,2,1,0:T(4,128)(2,1)S(1)}, bf16[2,8,3,256]{3,2,1,0:T(4,128)(2,1)S(1)}, u32[]{:S(2)}, u32[]{:S(2)}) %collective-permute-start.9) | collective-permute-done | bytes 24608 | tf_op jit(solution)/shard_map/ppermute | solution.py:14
  162.8 10.0 %all_gather.7 = bf16[4,2,2,8,3,256]{5,3,4,2,1,0:T(8,128)(2,1)S(1)} all-gather(bf16[1,2,2,8,3,256]{5,3,4,2,1,0:T(8,128)(2,1)S(1)} %copy.31), channel_id=1, replica_groups=mesh['face'=4,'tile'=8] {'face'}, dimensions={0}, use_global_device_ids=true | all-gather | bytes 245760 | tf_op jit(solution)/shard_map/all_gather | solution.py:162
  173.4 0.9 fusion.109
  174.4 114.8 %all-reduce.5.cloned.1.call-done = (f32[256,1024]{1,0:T(8,128)}, f32[1024,256]{1,0:T(8,128)}) async-done(((f32[256,1024]{1,0:T(8,128)}, f32[1024,256]{1,0:T(8,128)}), (f32[256,1024]{1,0:T(8,128)}, f32[1024,256]{1,0:T(8,128)})) %all-reduce.5.cloned.1.call-update) | async-done | bytes 2097168 | tf_op jit(solution)/shard_map/psum | solution.py:238
  289.1 2.4 broadcast_multiply_fusion
  291.5 1.1 broadcast_multiply_fusion.1
  (162 shorter events, 3.1 us)
Async XLA Ops:
  7.2 47.3 %copy-start = (bf16[256,1024]{1,0:T(8,128)(2,1)S(1)}, bf16[256,1024]{1,0:T(8,128)(2,1)}, u32[]{:S(2)}) copy-start(bf16[256,1024]{1,0:T(8,128)(2,1)} %param.27) | copy-start | bytes 1572868
  7.2 29.8 %copy-start.1 = (bf16[1,8,128,256]{3,2,1,0:T(8,128)(2,1)S(1)}, bf16[1,8,128,256]{3,2,1,0:T(8,128)(2,1)}, u32[]{:S(2)}) copy-start(bf16[1,8,128,256]{3,2,1,0:T(8,128)(2,1)} %param.20) | copy-start | bytes 1572868
  7.2 281.9 %all-reduce.5.cloned.1.call-start = ((), (), s32[]{:S(2)}) async-start(), calls=%async_computation | async-start | bytes 4194304 | tf_op jit(solution)/shard_map/psum | solution.py:238
  8.3 5.0 %collective-permute-start = (bf16[2,8,3,256]{3,2,1,0:T(4,128)(2,1)S(1)}, bf16[2,8,3,256]{3,2,1,0:T(4,128)(2,1)S(1)}, u32[]{:S(2)}, u32[]{:S(2)}) collective-permute-start(bf16[2,8,3,256]{3,2,1,0:T(4,128)(2,1)S(1)} %get-tuple-element.142), channel_id=1, source_target_pairs={{0,1},{1,0},{2,3},{3,2},{4,5},{5,4},{6,7},{7,6},{8,9},{9,8},{10,11... | collective-permute-start | bytes 73736 | tf_op jit(solution)/shard_map/ppermute | solution.py:14
  10.4 33.3 %copy-start.8 = (f32[1,1,256]{2,1,0:T(1,128)}, f32[1,1,256]{2,1,0:T(1,128)S(1)}, u32[]{:S(2)}) copy-start(f32[1,1,256]{2,1,0:T(1,128)S(1)} %get-tuple-element.148) | copy-start | bytes 3076
  13.3 4.7 %collective-permute-start.1 = (bf16[2,8,3,256]{3,2,1,0:T(4,128)(2,1)S(1)}, bf16[2,8,3,256]{3,2,1,0:T(4,128)(2,1)S(1)}, u32[]{:S(2)}, u32[]{:S(2)}) collective-permute-start(bf16[2,8,3,256]{3,2,1,0:T(4,128)(2,1)S(1)} %collective-permute-done), channel_id=1, source_target_pairs={{0,2},{1,3},{2,0},{3,1},{4,6},{5,7},{6,4},{7,5},{8,10},{9,11},{10,... | collective-permute-start | bytes 73736 | tf_op jit(solution)/shard_map/ppermute | solution.py:14
  18.0 10.0 %collective-permute-start.2 = (bf16[2,8,3,256]{3,2,1,0:T(4,128)(2,1)S(1)}, bf16[2,8,3,256]{3,2,1,0:T(4,128)(2,1)S(1)}, u32[]{:S(2)}, u32[]{:S(2)}) collective-permute-start(bf16[2,8,3,256]{3,2,1,0:T(4,128)(2,1)S(1)} %collective-permute-done.1), channel_id=1, source_target_pairs={{0,4},{1,5},{2,6},{3,7},{4,0},{5,1},{6,2},{7,3},{8,12},{9,13},{10,... | collective-permute-start | bytes 73736 | tf_op jit(solution)/shard_map/ppermute | solution.py:14
  37.1 4.2 %collective-permute-start.3 = (bf16[3,134,256]{2,1,0:T(8,128)(2,1)S(1)}, bf16[3,134,256]{2,1,0:T(8,128)(2,1)S(1)}, u32[]{:S(2)}, u32[]{:S(2)}) collective-permute-start(bf16[3,134,256]{2,1,0:T(8,128)(2,1)S(1)} %get-tuple-element.132), channel_id=1, source_target_pairs={{0,1},{1,2},{2,3},{3,4},{4,5},{5,6},{6,7},{8,9},{9,10},{10,11},{11... | collective-permute-start | bytes 617480 | tf_op jit(solution)/shard_map/ppermute | solution.py:25
  38.4 5.2 %collective-permute-start.4 = (bf16[3,134,256]{2,1,0:T(8,128)(2,1)S(1)}, bf16[3,134,256]{2,1,0:T(8,128)(2,1)S(1)}, u32[]{:S(2)}, u32[]{:S(2)}) collective-permute-start(bf16[3,134,256]{2,1,0:T(8,128)(2,1)S(1)} %get-tuple-element.133), channel_id=1, source_target_pairs={{1,0},{2,1},{3,2},{4,3},{5,4},{6,5},{7,6},{9,8},{10,9},{11,10},{12... | collective-permute-start | bytes 617480 | tf_op jit(solution)/shard_map/ppermute | solution.py:27
  43.8 9.6 %copy-start.7 = (f32[256]{0:T(256)S(1)}, f32[256]{0:T(256)}, u32[]{:S(2)}) copy-start(f32[256]{0:T(256)} %param.25) | copy-start | bytes 3076
  76.5 2.9 copy-start.9
  76.5 2.9 copy-start.10
  76.5 2.9 copy-start.11
  76.5 2.9 copy-start.12
  76.5 2.9 copy-start.13
  76.5 2.9 copy-start.14
  76.6 2.9 copy-start.15
  76.6 2.9 copy-start.16
  76.6 2.9 copy-start.17
  76.6 2.9 copy-start.18
  76.6 2.9 copy-start.19
  76.6 2.9 copy-start.20
  76.6 2.9 copy-start.21
  76.6 2.9 copy-start.22
  76.6 2.9 copy-start.23
  76.6 2.9 copy-start.24
  76.7 2.9 copy-start.25
  76.7 2.9 copy-start.26
  76.7 2.9 copy-start.27
  76.7 2.9 copy-start.28
  76.7 2.9 copy-start.29
  76.7 2.9 copy-start.30
  76.7 2.9 copy-start.31
  76.7 2.9 copy-start.32
  76.7 2.9 copy-start.33
  76.7 2.9 copy-start.34
  76.8 2.9 copy-start.35
  97.6 11.7 %copy-start.49 = (f32[256]{0:T(256)S(1)}, f32[256]{0:T(256)}, u32[]{:S(2)}) copy-start(f32[256]{0:T(256)} %get-tuple-element.111) | copy-start | bytes 3076
  97.6 11.8 %copy-start.51 = (f32[256]{0:T(256)S(1)}, f32[256]{0:T(256)}, u32[]{:S(2)}) copy-start(f32[256]{0:T(256)} %mul.1536) | copy-start | bytes 3076
  97.6 11.8 %copy-start.53 = (f32[256]{0:T(256)S(1)}, f32[256]{0:T(256)}, u32[]{:S(2)}) copy-start(f32[256]{0:T(256)} %get-tuple-element.128) | copy-start | bytes 3076
  97.6 11.8 %copy-start.54 = (f32[256]{0:T(256)S(1)}, f32[256]{0:T(256)}, u32[]{:S(2)}) copy-start(f32[256]{0:T(256)} %get-tuple-element.113) | copy-start | bytes 3076
  97.6 11.8 %copy-start.50 = (f32[1024]{0:T(1024)S(1)}, f32[1024]{0:T(1024)}, u32[]{:S(2)}) copy-start(f32[1024]{0:T(1024)} %get-tuple-element.201) | copy-start | bytes 12292
  101.9 49.3 %collective-permute-start.5 = (bf16[3,134,256]{2,1,0:T(8,128)(2,1)S(1)}, bf16[3,134,256]{2,1,0:T(8,128)(2,1)S(1)}, u32[]{:S(2)}, u32[]{:S(2)}) collective-permute-start(bf16[3,134,256]{2,1,0:T(8,128)(2,1)S(1)} %get-tuple-element.130), channel_id=1, source_target_pairs={{0,1},{1,2},{2,3},{3,4},{4,5},{5,6},{6,7},{8,9},{9,10},{10,11},{11... | collective-permute-start | bytes 617480 | tf_op jit(solution)/shard_map/ppermute | solution.py:25
  108.1 43.1 %collective-permute-start.6 = (bf16[3,134,256]{2,1,0:T(8,128)(2,1)S(1)}, bf16[3,134,256]{2,1,0:T(8,128)(2,1)S(1)}, u32[]{:S(2)}, u32[]{:S(2)}) collective-permute-start(bf16[3,134,256]{2,1,0:T(8,128)(2,1)S(1)} %get-tuple-element.131), channel_id=1, source_target_pairs={{1,0},{2,1},{3,2},{4,3},{5,4},{6,5},{7,6},{9,8},{10,9},{11,10},{12... | collective-permute-start | bytes 617480 | tf_op jit(solution)/shard_map/ppermute | solution.py:27
  152.5 1.3 collective-permute-start.7
  153.7 3.9 %collective-permute-start.8 = (bf16[2,8,3,256]{3,2,1,0:T(4,128)(2,1)S(1)}, bf16[2,8,3,256]{3,2,1,0:T(4,128)(2,1)S(1)}, u32[]{:S(2)}, u32[]{:S(2)}) collective-permute-start(bf16[2,8,3,256]{3,2,1,0:T(4,128)(2,1)S(1)} %collective-permute-done.7), channel_id=1, source_target_pairs={{0,2},{1,3},{2,0},{3,1},{4,6},{5,7},{6,4},{7,5},{8,10},{9,11},{10,... | collective-permute-start | bytes 73736 | tf_op jit(solution)/shard_map/ppermute | solution.py:14
  154.8 18.6 %copy-start.5 = (bf16[1,8,128,256]{3,2,1,0:T(8,128)(2,1)S(1)}, bf16[1,8,128,256]{3,2,1,0:T(8,128)(2,1)}, u32[]{:S(2)}) copy-start(bf16[1,8,128,256]{3,2,1,0:T(8,128)(2,1)} %param.21) | copy-start | bytes 1572868
  157.7 5.0 %collective-permute-start.9 = (bf16[2,8,3,256]{3,2,1,0:T(4,128)(2,1)S(1)}, bf16[2,8,3,256]{3,2,1,0:T(4,128)(2,1)S(1)}, u32[]{:S(2)}, u32[]{:S(2)}) collective-permute-start(bf16[2,8,3,256]{3,2,1,0:T(4,128)(2,1)S(1)} %collective-permute-done.8), channel_id=1, source_target_pairs={{0,4},{1,5},{2,6},{3,7},{4,0},{5,1},{6,2},{7,3},{8,12},{9,13},{10,... | collective-permute-start | bytes 73736 | tf_op jit(solution)/shard_map/ppermute | solution.py:14
  (21 other events, 52.3 us)
Sparse Core Ops, SparseCore 0:
  154.9 134.1 all-reduce.4
where the time goes:
time: 300 us; the launch traced here: 299 us
  waiting for transfers between devices  126 us (42%)
  blocking collectives  59.8 us (20%)
  other arithmetic  47.6 us (16%)
  between operations  20.4 us (7%)
  starting transfers between devices  17.2 us (6%)
  matrix products  14.3 us (5%)
  local copies, waits for them, and re-layouts  14.1 us (5%)
    psum x1, waiting for transfers between devices, shards(): lax.psum((grad_kernel, grad_expand, grad_reduce, grad_expand_bias, vector...  115 us
    psum x1, blocking collectives, shards(): lax.psum((grad_kernel, grad_expand, grad_reduce, grad_expand_bias, vector...  41.1 us
    another operation x2, other arithmetic  17.9 us
    all_gather x1, blocking collectives, partner_strips(): lax.all_gather(both_kinds[None].astype(jnp.bfloat16), 'face', axis=0, til...  9.98 us
    reduce_sum x1, other arithmetic, block_pass(): average = jnp.mean(convolved, axis=-1, keepdims=True)  9.21 us
    ppermute x6, waiting for transfers between devices, swapped(): lax.ppermute(x, axis, [(i, i ^ 1 << stride) for i in range(lax.axis_size(...  9.02 us
    all_gather x1, blocking collectives, partner_strips(): gathered = lax.all_gather(both_kinds[None], 'face', axis=0, tiled=True)  8.74 us
    reduce_sum x3, other arithmetic, block_pass(): jnp.sum(grad_conv * padded[row_off:row_off + row_count, col_off:col_off +...  7.8 us
  transfers between devices with their start and end apart: 11, of which 6 were waited for; matrix products, arithmetic and copies ran while one was open for 4% of the time, Pallas kernels for 0%

commit v1 on v0

v1 whole, which is shorter than its diff:
```python
import math

import jax
import jax.numpy as jnp
from jax import lax
from jax.experimental import pallas as pl
from jax.experimental.pallas import tpu as pltpu
from jax.sharding import PartitionSpec as P

EPSILON = 1e-06
ROOT_COEF = 0.7978845608028654
CUBIC_COEF = 0.044715
LANES = 128
SUB = 8
LEAD = 8
F32 = jnp.float32
BF16 = jnp.bfloat16


def swapped(x, axis, mask):
    return lax.ppermute(x, axis, [(i, i ^ mask) for i in range(lax.axis_size(axis))])


def dot(a, b, dims):
    return lax.dot_general(a, b, (dims, ((), ())), preferred_element_type=F32)


def whole(n):
    return [pl.BlockSpec(memory_space=pltpu.VMEM)] * n


def call(body, outs, scratch, flops, *args):
    return pl.pallas_call(
        body,
        out_shape=outs,
        in_specs=whole(len(args)),
        out_specs=whole(len(outs)),
        scratch_shapes=scratch,
        compiler_params=pltpu.CompilerParams(vmem_limit_bytes=40 * 1024 * 1024),
        cost_estimate=pl.CostEstimate(flops=flops, bytes_accessed=4 << 20, transcendentals=0),
    )(*args)


def forward_kernel(
    band, up, down, west, east, cot, taps, chan, bias1, w1, w2, core,
    result, pad, grad, mine, other, vecs, bias_out,
    conv, normed, act, pre, gbr, tmp,
):
    rows, cols, channels = band.shape
    halves = channels // LANES
    pitch = cols + 2 * LEAD
    ext = rows + 6
    groups = cols // SUB
    hidden = w1.shape[1]
    cells = rows * cols

    for h in range(halves):
        lane = slice(h * LANES, (h + 1) * LANES)
        for i in range(ext):
            at = (h * ext + i) * pitch
            src = up[i] if i < 3 else (band[i - 3] if i < rows + 3 else down[i - rows - 3])
            pad[at : at + LEAD, :] = west[i][:, lane].astype(F32)
            pad[at + LEAD : at + LEAD + cols, :] = src[:, lane].astype(F32)
            pad[at + LEAD + cols : at + pitch, :] = east[i][:, lane].astype(F32)
        for r in range(rows):
            at = (h * rows + r) * pitch
            grad[at : at + LEAD, :] = jnp.zeros((LEAD, LANES), F32)
            grad[at + LEAD + cols : at + pitch, :] = jnp.zeros((LEAD, LANES), F32)

    for h in range(halves):
        first = jnp.broadcast_to(chan[0:1, h * LANES : (h + 1) * LANES], (SUB, LANES))

        def conv_row(r, carry, h=h, first=first):
            acc = [first] * groups
            for a in range(7):
                base = (h * ext + r + a) * pitch + LEAD - 3
                tap = [taps[h, a * 7 + b] for b in range(7)]
                for jj in range(groups + 6):
                    x = pad[pl.ds(base + jj, SUB, stride=groups), :]
                    for b in range(7):
                        j = jj - b
                        if 0 <= j < groups:
                            acc[j] = acc[j] + tap[b] * x
            for j in range(groups):
                conv[pl.ds((h * rows + r) * cols + j, SUB, stride=groups), :] = acc[j]
            return carry

        lax.fori_loop(0, rows, conv_row, 0)

    step = 2 * cols
    gain = chan[1:2, :]
    shift = chan[2:3, :]
    bias2 = chan[3:4, :]
    scale = chan[4:5, :]
    tiles = hidden // 256

    def chunk(m, carry):
        s_conv, s_gain, s_norm, s_cot, s_scale = carry
        at = pl.multiple_of(m * step, step)
        x = jnp.concatenate(
            [conv[pl.ds(h * cells + at, step), :] for h in range(halves)], axis=1
        )
        centred = x - jnp.mean(x, axis=-1, keepdims=True)
        inverse = lax.rsqrt(jnp.mean(centred * centred, axis=-1, keepdims=True) + EPSILON)
        standard = centred * inverse
        lane_in = (standard * gain + shift).astype(BF16)
        normed[pl.ds(at, step), :] = lane_in
        tmp[...] = standard
        upstream = cot[pl.ds(2 * m, 2)].reshape(step, channels).astype(F32)
        g_branch = (upstream * scale).astype(BF16)
        gbr[pl.ds(at, step), :] = g_branch
        for n in range(tiles):
            hid = slice(n * 256, (n + 1) * 256)
            v = dot(lane_in, w1[:, hid], ((1,), (0,))) + bias1[:, hid]
            v2 = v * v
            half = 0.5 + 0.5 * jnp.tanh(v * (ROOT_COEF + ROOT_COEF * CUBIC_COEF * v2))
            act[pl.ds(at, step), hid] = (v * half).astype(BF16)
            slope = half * (
                1.0 + (1.0 - half) * (v * (2 * ROOT_COEF + 6 * ROOT_COEF * CUBIC_COEF * v2))
            )
            d_act = dot(g_branch, w2[hid, :], ((1,), (1,)))
            g_pre = (d_act * slope).astype(BF16)
            pre[pl.ds(at, step), hid] = g_pre
            bias_out[:, hid] += jnp.sum(g_pre.astype(F32), axis=0, keepdims=True)
        branch = dot(act[pl.ds(at, step), :], w2[...], ((1,), (0,))) + bias2
        residual = band[pl.ds(2 * m, 2)].reshape(step, channels).astype(F32)
        result[pl.ds(2 * m, 2)] = (residual + scale * branch).astype(BF16).reshape(2, cols, channels)
        s_cot = s_cot + jnp.sum(upstream, axis=0, keepdims=True)
        s_scale = s_scale + jnp.sum(upstream * branch, axis=0, keepdims=True)
        g_norm = dot(pre[pl.ds(at, step), :], w1[...], ((1,), (1,)))
        standard = tmp[...]
        u = g_norm * gain
        g_conv = (
            u
            - jnp.mean(u, axis=-1, keepdims=True)
            - standard * jnp.mean(u * standard, axis=-1, keepdims=True)
        ) * inverse
        for h in range(halves):
            for k in range(2):
                dst = (h * rows + 2 * m + k) * pitch + LEAD
                grad[pl.ds(pl.multiple_of(dst, 8), cols), :] = g_conv[
                    k * cols : (k + 1) * cols, h * LANES : (h + 1) * LANES
                ]
        s_conv = s_conv + jnp.sum(g_conv, axis=0, keepdims=True)
        s_gain = s_gain + jnp.sum(g_norm * standard, axis=0, keepdims=True)
        s_norm = s_norm + jnp.sum(g_norm, axis=0, keepdims=True)
        return (s_conv, s_gain, s_norm, s_cot, s_scale)

    bias_out[...] = jnp.zeros_like(bias_out)
    zero = jnp.zeros((1, channels), F32)
    sums = lax.fori_loop(0, rows // 2, chunk, (zero,) * 5)
    sums = (sums[0], sums[1], sums[2], sums[3] * scale, sums[4])
    vecs[...] = jnp.concatenate(list(sums) + [zero] * 3, axis=0)

    even = core[0, 0] == 0
    for n in range(tiles):
        hid = slice(n * 256, (n + 1) * 256)
        g_expand = dot(normed[...], pre[:, hid], ((0,), (0,)))
        g_reduce = dot(act[:, hid], gbr[...], ((0,), (0,)))
        mine[n] = jnp.where(even, g_expand, g_reduce)
        other[n] = jnp.where(even, g_reduce, g_expand).astype(BF16)


def spread_kernel(grad, taps, out):
    halves = taps.shape[0]
    pitch = out.shape[2]
    ext = out.shape[1]
    rows = ext - 6
    cols = pitch - 2 * LEAD
    groups = cols // SUB + 1
    out[...] = jnp.zeros_like(out)
    flat = out.reshape(halves * ext * pitch, LANES)
    for h in range(halves):

        def row(r, carry, h=h):
            src = (h * rows + r) * pitch + LEAD
            for a in range(7):
                dst = (h * ext + r + a) * pitch + LEAD - 3
                tap = [taps[h, a * 7 + b] for b in range(7)]
                acc = [flat[pl.ds(dst + j, SUB, stride=groups), :] for j in range(groups)]
                for jj in range(-6, groups):
                    x = grad[pl.ds(src + jj, SUB, stride=groups), :]
                    for b in range(7):
                        j = jj + b
                        if 0 <= j < groups:
                            acc[j] = acc[j] + tap[b] * x
                for j in range(groups):
                    flat[pl.ds(dst + j, SUB, stride=groups), :] = acc[j]
            return carry

        lax.fori_loop(0, rows, row, 0)


def taps_kernel(grad, pad, out):
    pitch = 128 + 2 * LEAD
    halves = out.shape[0]
    rows = grad.shape[0] // (halves * pitch)
    ext = rows + 6
    cols = pitch - 2 * LEAD
    groups = cols // SUB
    for h in range(halves):

        def one(a, carry, h=h):
            acc = [jnp.zeros((SUB, LANES), F32)] * 7
            for r in range(rows):
                src = (h * rows + r) * pitch + LEAD
                base = (h * ext + r + a) * pitch + LEAD - 3
                g = [grad[pl.ds(src + j, SUB, stride=groups), :] for j in range(groups)]
                for jj in range(groups + 6):
                    x = pad[pl.ds(base + jj, SUB, stride=groups), :]
                    for b in range(7):
                        j = jj - b
                        if 0 <= j < groups:
                            acc[b] = acc[b] + g[j] * x
            for b in range(7):
                out[h, pl.ds(a * 7 + b, 1), :] = jnp.sum(acc[b], axis=0, keepdims=True)
            return carry

        lax.fori_loop(0, 7, one, 0)


def partner_swap(by_side, edge_match):
    faces = lax.axis_size("face")
    tiles = lax.axis_size("tile")
    own = lax.dynamic_index_in_dim(edge_match, lax.axis_index("face"), 0, keepdims=False)
    face = lax.axis_index("face")
    near_side = jnp.where(own[0, 0] == face ^ 1, 0, 1)
    got = []
    for which, mask in ((0, 1), (1, faces // 2)):
        side = near_side if which == 0 else 1 - near_side
        reverse = own[side, 2] == 1
        sent = lax.dynamic_index_in_dim(by_side, side, 0, keepdims=False)
        pairs = [
            (f * tiles + t, (f ^ mask) * tiles + t) for f in range(faces) for t in range(tiles)
        ]
        turned = [
            (f * tiles + t, (f ^ mask) * tiles + tiles - 1 - t)
            for f in range(faces)
            for t in range(tiles)
        ]
        plain = lax.ppermute(sent, ("face", "tile"), pairs)
        flipped = lax.ppermute(sent, ("face", "tile"), turned)
        got.append(jnp.where(reverse, jnp.flip(flipped, 0), plain))
    first, second = got
    return jnp.where(near_side == 0, first, second), jnp.where(near_side == 0, second, first)


def row_exchange(to_up, to_down):
    count = lax.axis_size("tile")
    from_up = lax.ppermute(to_down, "tile", [(i, i + 1) for i in range(count - 1)])
    from_down = lax.ppermute(to_up, "tile", [(i + 1, i) for i in range(count - 1)])
    return from_up, from_down


def bit_of(axis, mask):
    return (lax.axis_index(axis) & mask) // mask


def face_and_tile_steps():
    face = [("face", 1 << k) for k in range(lax.axis_size("face").bit_length() - 1)]
    tile = [("tile", 1 << k) for k in range(1, lax.axis_size("tile").bit_length() - 1)]
    return face + tile, face[1::-1] + face[2:] + tile


def halving(x, step):
    axis, mask = step
    bit = bit_of(axis, mask)
    pair = x.reshape((2, x.shape[0] // 2) + x.shape[1:])
    kept = lax.dynamic_index_in_dim(pair, bit, 0, keepdims=False)
    sent = lax.dynamic_index_in_dim(pair, 1 - bit, 0, keepdims=False).astype(BF16)
    return kept + swapped(sent, axis, mask).astype(F32)


def doubling(x, step):
    axis, mask = step
    bit = bit_of(axis, mask)
    got = swapped(x, axis, mask)
    return jnp.where(bit == 0, jnp.concatenate([x, got], 0), jnp.concatenate([got, x], 0))


def shards(
    fields,
    cotangent,
    edge_match,
    depth_kernel,
    depth_bias,
    norm_gain,
    norm_bias,
    expand_weight,
    expand_bias,
    reduce_weight,
    reduce_bias,
    layer_scale,
):
    band = fields[0]
    cot = cotangent[0]
    rows, cols, channels = band.shape
    halves = channels // LANES
    hidden = expand_weight.shape[1]
    pitch = cols + 2 * LEAD
    ext = rows + 6
    cells = rows * cols

    up, down = row_exchange(band[0:3], band[rows - 3 :])
    tall_west = jnp.concatenate([up[:, 0:3], band[:, 0:3], down[:, 0:3]], 0)
    tall_east = jnp.concatenate(
        [up[:, cols - 3 :], band[:, cols - 3 :], down[:, cols - 3 :]], 0
    )
    west, east = partner_swap(jnp.stack([tall_west, jnp.flip(tall_east, 1)]), edge_match)
    west = jnp.pad(jnp.flip(west, 1), ((0, 0), (LEAD - 3, 0), (0, 0)))
    east = jnp.pad(east, ((0, 0), (0, LEAD - 3), (0, 0)))

    taps = depth_kernel.astype(F32).reshape(49, halves, 1, LANES).transpose(1, 0, 2, 3)
    taps = jnp.broadcast_to(taps, (halves, 49, SUB, LANES))
    zero = jnp.zeros((3, channels), F32)
    chan = jnp.concatenate(
        [jnp.stack([depth_bias, norm_gain, norm_bias, reduce_bias, layer_scale]), zero], 0
    )
    core = jnp.full((1, LANES), lax.axis_index("tile") & 1, jnp.int32)

    shape = jax.ShapeDtypeStruct
    result, pad, grad, mine, other, vecs, bias_out = call(
        forward_kernel,
        [
            shape(band.shape, BF16),
            shape((halves * ext * pitch, LANES), F32),
            shape((halves * rows * pitch, LANES), F32),
            shape((hidden // 256, 256, 256), F32),
            shape((hidden // 256, 256, 256), BF16),
            shape((8, channels), F32),
            shape((1, hidden), F32),
        ],
        [
            pltpu.VMEM((halves * cells, LANES), F32),
            pltpu.VMEM((cells, channels), BF16),
            pltpu.VMEM((cells, hidden), BF16),
            pltpu.VMEM((cells, hidden), BF16),
            pltpu.VMEM((cells, channels), BF16),
            pltpu.VMEM((2 * cols, channels), F32),
        ],
        3_000_000_000,
        band, up, down, west, east, cot, taps, chan,
        expand_bias.reshape(1, hidden), expand_weight, reduce_weight, core,
    )

    total = mine + swapped(other, "tile", 1).astype(F32)
    total = total.reshape(hidden, 256)
    order_a, order_b = face_and_tile_steps()
    part_a, part_b = total[: hidden // 2], total[hidden // 2 :]
    for step_a, step_b in zip(order_a, order_b):
        part_a, part_b = halving(part_a, step_a), halving(part_b, step_b)

    (wide,) = call(
        spread_kernel, [shape((halves, ext, pitch, LANES), F32)], [], 1_000_000_000, grad, taps
    )
    (g_taps,) = call(taps_kernel, [shape((halves, 49, LANES), F32)], [], 1_000_000_000, grad, pad)

    small = jnp.concatenate(
        [
            g_taps.transpose(1, 0, 2).reshape(49, channels),
            bias_out.reshape(hidden // channels, channels),
            vecs[0:5],
            jnp.zeros((64 - 54 - hidden // channels, channels), F32),
        ],
        0,
    )
    part_a, part_b = part_a.astype(BF16), part_b.astype(BF16)
    for step_a, step_b in zip(order_a[::-1], order_b[::-1]):
        part_a, part_b = doubling(part_a, step_a), doubling(part_b, step_b)
        small = small + swapped(small, *step_a)
    total = jnp.concatenate([part_a, part_b], 0)
    small = small + swapped(small, "tile", 1)
    peer = swapped(total, "tile", 1)
    even = (lax.axis_index("tile") & 1) == 0
    factor = 1.0 / math.sqrt(lax.axis_size("face") * lax.axis_size("tile") * cells)
    g_expand = jnp.where(even, total, peer).astype(F32) * factor
    g_expand = g_expand.reshape(hidden // 256, 256, 256).transpose(1, 0, 2).reshape(channels, hidden)
    g_reduce = jnp.where(even, peer, total).astype(F32) * factor
    small = small * factor

    rim = wide.astype(BF16)
    arrived_up, arrived_down = row_exchange(rim[:, 0:3], rim[:, rows + 3 :])
    middle = wide[:, 3 : rows + 3]
    middle = middle.at[:, 0:3].add(arrived_up.astype(F32))
    middle = middle.at[:, rows - 3 :].add(arrived_down.astype(F32))
    ghost_west = jnp.flip(middle[:, :, LEAD - 3 : LEAD], 2)
    ghost_east = middle[:, :, LEAD + cols : LEAD + cols + 3]
    ghosts = jnp.stack([ghost_west, ghost_east]).astype(BF16).transpose(0, 2, 3, 1, 4)
    back_west, back_east = partner_swap(ghosts.reshape(2, rows, 3, channels), edge_match)
    inner = middle[:, :, LEAD : LEAD + cols].transpose(1, 2, 0, 3).reshape(rows, cols, channels)
    inner = inner.at[:, 0:3].add(back_west.astype(F32))
    inner = inner.at[:, cols - 3 :].add(jnp.flip(back_east, 1).astype(F32))
    grad_fields = (cot.astype(F32) + inner).astype(BF16)

    n_bias = hidden // channels
    return (
        result[None],
        grad_fields[None],
        small[0:49].reshape(7, 7, channels),
        g_expand,
        g_reduce,
        small[49 : 49 + n_bias].reshape(hidden),
        small[49 + n_bias : 54 + n_bias],
    )


def solution(mesh):
    return jax.shard_map(
        shards,
        mesh=mesh,
        in_specs=(P("face", "tile"), P("face", "tile")) + (P(),) * 10,
        out_specs=(P("face", "tile"), P("face", "tile")) + (P(),) * 5,
        check_vma=False,
    )
```

time: 300 us -> 132 us (0.44)
  waiting for transfers between devices: 126 us -> 28.8 us
  blocking collectives: 59.8 us -> 0 us
  other arithmetic: 47.6 us -> 6.88 us
  starting transfers between devices: 17.2 us -> 46.5 us
  Pallas kernels: 0 us -> 27.9 us
  between operations: 20.4 us -> 3.38 us
  matrix products: 14.3 us -> 0 us
  local copies, waits for them, and re-layouts: 14.1 us -> 18.1 us
    psum x1 -> x0, waiting for transfers between devices: 115 us -> none  [shards(): lax.psum((grad_kernel, grad_expand, grad_reduce, grad_expand_bias, vector...]
    psum x1 -> x0, blocking collectives: 41.1 us -> none  [shards(): lax.psum((grad_kernel, grad_expand, grad_reduce, grad_expand_bias, vector...]
    ppermute x10 -> x35, starting transfers between devices: 17.1 us -> 46.5 us  [the longest x23 21.8 us: swapped(): lax.ppermute(x, axis, [(i, i ^ mask) for i in range(lax.axis_size(axis))])]
    pallas_call x0 -> x3, Pallas kernels: none -> 27.9 us  [call(): pl.pallas_call(body, out_shape=outs, in_specs=whole(len(args)), out_specs...]
    reduce_sum x7 -> x0, other arithmetic: 19.5 us -> none  [the longest x1 9.21 us: block_pass(): average = jnp.mean(convolved, axis=-1, keepdims=True)]
    all_gather x2 -> x0, blocking collectives: 18.7 us -> none  [the longest x1 9.98 us: partner_strips(): lax.all_gather(both_kinds[None].astype(jnp.bfloat16), 'face', axis=0, til...]
    another operation x6 -> x1, other arithmetic: 18 us -> 0.03 us  [shards(): jnp.stack([tall_west, jnp.flip(tall_east, 1)])]
    ppermute x10 -> x35, waiting for transfers between devices: 11.3 us -> 28.8 us  [the longest x23 25.4 us: swapped(): lax.ppermute(x, axis, [(i, i ^ mask) for i in range(lax.axis_size(axis))])]
  transfers between devices with their start and end apart: 11 -> 35, of which waited for: 6 -> 20; matrix products, arithmetic and copies ran while one was open for 4% -> 11% of each run, Pallas kernels for 0% -> 0%
where the time goes in v1:
time: 132 us
  starting transfers between devices  46.5 us (35%)
  waiting for transfers between devices  28.8 us (22%)
  Pallas kernels  27.9 us (21%)
  local copies, waits for them, and re-layouts  18.1 us (14%)
  other arithmetic  6.88 us (5%)
  between operations  3.38 us (3%)
    pallas_call x3, Pallas kernels, call(): pl.pallas_call(body, out_shape=outs, in_specs=whole(len(args)), out_specs...  27.9 us
    ppermute x23, waiting for transfers between devices, swapped(): lax.ppermute(x, axis, [(i, i ^ mask) for i in range(lax.axis_size(axis))])  25.4 us
    ppermute x23, starting transfers between devices, swapped(): lax.ppermute(x, axis, [(i, i ^ mask) for i in range(lax.axis_size(axis))])  21.8 us
    ppermute x2, starting transfers between devices, row_exchange(): lax.ppermute(to_down, 'tile', [(i, i + 1) for i in range(count - 1)])  8.16 us
    ppermute x4, starting transfers between devices, partner_swap(): flipped = lax.ppermute(sent, ('face', 'tile'), turned)  7.13 us
    ppermute x4, starting transfers between devices, partner_swap(): plain = lax.ppermute(sent, ('face', 'tile'), pairs)  6.64 us
    unnamed x40, local copies, waits for them, and re-layouts  6.42 us
    ppermute x4, waiting for transfers between devices, partner_swap(): flipped = lax.ppermute(sent, ('face', 'tile'), turned)  3.37 us
  transfers between devices with their start and end apart: 35, of which 20 were waited for; matrix products, arithmetic and copies ran while one was open for 11% of the time, Pallas kernels for 0%

profile of v1, /device:TPU:0, one launch (start us, length us, event | category | flops | bytes accessed | tf_op | source)
XLA Modules:
  0.0 131.5 jit_solution(5134653641667891273)
XLA Ops:
  0.7 1.2 slice_bitcast_fusion.1
  1.9 1.3 collective-permute-start.1
  3.2 3.0 %collective-permute-start = (bf16[3,128,256]{2,1,0:T(8,128)(2,1)S(1)}, bf16[3,128,256]{2,1,0:T(8,128)(2,1)S(1)}, u32[]{:S(2)}, u32[]{:S(2)}) collective-permute-start(bf16[3,128,256]{2,1,0:T(8,128)(2,1)S(1)} %get-tuple-element.80), channel_id=1, source_target_pairs={{0,1},{1,2},{2,3},{3,4},{4,5},{5,6},{6,7},{8,9},{9,10},{10,11},{11... | collective-permute-start | bytes 589832 | tf_op jit(solution)/shard_map/ppermute | solution.py:250
  9.5 3.0 %collective-permute-start.5 = (bf16[14,3,256]{2,1,0:T(4,128)(2,1)S(1)}, bf16[14,3,256]{2,1,0:T(4,128)(2,1)S(1)}, u32[]{:S(2)}, u32[]{:S(2)}) collective-permute-start(bf16[14,3,256]{2,1,0:T(4,128)(2,1)S(1)} %get-tuple-element.87), channel_id=1, source_target_pairs={{0,16},{1,17},{2,18},{3,19},{4,20},{5,21},{6,22},{7,23},{8,24},{9,... | collective-permute-start | bytes 64520 | tf_op jit(solution)/shard_map/ppermute | solution.py:241
  12.5 2.3 %collective-permute-start.4 = (bf16[14,3,256]{2,1,0:T(4,128)(2,1)S(1)}, bf16[14,3,256]{2,1,0:T(4,128)(2,1)S(1)}, u32[]{:S(2)}, u32[]{:S(2)}) collective-permute-start(bf16[14,3,256]{2,1,0:T(4,128)(2,1)S(1)} %get-tuple-element.87), channel_id=1, source_target_pairs={{0,23},{1,22},{2,21},{3,20},{4,19},{5,18},{6,17},{7,16},{8,31},{9,... | collective-permute-start | bytes 64520 | tf_op jit(solution)/shard_map/ppermute | solution.py:242
  14.8 1.5 %collective-permute-start.3 = (bf16[14,3,256]{2,1,0:T(4,128)(2,1)S(1)}, bf16[14,3,256]{2,1,0:T(4,128)(2,1)S(1)}, u32[]{:S(2)}, u32[]{:S(2)}) collective-permute-start(bf16[14,3,256]{2,1,0:T(4,128)(2,1)S(1)} %get-tuple-element.88), channel_id=1, source_target_pairs={{0,8},{1,9},{2,10},{3,11},{4,12},{5,13},{6,14},{7,15},{8,0},{9,1},... | collective-permute-start | bytes 64520 | tf_op jit(solution)/shard_map/ppermute | solution.py:241
  16.9 1.3 %constant_dynamic-slice_fusion.3 = (s32[1,1,1]{0,1,2:T(1,128)}, s32[1,1,1]{0,1,2:T(1,128)}) fusion(s32[4,2,3]{0,1,2:T(2,128)} %param.22, s32[]{:T(128)S(6)} %select_n.207, s32[]{:T(128)S(6)} %select_n.212, s32[]{:T(128)S(6)} %select_n.208), kind=kLoop, calls=%fused_computation.79 | loop fusion | bytes 28 | tf_op jit(solution)/shard_map/dynamic_slice | solution.py:231
  19.8 2.4 %collective-permute-done.2 = bf16[14,3,256]{2,1,0:T(4,128)(2,1)S(1)} collective-permute-done((bf16[14,3,256]{2,1,0:T(4,128)(2,1)S(1)}, bf16[14,3,256]{2,1,0:T(4,128)(2,1)S(1)}, u32[]{:S(2)}, u32[]{:S(2)}) %collective-permute-start.2) | collective-permute-done | bytes 21536 | tf_op jit(solution)/shard_map/ppermute | solution.py:242
  22.6 1.0 copy-done.4
  23.6 14.9 %shard_map.171 = (bf16[8,128,256]{2,1,0:T(8,128)(2,1)}, f32[4032,128]{1,0:T(8,128)S(1)}, f32[2304,128]{1,0:T(8,128)S(1)}, f32[4,256,256]{2,1,0:T(8,128)S(1)}, bf...) custom-call(bf16[8,128,256]{2,1,0:T(8,128)(2,1)S(1)} %bitcast.107, ...), custom_call_target="tpu_custom_call" | custom-call | flops 3000000000 | bytes 4194304 | tf_op jit(solution)/shard_map/pallas_call | solution.py:33
  39.5 1.4 %copy-done.9 = f32[4032,128]{1,0:T(8,128)} copy-done((f32[4032,128]{1,0:T(8,128)}, f32[4032,128]{1,0:T(8,128)S(1)}, u32[]{:S(2)}) %copy-start.9) | copy-done | bytes 2064408
  42.1 1.3 copy-done.7
  43.3 3.8 %shard_map.172 = f32[2,14,144,128]{3,2,1,0:T(8,128)S(1)} custom-call(f32[2304,128]{1,0:T(8,128)S(1)} %copy-done.7, f32[2,49,8,128]{3,2,1,0:T(8,128)S(1)} %broadcast_in_dim.27.taps), custom_call_target="tpu_custom_call" | custom-call | flops 1000000000 | bytes 4194304 | tf_op jit(solution)/shard_map/pallas_call | solution.py:33
  47.1 9.3 %shard_map.173 = f32[2,49,128]{2,1,0:T(8,128)S(1)} custom-call(f32[2304,128]{1,0:T(8,128)S(1)} %copy-done.8, f32[4032,128]{1,0:T(8,128)S(1)} %copy-done.10), custom_call_target="tpu_custom_call" | custom-call | flops 1000000000 | bytes 4194304 | tf_op jit(solution)/shard_map/pallas_call | solution.py:33
  57.8 5.1 %collective-permute-start.6 = (bf16[2,3,144,128]{3,2,1,0:T(8,128)(2,1)}, bf16[2,3,144,128]{3,2,1,0:T(8,128)(2,1)}, u32[]{:S(2)}, u32[]{:S(2)}) collective-permute-start(bf16[2,3,144,128]{3,2,1,0:T(8,128)(2,1)} %get-tuple-element.76), channel_id=1, source_target_pairs={{0,1},{1,2},{2,3},{3,4},{4,5},{5,6},{6,7},{8,9},{9,10},{10,11},{11... | collective-permute-start | bytes 663560 | tf_op jit(solution)/shard_map/ppermute | solution.py:250
  63.2 4.3 %collective-permute-done.13 = f32[64,256]{1,0:T(8,128)S(1)} collective-permute-done((f32[64,256]{1,0:T(8,128)S(1)}, f32[64,256]{1,0:T(8,128)S(1)}, u32[]{:S(2)}, u32[]{:S(2)}) %collective-permute-start.13) | collective-permute-done | bytes 65568 | tf_op jit(solution)/shard_map/ppermute | solution.py:21
  67.6 1.6 %collective-permute-start.14 = (f32[64,256]{1,0:T(8,128)S(1)}, f32[64,256]{1,0:T(8,128)}, u32[]{:S(2)}, u32[]{:S(2)}) collective-permute-start(f32[64,256]{1,0:T(8,128)S(1)} %add.153), channel_id=1, source_target_pairs={{0,16},{8,24},{16,0},{24,8},{1,17},{9,25},{17,1},{25,9},{2,18},{10... | collective-permute-start | bytes 196616 | tf_op jit(solution)/shard_map/ppermute | solution.py:21
  69.3 1.5 %collective-permute-start.7 = (bf16[2,3,144,128]{3,2,1,0:T(8,128)(2,1)S(1)}, bf16[2,3,144,128]{3,2,1,0:T(8,128)(2,1)S(1)}, u32[]{:S(2)}, u32[]{:S(2)}) collective-permute-start(bf16[2,3,144,128]{3,2,1,0:T(8,128)(2,1)S(1)} %get-tuple-element.75), channel_id=1, source_target_pairs={{1,0},{2,1},{3,2},{4,3},{5,4},{6,5},{7,6},{9,8},{10,9},{11,10},{12... | collective-permute-start | bytes 663560 | tf_op jit(solution)/shard_map/ppermute | solution.py:251
  70.8 1.2 collective-permute-done.14
  74.0 1.1 copy-done.11
  75.2 1.4 %collective-permute-start.9 = (bf16[8,3,256]{2,1,0:T(4,128)(2,1)S(1)}, bf16[8,3,256]{2,1,0:T(4,128)(2,1)S(1)}, u32[]{:S(2)}, u32[]{:S(2)}) collective-permute-start(bf16[8,3,256]{2,1,0:T(4,128)(2,1)S(1)} %bitcast.133), channel_id=1, source_target_pairs={{0,8},{1,9},{2,10},{3,11},{4,12},{5,13},{6,14},{7,15},{8,0},{9,1},... | collective-permute-start | bytes 36872 | tf_op jit(solution)/shard_map/ppermute | solution.py:241
  76.6 2.5 %collective-permute-start.8 = (bf16[8,3,256]{2,1,0:T(4,128)(2,1)S(1)}, bf16[8,3,256]{2,1,0:T(4,128)(2,1)S(1)}, u32[]{:S(2)}, u32[]{:S(2)}) collective-permute-start(bf16[8,3,256]{2,1,0:T(4,128)(2,1)S(1)} %bitcast.134), channel_id=1, source_target_pairs={{0,15},{1,14},{2,13},{3,12},{4,11},{5,10},{6,9},{7,8},{8,7},{9,6},... | collective-permute-start | bytes 36872 | tf_op jit(solution)/shard_map/ppermute | solution.py:242
  79.9 1.7 %collective-permute-start.10 = (bf16[8,3,256]{2,1,0:T(4,128)(2,1)S(1)}, bf16[8,3,256]{2,1,0:T(4,128)(2,1)S(1)}, u32[]{:S(2)}, u32[]{:S(2)}) collective-permute-start(bf16[8,3,256]{2,1,0:T(4,128)(2,1)S(1)} %bitcast.136), channel_id=1, source_target_pairs={{0,23},{1,22},{2,21},{3,20},{4,19},{5,18},{6,17},{7,16},{8,31},{9,... | collective-permute-start | bytes 36872 | tf_op jit(solution)/shard_map/ppermute | solution.py:242
  81.5 1.3 slice_bitcast_fusion
  83.5 1.4 %collective-permute-start.15 = (f32[64,256]{1,0:T(8,128)S(1)}, f32[64,256]{1,0:T(8,128)S(1)}, u32[]{:S(2)}, u32[]{:S(2)}) collective-permute-start(f32[64,256]{1,0:T(8,128)S(1)} %add.154), channel_id=1, source_target_pairs={{0,8},{8,0},{16,24},{24,16},{1,9},{9,1},{17,25},{25,17},{2,10},{10... | collective-permute-start | bytes 196616 | tf_op jit(solution)/shard_map/ppermute | solution.py:21
  85.9 1.2 convert_add_fusion
  87.1 1.3 %collective-permute-start.26 = (bf16[256,256]{1,0:T(8,128)(2,1)S(1)}, bf16[256,256]{1,0:T(8,128)(2,1)S(1)}, u32[]{:S(2)}, u32[]{:S(2)}) collective-permute-start(bf16[256,256]{1,0:T(8,128)(2,1)S(1)} %fusion.4), channel_id=1, source_target_pairs={{0,16},{8,24},{16,0},{24,8},{1,17},{9,25},{17,1},{25,9},{2,18},{10... | collective-permute-start | bytes 393224 | tf_op jit(solution)/shard_map/ppermute | solution.py:21
  88.8 1.0 collective-permute-start.18
  89.9 2.6 %collective-permute-done.26 = bf16[256,256]{1,0:T(8,128)(2,1)S(1)} collective-permute-done((bf16[256,256]{1,0:T(8,128)(2,1)S(1)}, bf16[256,256]{1,0:T(8,128)(2,1)S(1)}, u32[]{:S(2)}, u32[]{:S(2)}) %collective-permute-start.26) | collective-permute-done | bytes 131104 | tf_op jit(solution)/shard_map/ppermute | solution.py:21
  93.3 1.7 %collective-permute-done.18 = bf16[256,256]{1,0:T(8,128)(2,1)S(1)} collective-permute-done((bf16[256,256]{1,0:T(8,128)(2,1)S(1)}, bf16[256,256]{1,0:T(8,128)(2,1)S(1)}, u32[]{:S(2)}, u32[]{:S(2)}) %collective-permute-start.18) | collective-permute-done | bytes 131104 | tf_op jit(solution)/shard_map/ppermute | solution.py:21
  95.7 1.6 %collective-permute-done.27 = bf16[128,256]{1,0:T(8,128)(2,1)S(1)} collective-permute-done((bf16[128,256]{1,0:T(8,128)(2,1)S(1)}, bf16[128,256]{1,0:T(8,128)(2,1)S(1)}, u32[]{:S(2)}, u32[]{:S(2)}) %collective-permute-start.27) | collective-permute-done | bytes 65568 | tf_op jit(solution)/shard_map/ppermute | solution.py:21
  98.3 1.1 collective-permute-done.19
  99.7 1.9 %collective-permute-done.28 = bf16[64,256]{1,0:T(8,128)(2,1)S(1)} collective-permute-done((bf16[64,256]{1,0:T(8,128)(2,1)S(1)}, bf16[64,256]{1,0:T(8,128)(2,1)S(1)}, u32[]{:S(2)}, u32[]{:S(2)}) %collective-permute-start.28) | collective-permute-done | bytes 32800 | tf_op jit(solution)/shard_map/ppermute | solution.py:21
  101.6 1.4 %collective-permute-start.29 = (bf16[32,256]{1,0:T(8,128)(2,1)S(1)}, bf16[32,256]{1,0:T(8,128)(2,1)S(1)}, u32[]{:S(2)}, u32[]{:S(2)}) collective-permute-start(bf16[32,256]{1,0:T(8,128)(2,1)S(1)} %fusion.16), channel_id=1, source_target_pairs={{0,4},{1,5},{2,6},{3,7},{4,0},{5,1},{6,2},{7,3},{8,12},{9,13},{10,... | collective-permute-start | bytes 49160 | tf_op jit(solution)/shard_map/ppermute | solution.py:21
  103.5 1.6 %collective-permute-start.21 = (bf16[32,256]{1,0:T(8,128)(2,1)S(1)}, bf16[32,256]{1,0:T(8,128)(2,1)S(1)}, u32[]{:S(2)}, u32[]{:S(2)}) collective-permute-start(bf16[32,256]{1,0:T(8,128)(2,1)S(1)} %fusion.15), channel_id=1, source_target_pairs={{0,4},{1,5},{2,6},{3,7},{4,0},{5,1},{6,2},{7,3},{8,12},{9,13},{10,... | collective-permute-start | bytes 49160 | tf_op jit(solution)/shard_map/ppermute | solution.py:21
  105.1 1.2 collective-permute-done.29
  106.3 1.5 %collective-permute-start.30 = (bf16[32,256]{1,0:T(8,128)(2,1)S(1)}, bf16[32,256]{1,0:T(8,128)(2,1)S(1)}, u32[]{:S(2)}, u32[]{:S(2)}) collective-permute-start(bf16[32,256]{1,0:T(8,128)(2,1)S(1)} %fusion.9), channel_id=1, source_target_pairs={{0,4},{1,5},{2,6},{3,7},{4,0},{5,1},{6,2},{7,3},{8,12},{9,13},{10,... | collective-permute-start | bytes 49160 | tf_op jit(solution)/shard_map/ppermute | solution.py:21
  108.2 1.6 %collective-permute-start.22 = (bf16[32,256]{1,0:T(8,128)(2,1)S(1)}, bf16[32,256]{1,0:T(8,128)(2,1)S(1)}, u32[]{:S(2)}, u32[]{:S(2)}) collective-permute-start(bf16[32,256]{1,0:T(8,128)(2,1)S(1)} %fusion.10), channel_id=1, source_target_pairs={{0,4},{1,5},{2,6},{3,7},{4,0},{5,1},{6,2},{7,3},{8,12},{9,13},{10,... | collective-permute-start | bytes 49160 | tf_op jit(solution)/shard_map/ppermute | solution.py:21
  109.8 1.2 collective-permute-done.30
  112.8 1.7 %collective-permute-start.23 = (bf16[64,256]{1,0:T(8,128)(2,1)S(1)}, bf16[64,256]{1,0:T(8,128)(2,1)S(1)}, u32[]{:S(2)}, u32[]{:S(2)}) collective-permute-start(bf16[64,256]{1,0:T(8,128)(2,1)S(1)} %maximum_select_fusion.6), channel_id=1, source_target_pairs={{0,2},{1,3},{2,0},{3,1},{4,6},{5,7},{6,4},{7,5},{8,10},{9,11},{10,... | collective-permute-start | bytes 98312 | tf_op jit(solution)/shard_map/ppermute | solution.py:21
  116.8 1.2 collective-permute-start.24
  118.0 1.9 %collective-permute-done.32 = bf16[128,256]{1,0:T(8,128)(2,1)S(1)} collective-permute-done((bf16[128,256]{1,0:T(8,128)(2,1)S(1)}, bf16[128,256]{1,0:T(8,128)(2,1)S(1)}, u32[]{:S(2)}, u32[]{:S(2)}) %collective-permute-start.32) | collective-permute-done | bytes 65568 | tf_op jit(solution)/shard_map/ppermute | solution.py:21
  119.9 1.1 collective-permute-start.33
  121.2 1.2 collective-permute-start.25
  122.7 2.2 %collective-permute-done.33 = bf16[256,256]{1,0:T(8,128)(2,1)S(1)} collective-permute-done((bf16[256,256]{1,0:T(8,128)(2,1)S(1)}, bf16[256,256]{1,0:T(8,128)(2,1)S(1)}, u32[]{:S(2)}, u32[]{:S(2)}) %collective-permute-start.33) | collective-permute-done | bytes 131104 | tf_op jit(solution)/shard_map/ppermute | solution.py:21
  125.0 1.2 collective-permute-done.25
  129.3 1.2 convert_multiply_fusion
  130.4 1.1 copy.32
  (154 shorter events, 23.9 us)
Async XLA Ops:
  0.6 21.9 %copy-start.2 = (bf16[1,8,128,256]{3,2,1,0:T(8,128)(2,1)S(1)}, bf16[1,8,128,256]{3,2,1,0:T(8,128)(2,1)}, u32[]{:S(2)}) copy-start(bf16[1,8,128,256]{3,2,1,0:T(8,128)(2,1)} %param.20) | copy-start | bytes 1572868
  0.6 18.9 %copy-start.12 = (bf16[7,7,256]{2,1,0:T(8,128)(2,1)S(1)}, bf16[7,7,256]{2,1,0:T(8,128)(2,1)}, u32[]{:S(2)}) copy-start(bf16[7,7,256]{2,1,0:T(8,128)(2,1)} %param.23) | copy-start | bytes 75268
  0.7 19.1 %copy-start.17 = (f32[256]{0:T(256)S(1)}, f32[256]{0:T(256)}, u32[]{:S(2)}) copy-start(f32[256]{0:T(256)} %param.31) | copy-start | bytes 3076
  0.7 19.1 %copy-start.16 = (f32[256]{0:T(256)S(1)}, f32[256]{0:T(256)}, u32[]{:S(2)}) copy-start(f32[256]{0:T(256)} %param.30) | copy-start | bytes 3076
  0.7 19.1 %copy-start.15 = (f32[256]{0:T(256)S(1)}, f32[256]{0:T(256)}, u32[]{:S(2)}) copy-start(f32[256]{0:T(256)} %param.26) | copy-start | bytes 3076
  0.7 19.1 %copy-start.14 = (f32[256]{0:T(256)S(1)}, f32[256]{0:T(256)}, u32[]{:S(2)}) copy-start(f32[256]{0:T(256)} %param.25) | copy-start | bytes 3076
  0.7 19.1 %copy-start.13 = (f32[256]{0:T(256)S(1)}, f32[256]{0:T(256)}, u32[]{:S(2)}) copy-start(f32[256]{0:T(256)} %param.24) | copy-start | bytes 3076
  0.7 21.9 %copy-start = (bf16[1,8,128,256]{3,2,1,0:T(8,128)(2,1)S(1)}, bf16[1,8,128,256]{3,2,1,0:T(8,128)(2,1)}, u32[]{:S(2)}) copy-start(bf16[1,8,128,256]{3,2,1,0:T(8,128)(2,1)} %param.21) | copy-start | bytes 1572868
  0.7 21.9 %copy-start.5 = (f32[1024]{0:T(1024)S(1)}, f32[1024]{0:T(1024)}, u32[]{:S(2)}) copy-start(f32[1024]{0:T(1024)} %param.28) | copy-start | bytes 12292
  0.7 21.9 %copy-start.3 = (bf16[256,1024]{1,0:T(8,128)(2,1)S(1)}, bf16[256,1024]{1,0:T(8,128)(2,1)}, u32[]{:S(2)}) copy-start(bf16[256,1024]{1,0:T(8,128)(2,1)} %w1.1) | copy-start | bytes 1572868
  1.9 7.2 %collective-permute-start.1 = (bf16[3,128,256]{2,1,0:T(8,128)(2,1)S(1)}, bf16[3,128,256]{2,1,0:T(8,128)(2,1)S(1)}, u32[]{:S(2)}, u32[]{:S(2)}) collective-permute-start(bf16[3,128,256]{2,1,0:T(8,128)(2,1)S(1)} %get-tuple-element.79), channel_id=1, source_target_pairs={{1,0},{2,1},{3,2},{4,3},{5,4},{6,5},{7,6},{9,8},{10,9},{11,10},{12... | collective-permute-start | bytes 589832 | tf_op jit(solution)/shard_map/ppermute | solution.py:251
  3.2 5.9 %collective-permute-start = (bf16[3,128,256]{2,1,0:T(8,128)(2,1)S(1)}, bf16[3,128,256]{2,1,0:T(8,128)(2,1)S(1)}, u32[]{:S(2)}, u32[]{:S(2)}) collective-permute-start(bf16[3,128,256]{2,1,0:T(8,128)(2,1)S(1)} %get-tuple-element.80), channel_id=1, source_target_pairs={{0,1},{1,2},{2,3},{3,4},{4,5},{5,6},{6,7},{8,9},{9,10},{10,11},{11... | collective-permute-start | bytes 589832 | tf_op jit(solution)/shard_map/ppermute | solution.py:250
  9.5 10.3 %collective-permute-start.5 = (bf16[14,3,256]{2,1,0:T(4,128)(2,1)S(1)}, bf16[14,3,256]{2,1,0:T(4,128)(2,1)S(1)}, u32[]{:S(2)}, u32[]{:S(2)}) collective-permute-start(bf16[14,3,256]{2,1,0:T(4,128)(2,1)S(1)} %get-tuple-element.87), channel_id=1, source_target_pairs={{0,16},{1,17},{2,18},{3,19},{4,20},{5,21},{6,22},{7,23},{8,24},{9,... | collective-permute-start | bytes 64520 | tf_op jit(solution)/shard_map/ppermute | solution.py:241
  12.5 7.3 %collective-permute-start.4 = (bf16[14,3,256]{2,1,0:T(4,128)(2,1)S(1)}, bf16[14,3,256]{2,1,0:T(4,128)(2,1)S(1)}, u32[]{:S(2)}, u32[]{:S(2)}) collective-permute-start(bf16[14,3,256]{2,1,0:T(4,128)(2,1)S(1)} %get-tuple-element.87), channel_id=1, source_target_pairs={{0,23},{1,22},{2,21},{3,20},{4,19},{5,18},{6,17},{7,16},{8,31},{9,... | collective-permute-start | bytes 64520 | tf_op jit(solution)/shard_map/ppermute | solution.py:242
  14.8 5.0 %collective-permute-start.3 = (bf16[14,3,256]{2,1,0:T(4,128)(2,1)S(1)}, bf16[14,3,256]{2,1,0:T(4,128)(2,1)S(1)}, u32[]{:S(2)}, u32[]{:S(2)}) collective-permute-start(bf16[14,3,256]{2,1,0:T(4,128)(2,1)S(1)} %get-tuple-element.88), channel_id=1, source_target_pairs={{0,8},{1,9},{2,10},{3,11},{4,12},{5,13},{6,14},{7,15},{8,0},{9,1},... | collective-permute-start | bytes 64520 | tf_op jit(solution)/shard_map/ppermute | solution.py:241
  16.3 6.0 %collective-permute-start.2 = (bf16[14,3,256]{2,1,0:T(4,128)(2,1)S(1)}, bf16[14,3,256]{2,1,0:T(4,128)(2,1)S(1)}, u32[]{:S(2)}, u32[]{:S(2)}) collective-permute-start(bf16[14,3,256]{2,1,0:T(4,128)(2,1)S(1)} %get-tuple-element.88), channel_id=1, source_target_pairs={{0,15},{1,14},{2,13},{3,12},{4,11},{5,10},{6,9},{7,8},{8,7},{9,6},... | collective-permute-start | bytes 64520 | tf_op jit(solution)/shard_map/ppermute | solution.py:242
  43.3 3.8 %copy-start.8 = (f32[2304,128]{1,0:T(8,128)S(1)}, f32[2304,128]{1,0:T(8,128)}, u32[]{:S(2)}) copy-start(f32[2304,128]{1,0:T(8,128)} %copy-done.6) | copy-start | bytes 3538948
  43.3 3.8 %copy-start.10 = (f32[4032,128]{1,0:T(8,128)S(1)}, f32[4032,128]{1,0:T(8,128)}, u32[]{:S(2)}) copy-start(f32[4032,128]{1,0:T(8,128)} %copy-done.9) | copy-start | bytes 6193156
  56.6 6.3 %collective-permute-start.12 = (f32[64,256]{1,0:T(8,128)S(1)}, f32[64,256]{1,0:T(8,128)S(1)}, u32[]{:S(2)}, u32[]{:S(2)}) collective-permute-start(f32[64,256]{1,0:T(8,128)S(1)} %maximum_maximum_fusion), channel_id=1, source_target_pairs={{0,4},{1,5},{2,6},{3,7},{4,0},{5,1},{6,2},{7,3},{8,12},{9,13},{10,... | collective-permute-start | bytes 196616 | tf_op jit(solution)/shard_map/ppermute | solution.py:21
  57.8 15.1 %collective-permute-start.6 = (bf16[2,3,144,128]{3,2,1,0:T(8,128)(2,1)}, bf16[2,3,144,128]{3,2,1,0:T(8,128)(2,1)}, u32[]{:S(2)}, u32[]{:S(2)}) collective-permute-start(bf16[2,3,144,128]{3,2,1,0:T(8,128)(2,1)} %get-tuple-element.76), channel_id=1, source_target_pairs={{0,1},{1,2},{2,3},{3,4},{4,5},{5,6},{6,7},{8,9},{9,10},{10,11},{11... | collective-permute-start | bytes 663560 | tf_op jit(solution)/shard_map/ppermute | solution.py:250
  63.0 4.6 %collective-permute-start.13 = (f32[64,256]{1,0:T(8,128)S(1)}, f32[64,256]{1,0:T(8,128)S(1)}, u32[]{:S(2)}, u32[]{:S(2)}) collective-permute-start(f32[64,256]{1,0:T(8,128)S(1)} %fusion.24), channel_id=1, source_target_pairs={{0,2},{1,3},{2,0},{3,1},{4,6},{5,7},{6,4},{7,5},{8,10},{9,11},{10,... | collective-permute-start | bytes 196616 | tf_op jit(solution)/shard_map/ppermute | solution.py:21
  67.6 4.4 %collective-permute-start.14 = (f32[64,256]{1,0:T(8,128)S(1)}, f32[64,256]{1,0:T(8,128)}, u32[]{:S(2)}, u32[]{:S(2)}) collective-permute-start(f32[64,256]{1,0:T(8,128)S(1)} %add.153), channel_id=1, source_target_pairs={{0,16},{8,24},{16,0},{24,8},{1,17},{9,25},{17,1},{25,9},{2,18},{10... | collective-permute-start | bytes 196616 | tf_op jit(solution)/shard_map/ppermute | solution.py:21
  69.2 16.6 %collective-permute-start.17 = (bf16[4,256,256]{2,1,0:T(8,128)(2,1)}, bf16[4,256,256]{2,1,0:T(8,128)(2,1)}, u32[]{:S(2)}, u32[]{:S(2)}) collective-permute-start(bf16[4,256,256]{2,1,0:T(8,128)(2,1)} %get-tuple-element.68), channel_id=1, source_target_pairs={{0,1},{1,0},{2,3},{3,2},{4,5},{5,4},{6,7},{7,6},{8,9},{9,8},{10,11... | collective-permute-start | bytes 1572872 | tf_op jit(solution)/shard_map/ppermute | solution.py:21
  69.3 4.5 %collective-permute-start.7 = (bf16[2,3,144,128]{3,2,1,0:T(8,128)(2,1)S(1)}, bf16[2,3,144,128]{3,2,1,0:T(8,128)(2,1)S(1)}, u32[]{:S(2)}, u32[]{:S(2)}) collective-permute-start(bf16[2,3,144,128]{3,2,1,0:T(8,128)(2,1)S(1)} %get-tuple-element.75), channel_id=1, source_target_pairs={{1,0},{2,1},{3,2},{4,3},{5,4},{6,5},{7,6},{9,8},{10,9},{11,10},{12... | collective-permute-start | bytes 663560 | tf_op jit(solution)/shard_map/ppermute | solution.py:251
  75.2 8.3 %collective-permute-start.9 = (bf16[8,3,256]{2,1,0:T(4,128)(2,1)S(1)}, bf16[8,3,256]{2,1,0:T(4,128)(2,1)S(1)}, u32[]{:S(2)}, u32[]{:S(2)}) collective-permute-start(bf16[8,3,256]{2,1,0:T(4,128)(2,1)S(1)} %bitcast.133), channel_id=1, source_target_pairs={{0,8},{1,9},{2,10},{3,11},{4,12},{5,13},{6,14},{7,15},{8,0},{9,1},... | collective-permute-start | bytes 36872 | tf_op jit(solution)/shard_map/ppermute | solution.py:241
  76.6 8.3 %collective-permute-start.8 = (bf16[8,3,256]{2,1,0:T(4,128)(2,1)S(1)}, bf16[8,3,256]{2,1,0:T(4,128)(2,1)S(1)}, u32[]{:S(2)}, u32[]{:S(2)}) collective-permute-start(bf16[8,3,256]{2,1,0:T(4,128)(2,1)S(1)} %bitcast.134), channel_id=1, source_target_pairs={{0,15},{1,14},{2,13},{3,12},{4,11},{5,10},{6,9},{7,8},{8,7},{9,6},... | collective-permute-start | bytes 36872 | tf_op jit(solution)/shard_map/ppermute | solution.py:242
  79.1 5.8 %collective-permute-start.11 = (bf16[8,3,256]{2,1,0:T(4,128)(2,1)S(1)}, bf16[8,3,256]{2,1,0:T(4,128)(2,1)S(1)}, u32[]{:S(2)}, u32[]{:S(2)}) collective-permute-start(bf16[8,3,256]{2,1,0:T(4,128)(2,1)S(1)} %bitcast.135), channel_id=1, source_target_pairs={{0,16},{1,17},{2,18},{3,19},{4,20},{5,21},{6,22},{7,23},{8,24},{9,... | collective-permute-start | bytes 36872 | tf_op jit(solution)/shard_map/ppermute | solution.py:241
  79.9 5.9 %collective-permute-start.10 = (bf16[8,3,256]{2,1,0:T(4,128)(2,1)S(1)}, bf16[8,3,256]{2,1,0:T(4,128)(2,1)S(1)}, u32[]{:S(2)}, u32[]{:S(2)}) collective-permute-start(bf16[8,3,256]{2,1,0:T(4,128)(2,1)S(1)} %bitcast.136), channel_id=1, source_target_pairs={{0,23},{1,22},{2,21},{3,20},{4,19},{5,18},{6,17},{7,16},{8,31},{9,... | collective-permute-start | bytes 36872 | tf_op jit(solution)/shard_map/ppermute | solution.py:242
  83.5 39.1 %collective-permute-start.15 = (f32[64,256]{1,0:T(8,128)S(1)}, f32[64,256]{1,0:T(8,128)S(1)}, u32[]{:S(2)}, u32[]{:S(2)}) collective-permute-start(f32[64,256]{1,0:T(8,128)S(1)} %add.154), channel_id=1, source_target_pairs={{0,8},{8,0},{16,24},{24,16},{1,9},{9,1},{17,25},{25,17},{2,10},{10... | collective-permute-start | bytes 196616 | tf_op jit(solution)/shard_map/ppermute | solution.py:21
  87.1 5.3 %collective-permute-start.26 = (bf16[256,256]{1,0:T(8,128)(2,1)S(1)}, bf16[256,256]{1,0:T(8,128)(2,1)S(1)}, u32[]{:S(2)}, u32[]{:S(2)}) collective-permute-start(bf16[256,256]{1,0:T(8,128)(2,1)S(1)} %fusion.4), channel_id=1, source_target_pairs={{0,16},{8,24},{16,0},{24,8},{1,17},{9,25},{17,1},{25,9},{2,18},{10... | collective-permute-start | bytes 393224 | tf_op jit(solution)/shard_map/ppermute | solution.py:21
  88.8 6.2 %collective-permute-start.18 = (bf16[256,256]{1,0:T(8,128)(2,1)S(1)}, bf16[256,256]{1,0:T(8,128)(2,1)S(1)}, u32[]{:S(2)}, u32[]{:S(2)}) collective-permute-start(bf16[256,256]{1,0:T(8,128)(2,1)S(1)} %fusion.3), channel_id=1, source_target_pairs={{0,8},{8,0},{16,24},{24,16},{1,9},{9,1},{17,25},{25,17},{2,10},{10... | collective-permute-start | bytes 393224 | tf_op jit(solution)/shard_map/ppermute | solution.py:21
  92.5 4.8 %collective-permute-start.27 = (bf16[128,256]{1,0:T(8,128)(2,1)S(1)}, bf16[128,256]{1,0:T(8,128)(2,1)S(1)}, u32[]{:S(2)}, u32[]{:S(2)}) collective-permute-start(bf16[128,256]{1,0:T(8,128)(2,1)S(1)} %fusion.6), channel_id=1, source_target_pairs={{0,8},{8,0},{16,24},{24,16},{1,9},{9,1},{17,25},{25,17},{2,10},{10... | collective-permute-start | bytes 196616 | tf_op jit(solution)/shard_map/ppermute | solution.py:21
  95.1 4.3 %collective-permute-start.19 = (bf16[128,256]{1,0:T(8,128)(2,1)S(1)}, bf16[128,256]{1,0:T(8,128)(2,1)S(1)}, u32[]{:S(2)}, u32[]{:S(2)}) collective-permute-start(bf16[128,256]{1,0:T(8,128)(2,1)S(1)} %fusion.5), channel_id=1, source_target_pairs={{0,16},{8,24},{16,0},{24,8},{1,17},{9,25},{17,1},{25,9},{2,18},{10... | collective-permute-start | bytes 196616 | tf_op jit(solution)/shard_map/ppermute | solution.py:21
  97.4 4.2 %collective-permute-start.28 = (bf16[64,256]{1,0:T(8,128)(2,1)S(1)}, bf16[64,256]{1,0:T(8,128)(2,1)S(1)}, u32[]{:S(2)}, u32[]{:S(2)}) collective-permute-start(bf16[64,256]{1,0:T(8,128)(2,1)S(1)} %fusion.8), channel_id=1, source_target_pairs={{0,2},{1,3},{2,0},{3,1},{4,6},{5,7},{6,4},{7,5},{8,10},{9,11},{10,... | collective-permute-start | bytes 98312 | tf_op jit(solution)/shard_map/ppermute | solution.py:21
  99.5 4.0 %collective-permute-start.20 = (bf16[64,256]{1,0:T(8,128)(2,1)S(1)}, bf16[64,256]{1,0:T(8,128)(2,1)S(1)}, u32[]{:S(2)}, u32[]{:S(2)}) collective-permute-start(bf16[64,256]{1,0:T(8,128)(2,1)S(1)} %fusion.7), channel_id=1, source_target_pairs={{0,2},{1,3},{2,0},{3,1},{4,6},{5,7},{6,4},{7,5},{8,10},{9,11},{10,... | collective-permute-start | bytes 98312 | tf_op jit(solution)/shard_map/ppermute | solution.py:21
  101.6 4.7 %collective-permute-start.29 = (bf16[32,256]{1,0:T(8,128)(2,1)S(1)}, bf16[32,256]{1,0:T(8,128)(2,1)S(1)}, u32[]{:S(2)}, u32[]{:S(2)}) collective-permute-start(bf16[32,256]{1,0:T(8,128)(2,1)S(1)} %fusion.16), channel_id=1, source_target_pairs={{0,4},{1,5},{2,6},{3,7},{4,0},{5,1},{6,2},{7,3},{8,12},{9,13},{10,... | collective-permute-start | bytes 49160 | tf_op jit(solution)/shard_map/ppermute | solution.py:21
  103.5 4.7 %collective-permute-start.21 = (bf16[32,256]{1,0:T(8,128)(2,1)S(1)}, bf16[32,256]{1,0:T(8,128)(2,1)S(1)}, u32[]{:S(2)}, u32[]{:S(2)}) collective-permute-start(bf16[32,256]{1,0:T(8,128)(2,1)S(1)} %fusion.15), channel_id=1, source_target_pairs={{0,4},{1,5},{2,6},{3,7},{4,0},{5,1},{6,2},{7,3},{8,12},{9,13},{10,... | collective-permute-start | bytes 49160 | tf_op jit(solution)/shard_map/ppermute | solution.py:21
  106.3 4.6 %collective-permute-start.30 = (bf16[32,256]{1,0:T(8,128)(2,1)S(1)}, bf16[32,256]{1,0:T(8,128)(2,1)S(1)}, u32[]{:S(2)}, u32[]{:S(2)}) collective-permute-start(bf16[32,256]{1,0:T(8,128)(2,1)S(1)} %fusion.9), channel_id=1, source_target_pairs={{0,4},{1,5},{2,6},{3,7},{4,0},{5,1},{6,2},{7,3},{8,12},{9,13},{10,... | collective-permute-start | bytes 49160 | tf_op jit(solution)/shard_map/ppermute | solution.py:21
  108.2 4.6 %collective-permute-start.22 = (bf16[32,256]{1,0:T(8,128)(2,1)S(1)}, bf16[32,256]{1,0:T(8,128)(2,1)S(1)}, u32[]{:S(2)}, u32[]{:S(2)}) collective-permute-start(bf16[32,256]{1,0:T(8,128)(2,1)S(1)} %fusion.10), channel_id=1, source_target_pairs={{0,4},{1,5},{2,6},{3,7},{4,0},{5,1},{6,2},{7,3},{8,12},{9,13},{10,... | collective-permute-start | bytes 49160 | tf_op jit(solution)/shard_map/ppermute | solution.py:21
  111.0 4.0 %collective-permute-start.31 = (bf16[64,256]{1,0:T(8,128)(2,1)S(1)}, bf16[64,256]{1,0:T(8,128)(2,1)S(1)}, u32[]{:S(2)}, u32[]{:S(2)}) collective-permute-start(bf16[64,256]{1,0:T(8,128)(2,1)S(1)} %maximum_select_fusion.7), channel_id=1, source_target_pairs={{0,2},{1,3},{2,0},{3,1},{4,6},{5,7},{6,4},{7,5},{8,10},{9,11},{10,... | collective-permute-start | bytes 98312 | tf_op jit(solution)/shard_map/ppermute | solution.py:21
  112.8 4.0 %collective-permute-start.23 = (bf16[64,256]{1,0:T(8,128)(2,1)S(1)}, bf16[64,256]{1,0:T(8,128)(2,1)S(1)}, u32[]{:S(2)}, u32[]{:S(2)}) collective-permute-start(bf16[64,256]{1,0:T(8,128)(2,1)S(1)} %maximum_select_fusion.6), channel_id=1, source_target_pairs={{0,2},{1,3},{2,0},{3,1},{4,6},{5,7},{6,4},{7,5},{8,10},{9,11},{10,... | collective-permute-start | bytes 98312 | tf_op jit(solution)/shard_map/ppermute | solution.py:21
  115.0 4.9 %collective-permute-start.32 = (bf16[128,256]{1,0:T(8,128)(2,1)S(1)}, bf16[128,256]{1,0:T(8,128)(2,1)S(1)}, u32[]{:S(2)}, u32[]{:S(2)}) collective-permute-start(bf16[128,256]{1,0:T(8,128)(2,1)S(1)} %maximum_select_fusion.5), channel_id=1, source_target_pairs={{0,8},{8,0},{16,24},{24,16},{1,9},{9,1},{17,25},{25,17},{2,10},{10... | collective-permute-start | bytes 196616 | tf_op jit(solution)/shard_map/ppermute | solution.py:21
  116.8 4.3 %collective-permute-start.24 = (bf16[128,256]{1,0:T(8,128)(2,1)S(1)}, bf16[128,256]{1,0:T(8,128)(2,1)S(1)}, u32[]{:S(2)}, u32[]{:S(2)}) collective-permute-start(bf16[128,256]{1,0:T(8,128)(2,1)S(1)} %maximum_select_fusion.4), channel_id=1, source_target_pairs={{0,16},{8,24},{16,0},{24,8},{1,17},{9,25},{17,1},{25,9},{2,18},{10... | collective-permute-start | bytes 196616 | tf_op jit(solution)/shard_map/ppermute | solution.py:21
  119.9 5.0 %collective-permute-start.33 = (bf16[256,256]{1,0:T(8,128)(2,1)S(1)}, bf16[256,256]{1,0:T(8,128)(2,1)S(1)}, u32[]{:S(2)}, u32[]{:S(2)}) collective-permute-start(bf16[256,256]{1,0:T(8,128)(2,1)S(1)} %maximum_select_fusion.3), channel_id=1, source_target_pairs={{0,16},{8,24},{16,0},{24,8},{1,17},{9,25},{17,1},{25,9},{2,18},{10... | collective-permute-start | bytes 393224 | tf_op jit(solution)/shard_map/ppermute | solution.py:21
  121.2 5.0 %collective-permute-start.25 = (bf16[256,256]{1,0:T(8,128)(2,1)S(1)}, bf16[256,256]{1,0:T(8,128)(2,1)S(1)}, u32[]{:S(2)}, u32[]{:S(2)}) collective-permute-start(bf16[256,256]{1,0:T(8,128)(2,1)S(1)} %maximum_select_fusion.2), channel_id=1, source_target_pairs={{0,8},{8,0},{16,24},{24,16},{1,9},{9,1},{17,25},{25,17},{2,10},{10... | collective-permute-start | bytes 393224 | tf_op jit(solution)/shard_map/ppermute | solution.py:21
  122.4 4.0 %copy-start.1 = (bf16[1,8,128,256]{3,2,1,0:T(8,128)(2,1)S(1)}, bf16[1,8,128,256]{3,2,1,0:T(8,128)(2,1)}, u32[]{:S(2)}) copy-start(bf16[1,8,128,256]{3,2,1,0:T(8,128)(2,1)} %param.21) | copy-start | bytes 1572868
  122.7 4.7 %collective-permute-start.16 = (f32[64,256]{1,0:T(8,128)S(1)}, f32[64,256]{1,0:T(8,128)S(1)}, u32[]{:S(2)}, u32[]{:S(2)}) collective-permute-start(f32[64,256]{1,0:T(8,128)S(1)} %add.155), channel_id=1, source_target_pairs={{0,1},{1,0},{2,3},{3,2},{4,5},{5,4},{6,7},{7,6},{8,9},{9,8},{10,11... | collective-permute-start | bytes 196616 | tf_op jit(solution)/shard_map/ppermute | solution.py:21
  126.4 2.9 %collective-permute-start.34 = (bf16[1024,256]{1,0:T(8,128)(2,1)S(1)}, bf16[1024,256]{1,0:T(8,128)(2,1)S(1)}, u32[]{:S(2)}, u32[]{:S(2)}) collective-permute-start(bf16[1024,256]{1,0:T(8,128)(2,1)S(1)} %pad_maximum_fusion), channel_id=1, source_target_pairs={{0,1},{1,0},{2,3},{3,2},{4,5},{5,4},{6,7},{7,6},{8,9},{9,8},{10,11... | collective-permute-start | bytes 1572872 | tf_op jit(solution)/shard_map/ppermute | solution.py:21
  (5 other events, 5.8 us)

commit v2 on v1

v2 whole, which is shorter than its diff:
```python
import math

import jax
import jax.numpy as jnp
from jax import lax
from jax.experimental import pallas as pl
from jax.experimental.pallas import tpu as pltpu
from jax.sharding import PartitionSpec as P

EPSILON = 1e-06
ROOT_COEF = 0.7978845608028654
CUBIC_COEF = 0.044715
LANES = 128
SUB = 8
LEAD = 8
SMALL = 64
F32 = jnp.float32
BF16 = jnp.bfloat16


def dot(a, b, dims):
    return lax.dot_general(a, b, (dims, ((), ())), preferred_element_type=F32)


def call(body, outs, scratch, flops, args, smem=0, after=(), limit=4, left=()):
    vmem = pl.BlockSpec(memory_space=pltpu.VMEM)
    scalar = pl.BlockSpec(memory_space=pltpu.SMEM)
    anywhere = pl.BlockSpec(memory_space=pl.ANY)
    outside = pl.BlockSpec(memory_space=pltpu.HBM)
    count = len(args)

    def run(*refs):
        body(*refs[:count], *refs[count + len(after) :])

    return pl.pallas_call(
        run,
        out_shape=outs,
        in_specs=[vmem] * (count - smem) + [scalar] * smem + [anywhere] * len(after),
        out_specs=[outside if i in left else vmem for i in range(len(outs))],
        scratch_shapes=scratch,
        compiler_params=pltpu.CompilerParams(vmem_limit_bytes=limit * 1024 * 1024),
        cost_estimate=pl.CostEstimate(flops=flops, bytes_accessed=1 << 20, transcendentals=0),
    )(*args, *after)


def kept(x):
    return pltpu.with_memory_space_constraint(x, pltpu.VMEM)


def strided(ref, start, groups):
    return ref[pl.ds(start, SUB, stride=groups), :]


def gluing(match):
    face = lax.axis_index("face")
    near = jnp.where(match[face, 0, 0] == face ^ 1, 0, 1)
    return near, match[face, near, 2], match[face, 1 - near, 2]


def pack_columns(tile, count, near, held, outs):
    vals = {}
    for side in range(2):
        for h in range(2):
            held[...] = jnp.zeros_like(held)
            for i in range(count):
                t = tile(side, h, i)
                held[0, i * SUB : (i + 1) * SUB, :] = t
                held[1, (count - 1 - i) * SUB : (count - i) * SUB, :] = t
            for v in range(2):
                for d in range(3):
                    vals[side, h, v, d] = held[v, pl.ds(tile.column(side, d), 16, stride=SUB), :]
    first = near == 0
    for h in range(2):
        lane = slice(h * LANES, (h + 1) * LANES)
        for v in range(2):
            for d in range(3):
                west, east = vals[0, h, v, d], vals[1, h, v, d]
                at = slice(d * 16, d * 16 + 16)
                outs[v][at, lane] = jnp.where(first, west, east).astype(BF16)
                outs[2 + v][at, lane] = jnp.where(first, east, west).astype(BF16)


def unpack_columns(near, turn_near, turn_far, got):
    first = near == 0

    def value(side, h, d):
        lane = slice(h * LANES, (h + 1) * LANES)
        parts = [g[d * 16 : d * 16 + 16, lane].astype(F32) for g in got]
        one = jnp.where(turn_near == 1, parts[1], parts[0])
        two = jnp.where(turn_far == 1, parts[3], parts[2])
        return jnp.where(first, one, two) if side == 0 else jnp.where(first, two, one)

    return value


def ends_kernel(band, within, across, columns):
    rows, cols, _ = band.shape
    even = (lax.axis_index("tile") & 1) == 0
    for k in range(3):
        top, bottom = band[k], band[rows - 3 + k]
        within[k] = jnp.where(even, bottom, top)
        across[k] = jnp.where(even, top, bottom)
    for r in range(rows):
        columns[r, 0:16, :] = band[r, 0:16, :]
        columns[r, 16:32, :] = band[r, cols - 16 : cols, :]


def edges_kernel(columns, within, across, match, *refs):
    outs, held = refs[:4], refs[4]
    up, down = above_below(within, across)
    rows, _, _ = columns.shape
    _, cols, _ = within.shape
    near, _, _ = gluing(match)

    def tile(side, h, i):
        lane = slice(h * LANES, (h + 1) * LANES)
        at = slice(0, 16) if side == 0 else slice(cols - 16, cols)
        if i < 3:
            v = up(i, at, lane)
        elif i < rows + 3:
            v = columns[i - 3, slice(0, 16) if side == 0 else slice(16, 32), lane]
        else:
            v = down(i - rows - 3, at, lane)
        return v.astype(F32)[0:SUB] if side == 0 else v.astype(F32)[SUB:16]

    tile.column = lambda side, d: d if side == 0 else SUB - 1 - d
    pack_columns(tile, rows + 6, near, held, outs)


def fill_pad(pad, halves, ext, wide, cols, source, which):
    for h in range(halves):
        lane = slice(h * LANES, (h + 1) * LANES)
        for i in which:
            at = (h * ext + i) * wide
            pad[at : at + LEAD, :] = jnp.zeros((LEAD, LANES), F32)
            pad[at + LEAD : at + LEAD + cols, :] = source(i, lane).astype(F32)
            pad[at + LEAD + cols : at + wide, :] = jnp.zeros((LEAD + SUB, LANES), F32)


def own_rows_kernel(band, kernel, bias, conv, taps, pad):
    for h in range(2):
        lane = slice(h * LANES, (h + 1) * LANES)
        for a in range(7):
            row = kernel[a].astype(F32)
            for b in range(7):
                taps[h, a * 7 + b] = jnp.broadcast_to(row[b : b + 1, lane], (SUB, LANES))
        taps[h, 49] = jnp.broadcast_to(bias[:, lane], (SUB, LANES))
    rows, cols, channels = band.shape
    halves = channels // LANES
    pitch = cols + 2 * LEAD
    wide = pitch + SUB
    ext = rows + 6
    groups = cols // SUB + 1
    cpitch = groups * SUB
    fill_pad(pad, halves, ext, wide, cols, lambda i, lane: band[i - 3, :, lane], range(3, rows + 3))

    def half(h, carry):
        for r in range(rows):
            acc = [taps[h, 49]] * groups
            for a in range(7):
                if not 3 <= r + a < rows + 3:
                    continue
                base = (h * ext + r + a) * wide + LEAD - 3
                tap = [taps[h, a * 7 + b] for b in range(7)]
                for jj in range(groups + 6):
                    x = strided(pad, base + jj, groups)
                    for b in range(7):
                        if 0 <= jj - b < groups:
                            acc[jj - b] = acc[jj - b] + tap[b] * x
            for j in range(groups):
                conv[pl.ds((h * rows + r) * cpitch + j, SUB, stride=groups), :] = acc[j]
        return carry

    lax.fori_loop(0, halves, half, 0)


def forward_kernel(
    band, within, across, got0, got1, got2, got3, cot, taps, gain, shift, bias2, scale, bias1, w1, w2, part, match,
    result_out, pad_out, grad_out, mine, other, plain_near, plain_far, rim, vecs, bias_out,
    result, pad, grad, conv, normed, act, pre, gbr, tmp, strip, sems,
):
    rows, cols, channels = band.shape
    halves = channels // LANES
    pitch = cols + 2 * LEAD
    wide = pitch + SUB
    ext = rows + 6
    groups = cols // SUB + 1
    cpitch = groups * SUB
    hidden = w1.shape[1]

    near, turn_near, turn_far = gluing(match)
    arrived = unpack_columns(near, turn_near, turn_far, (got0, got1, got2, got3))

    up, down = above_below(within, across)

    def source(i, lane):
        if i < 3:
            return up(i, slice(None), lane)
        return band[i - 3, :, lane] if i < rows + 3 else down(i - rows - 3, slice(None), lane)

    fill_pad(pad, halves, ext, wide, cols, source, range(ext))
    for h in range(halves):
        for d in range(3):
            for side in range(2):
                col = LEAD - 1 - d if side == 0 else LEAD + cols + d
                v = arrived(side, h, d)
                at = h * ext * wide + col
                pad[pl.ds(at, SUB, stride=wide), :] = v[0:SUB]
                pad[pl.ds(at + SUB * wide, ext - SUB, stride=wide), :] = v[SUB:ext]
        for r in range(rows):
            at = (h * rows + r) * pitch
            grad[at : at + LEAD, :] = jnp.zeros((LEAD, LANES), F32)
            grad[at + LEAD + cols : at + pitch, :] = jnp.zeros((LEAD, LANES), F32)

    keep_pad = pltpu.make_async_copy(pad, pad_out, sems.at[0])
    keep_pad.start()
    tail = halves * rows * pitch
    grad[tail : tail + SUB, :] = jnp.zeros((SUB, LANES), F32)

    where = lax.broadcasted_iota(jnp.int32, (SUB, LANES), 0)
    at_west, at_east = where == 0, where == SUB - 1
    none = jnp.zeros((SUB, LANES), F32)
    over = cols + 3 - (SUB - 1) * groups

    def complete(h, carry):
        for r in range(rows):
            acc = [strided(part, (h * rows + r) * cpitch + j, groups) for j in range(groups)]
            for a in range(7):
                base = (h * ext + r + a) * wide + LEAD - 3
                tap = [taps[h, a * 7 + b] for b in range(7)]
                if not 3 <= r + a < rows + 3:
                    for jj in range(groups + 6):
                        x = strided(pad, base + jj, groups)
                        for b in range(7):
                            if 0 <= jj - b < groups:
                                acc[jj - b] = acc[jj - b] + tap[b] * x
                    continue
                for d in range(3):
                    x = jnp.where(at_west, strided(pad, base + d, groups), none)
                    for b in range(d + 1):
                        acc[d - b] = acc[d - b] + tap[b] * x
                    x = jnp.where(at_east, strided(pad, base + over + d, groups), none)
                    for b in range(4 + d, 7):
                        acc[over + d - b] = acc[over + d - b] + tap[b] * x
            for j in range(groups):
                conv[pl.ds((h * rows + r) * cpitch + j, SUB, stride=groups), :] = acc[j]
        return carry

    lax.fori_loop(0, halves, complete, 0)

    step = 2 * cols
    gain, shift, bias2, scale = gain[...], shift[...], bias2[...], scale[...]
    tiles = hidden // 256

    def chunk(m, carry):
        s_conv, s_gain, s_norm, s_cot, s_scale = carry
        at = pl.multiple_of(m * step, step)
        x = jnp.concatenate(
            [
                jnp.concatenate(
                    [
                        conv[pl.ds(pl.multiple_of((h * rows + 2 * m + k) * cpitch, 8), cols), :]
                        for k in range(2)
                    ],
                    axis=0,
                )
                for h in range(halves)
            ],
            axis=1,
        )
        centred = x - jnp.mean(x, axis=-1, keepdims=True)
        inverse = lax.rsqrt(jnp.mean(centred * centred, axis=-1, keepdims=True) + EPSILON)
        standard = centred * inverse
        lane_in = (standard * gain + shift).astype(BF16)
        normed[pl.ds(at, step), :] = lane_in
        tmp[...] = standard
        upstream = cot[pl.ds(2 * m, 2)].reshape(step, channels).astype(F32)
        g_branch = (upstream * scale).astype(BF16)
        gbr[pl.ds(at, step), :] = g_branch
        for n in range(tiles):
            hid = slice(n * 256, (n + 1) * 256)
            v = dot(lane_in, w1[:, hid], ((1,), (0,))) + bias1[:, hid]
            v2 = v * v
            half = 0.5 + 0.5 * jnp.tanh(v * (ROOT_COEF + ROOT_COEF * CUBIC_COEF * v2))
            act[pl.ds(at, step), hid] = (v * half).astype(BF16)
            slope = half * (
                1.0 + (1.0 - half) * (v * (2 * ROOT_COEF + 6 * ROOT_COEF * CUBIC_COEF * v2))
            )
            d_act = dot(g_branch, w2[hid, :], ((1,), (1,)))
            g_pre = (d_act * slope).astype(BF16)
            pre[pl.ds(at, step), hid] = g_pre
            bias_out[:, hid] += jnp.sum(g_pre.astype(F32), axis=0, keepdims=True)
        branch = dot(act[pl.ds(at, step), :], w2[...], ((1,), (0,))) + bias2
        residual = band[pl.ds(2 * m, 2)].reshape(step, channels).astype(F32)
        result[pl.ds(2 * m, 2)] = (
            (residual + scale * branch).astype(BF16).reshape(2, cols, channels)
        )
        s_cot = s_cot + jnp.sum(upstream, axis=0, keepdims=True)
        s_scale = s_scale + jnp.sum(upstream * branch, axis=0, keepdims=True)
        g_norm = dot(pre[pl.ds(at, step), :], w1[...], ((1,), (1,)))
        standard = tmp[...]
        u = g_norm * gain
        g_conv = (
            u
            - jnp.mean(u, axis=-1, keepdims=True)
            - standard * jnp.mean(u * standard, axis=-1, keepdims=True)
        ) * inverse
        for h in range(halves):
            for k in range(2):
                dst = (h * rows + 2 * m + k) * pitch + LEAD
                grad[pl.ds(pl.multiple_of(dst, 8), cols), :] = g_conv[
                    k * cols : (k + 1) * cols, h * LANES : (h + 1) * LANES
                ]
        s_conv = s_conv + jnp.sum(g_conv, axis=0, keepdims=True)
        s_gain = s_gain + jnp.sum(g_norm * standard, axis=0, keepdims=True)
        s_norm = s_norm + jnp.sum(g_norm, axis=0, keepdims=True)
        return (s_conv, s_gain, s_norm, s_cot, s_scale)

    bias_out[...] = jnp.zeros_like(bias_out)
    zero = jnp.zeros((1, channels), F32)
    sums = lax.fori_loop(0, rows // 2, chunk, (zero,) * 5)
    sums = (sums[0], sums[1], sums[2], sums[3] * scale, sums[4])
    vecs[...] = jnp.concatenate(list(sums) + [zero] * 3, axis=0)

    keep_grad = pltpu.make_async_copy(grad, grad_out, sems.at[1])
    keep_grad.start()
    keep_result = pltpu.make_async_copy(result, result_out, sems.at[2])
    keep_result.start()

    even = (lax.axis_index("tile") & 1) == 0
    for n in range(tiles):
        hid = slice(n * 256, (n + 1) * 256)
        g_expand = dot(normed[...], pre[:, hid], ((0,), (0,)))
        g_reduce = dot(act[:, hid], gbr[...], ((0,), (0,)))
        mine[hid, :] = jnp.where(even, g_expand, g_reduce)
        other[hid, :] = jnp.where(even, g_reduce, g_expand).astype(BF16)

    def rim_half(h, carry):
        for k in range(6):
            acc = spread_row(grad, taps, h, k if k < 3 else rows + k, rows, pitch, groups)
            for j in range(groups):
                rim[pl.ds((h * 6 + k) * cpitch + j, SUB, stride=groups), :] = acc[j]
        return carry

    lax.fori_loop(0, halves, rim_half, 0)
    first = near == 0
    strip[...] = jnp.zeros_like(strip)
    for h in range(halves):
        lane = slice(h * LANES, (h + 1) * LANES)

        def column(c, h=h):
            return grad[pl.ds(h * rows * pitch + LEAD + c, SUB, stride=pitch), :]

        for side in range(2):
            edge = [column(c if side == 0 else cols - 1 - c) for c in range(3)]
            for d in range(3):
                slot = ((side * 3 + d) * halves + h) * 32
                for a in range(7):
                    total = none
                    for c in range(3 - d):
                        b = 2 - d - c if side == 0 else 4 + d + c
                        total = total + taps[h, a * 7 + b] * edge[c]
                    strip[slot + a : slot + a + SUB, :] += total
                for o in range(ext):
                    strip[slot + 16 + o : slot + 17 + o, :] = strip[
                        slot + ext - 1 - o : slot + ext - o, :
                    ]
        for d in range(3):
            slots = [((side * 3 + d) * halves + h) * 32 for side in range(2)]
            for turned in range(2):
                west, east = [strip[k + 16 * turned : k + 16 * turned + 16, :] for k in slots]
                one = jnp.where(first, west, east).astype(BF16)
                two = jnp.where(first, east, west).astype(BF16)
                if turned:
                    other[hidden + 16 * d : hidden + 16 * d + 16, lane] = one
                    other[hidden + 48 + 16 * d : hidden + 64 + 16 * d, lane] = two
                else:
                    plain_near[16 * d : 16 * d + 16, lane] = one
                    plain_far[16 * d : 16 * d + 16, lane] = two
    keep_pad.wait()
    keep_grad.wait()
    keep_result.wait()


def spread_row(grad, taps, h, o, rows, pitch, groups):
    acc = [jnp.zeros((SUB, LANES), F32)] * groups
    for a in range(7):
        if not 0 <= o - a < rows:
            continue
        src = (h * rows + o - a) * pitch + LEAD + 3
        tap = [taps[h, a * 7 + b] for b in range(7)]
        for jj in range(-6, groups):
            x = strided(grad, src + jj, groups)
            for b in range(7):
                if 0 <= jj + b < groups:
                    acc[jj + b] = acc[jj + b] + tap[b] * x
    return acc


def inner_kernel(h, grad, taps, out, token):
    token[...] = jnp.zeros_like(token)
    rows = 8
    cpitch = out.shape[0] // rows
    pitch = cpitch + LEAD
    groups = cpitch // SUB
    for r in range(rows):
        acc = spread_row(grad, taps, h, r + 3, rows, pitch, groups)
        for j in range(groups):
            out[pl.ds(r * cpitch + j, SUB, stride=groups), :] = acc[j]


def taps_kernel(h, grad, pad, out, token):
    token[...] = jnp.zeros_like(token)
    halves, rows = 2, 8
    ext = rows + 6
    pitch = (grad.shape[0] - SUB) // (halves * rows)
    wide = pad.shape[0] // (halves * ext)
    cols = pitch - 2 * LEAD
    groups = cols // SUB + 1

    def some(first, count):
        acc = [[jnp.zeros((SUB, LANES), F32)] * 7 for _ in range(count)]
        for i in range(rows + count - 1):
            base = (h * ext + i + first) * wide + LEAD - 3
            use = [k for k in range(count) if 0 <= i - k < rows]
            g = {}
            for jj in range(groups + 6):
                if jj < groups:
                    for k in use:
                        at = (h * rows + i - k) * pitch + LEAD + jj
                        g[k, jj] = strided(grad, at, groups)
                x = strided(pad, base + jj, groups)
                for b in range(7):
                    j = jj - b
                    if 0 <= j < groups:
                        for k in use:
                            acc[k][b] = acc[k][b] + g[k, j] * x
        for k in range(count):
            for b in range(7):
                out[pl.ds((first + k) * 7 + b, 1), :] = jnp.sum(acc[k][b], axis=0, keepdims=True)

    def pair(p, carry):
        some(2 * p, 2)
        return carry

    lax.fori_loop(0, 3, pair, 0)
    some(6, 1)


def rims_kernel(rim, got0, got1, got2, got3, match, within, across, token, total, held):
    token[...] = jnp.zeros_like(token)
    halves, _, cols, _ = within.shape
    even = (lax.axis_index("tile") & 1) == 0
    cpitch = rim.shape[0] // (halves * 6)
    near, turn_near, turn_far = gluing(match)
    arrived = unpack_columns(near, turn_near, turn_far, (got0, got1, got2, got3))
    for h in range(halves):
        for k in range(6):
            total[k * cols : (k + 1) * cols, :] = rim[
                (h * 6 + k) * cpitch : (h * 6 + k) * cpitch + cols, :
            ]
        for side in range(2):
            for d in range(3):
                held[...] = arrived(side, h, d)
                for k in range(6):
                    o = k if k < 3 else k + 8
                    at = k * cols + (d if side == 0 else cols - 1 - d)
                    total[at : at + 1, :] += held[o : o + 1, :]
        for k in range(3):
            top = total[k * cols : (k + 1) * cols, :].astype(BF16)
            bottom = total[(k + 3) * cols : (k + 4) * cols, :].astype(BF16)
            within[h, k] = jnp.where(even, bottom, top)
            across[h, k] = jnp.where(even, top, bottom)


def fields_kernel(inner0, inner1, within, across, got0, got1, got2, got3, cot, match, out, total, held):
    rows, cols, channels = cot.shape
    halves = channels // LANES
    cpitch = inner0.shape[0] // rows
    from_up, from_down = above_below(within, across)
    near, turn_near, turn_far = gluing(match)
    arrived = unpack_columns(near, turn_near, turn_far, (got0, got1, got2, got3))
    for h in range(halves):
        lane = slice(h * LANES, (h + 1) * LANES)
        for r in range(rows):
            at = r * cpitch
            own = (inner0, inner1)[h][at : at + cols, :] + cot[r, :, lane].astype(F32)
            if r < 3:
                own = own + from_up(h, r).astype(F32)
            if r >= rows - 3:
                own = own + from_down(h, r - rows + 3).astype(F32)
            total[r * cols : (r + 1) * cols, :] = own
        for side in range(2):
            for d in range(3):
                held[...] = arrived(side, h, d)
                at = pl.ds(d if side == 0 else cols - 1 - d, SUB, stride=cols)
                total[at, :] = total[at, :] + held[3 : 3 + rows, :]
        for r in range(rows):
            out[r, :, lane] = total[r * cols : (r + 1) * cols, :].astype(BF16)


def finish_kernel(factor, faces, chips, mine, peer, small, expand, reduce, g_taps, g_bias, vecs):
    hidden, channels = reduce.shape
    count = hidden // (faces * chips)
    face = lax.axis_index("face")
    chip = lax.axis_index("tile") >> 1
    even = (lax.axis_index("tile") & 1) == 0
    for f in range(faces):
        for z in range(chips):
            at = (f * chips + z) * count
            own = mine[at : at + count, :].astype(F32) * factor
            got = peer[at : at + count, :].astype(F32) * factor
            to = ((face ^ f) * chips + (chip ^ z)) * count
            reduce[pl.ds(pl.multiple_of(to, count), count), :] = jnp.where(even, got, own)
            row = pl.multiple_of(lax.rem(to, channels), count)
            col = pl.multiple_of((to // channels) * channels, channels)
            expand[pl.ds(row, count), pl.ds(col, channels)] = jnp.where(even, own, got)
    for a in range(7):
        g_taps[a] = small[a * 7 : a * 7 + 7, :] * factor
    for n in range(hidden // channels):
        g_bias[:, n * channels : (n + 1) * channels] = small[49 + n : 50 + n, :] * factor
    first = 49 + hidden // channels
    vecs[...] = small[first : first + 5, :] * factor


def face_swap(x, mask, turned=False):
    faces, tiles = lax.axis_size("face"), lax.axis_size("tile")
    pairs = [
        (f * tiles + t, (f ^ mask) * tiles + (tiles - 1 - t if turned else t))
        for f in range(faces)
        for t in range(tiles)
    ]
    return lax.ppermute(x, ("face", "tile"), pairs)


def glued_swap(strips):
    near_plain, near_turned, far_plain, far_turned = strips
    half = lax.axis_size("face") // 2
    return (
        face_swap(near_plain, 1),
        face_swap(near_turned, 1, True),
        face_swap(far_plain, half),
        face_swap(far_turned, half, True),
    )


def row_swap(within, across):
    count = lax.axis_size("tile")
    pairs = [(i, i + 1) for i in range(1, count - 1, 2)]
    return (
        swapped(within, "tile", 1),
        lax.ppermute(across, "tile", pairs + [(j, i) for i, j in pairs]),
    )


def above_below(within, across):
    even = (lax.axis_index("tile") & 1) == 0

    def up(*at):
        return jnp.where(even, across[at], within[at])

    def down(*at):
        return jnp.where(even, within[at], across[at])

    return up, down


def swapped(x, axis, mask):
    return lax.ppermute(x, axis, [(i, i ^ mask) for i in range(lax.axis_size(axis))])


def tree_sum(parts):
    parts = [p.astype(F32) for p in parts]
    while len(parts) > 1:
        parts = [parts[i] + parts[i + 1] for i in range(0, len(parts), 2)]
    return parts[0]


def joined(x, riders):
    return jnp.concatenate([x] + list(riders), 0) if riders else x


def scatter_start(x, axis, masks, index, riders):
    shares = x.reshape((len(masks) + 1, x.shape[0] // (len(masks) + 1)) + x.shape[1:])
    step = masks[0]
    cut = shares.shape[1]
    own = lax.dynamic_index_in_dim(shares, index, 0, keepdims=False)
    sent = [
        lax.dynamic_index_in_dim(shares, index ^ (m // step), 0, keepdims=False).astype(BF16)
        for m in masks
    ]
    got = [swapped(joined(v, riders.get(m)), axis, m) for v, m in zip(sent, masks)]
    return [own] + [g[:cut] for g in got], {m: got[masks.index(m)][cut:] for m in riders}


def gather_start(x, small, axis, masks):
    sent = jnp.concatenate([x, small.astype(BF16)], 0)
    return [swapped(sent, axis, m) for m in masks]


def gather_done(x, small, got):
    cut = x.shape[0]
    pieces = jnp.concatenate([x] + [g[:cut] for g in got], 0)
    return pieces, tree_sum([small.astype(BF16)] + [g[cut:] for g in got])


def ordered(x, token):
    blocks = x.reshape(x.shape[0] // SUB, SUB, x.shape[1] // LANES, LANES)
    return (blocks + token[None, :, None, :]).reshape(x.shape)


def shards(
    fields,
    cotangent,
    edge_match,
    depth_kernel,
    depth_bias,
    norm_gain,
    norm_bias,
    expand_weight,
    expand_bias,
    reduce_weight,
    reduce_bias,
    layer_scale,
):
    band = fields[0]
    cot = cotangent[0]
    rows, cols, channels = band.shape
    halves = channels // LANES
    hidden = expand_weight.shape[1]
    pitch = cols + 2 * LEAD
    wide = pitch + SUB
    ext = rows + 6
    cells = rows * cols
    faces, tiles = lax.axis_size("face"), lax.axis_size("tile")
    shape = jax.ShapeDtypeStruct
    strips = [shape((48, channels), BF16)] * 4

    *rim_rows, columns = call(
        ends_kernel,
        [
            shape((3, cols, channels), BF16),
            shape((3, cols, channels), BF16),
            shape((rows, 32, channels), BF16),
        ],
        [],
        1_000_000_000,
        (band,),
    )
    beside = row_swap(*rim_rows)
    sides = call(
        edges_kernel,
        strips,
        [pltpu.VMEM((2, 16 * SUB, LANES), F32)],
        900_000_000,
        (columns, *beside, edge_match),
        smem=1,
    )
    got = glued_swap(sides)
    part, taps = call(
        own_rows_kernel,
        [
            pltpu.VMEM((halves * rows * (cols + SUB), LANES), F32),
            pltpu.VMEM((halves, 50, SUB, LANES), F32),
        ],
        [pltpu.VMEM((halves * ext * wide, LANES), F32)],
        4_500_000_000,
        (band, depth_kernel, depth_bias[None]),
        limit=4,
        after=(sides[0],),
    )
    part, taps = kept(part), kept(taps)
    sign = shape((SUB, LANES), F32)
    result, pad, grad, mine, other, plain_near, plain_far, rim, vecs, bias_out = call(
        forward_kernel,
        [
            pltpu.HBM(band.shape, BF16),
            pltpu.HBM((halves * ext * wide, LANES), F32),
            pltpu.HBM((halves * rows * pitch + SUB, LANES), F32),
            shape((hidden, channels), F32),
            shape((hidden + 96, channels), BF16),
            shape((48, channels), BF16),
            shape((48, channels), BF16),
            shape((halves * 6 * (cols + SUB), LANES), F32),
            shape((8, channels), F32),
            shape((1, hidden), F32),
        ],
        [
            pltpu.VMEM(band.shape, BF16),
            pltpu.VMEM((halves * ext * wide, LANES), F32),
            pltpu.VMEM((halves * rows * pitch + SUB, LANES), F32),
            pltpu.VMEM((halves * rows * (cols + SUB), LANES), F32),
            pltpu.VMEM((cells, channels), BF16),
            pltpu.VMEM((cells, hidden), BF16),
            pltpu.VMEM((cells, hidden), BF16),
            pltpu.VMEM((cells, channels), BF16),
            pltpu.VMEM((2 * cols, channels), F32),
            pltpu.VMEM((12 * 32, LANES), F32),
            pltpu.SemaphoreType.DMA((3,)),
        ],
        12_000_000_000,
        (
            band, *beside, *got, cot, taps, norm_gain[None], norm_bias[None], reduce_bias[None],
            layer_scale[None], expand_bias.reshape(1, hidden), expand_weight, reduce_weight, part,
            edge_match,
        ),
        smem=1,
        limit=20,
        left=(0, 1, 2),
    )

    face_masks = list(range(1, faces))
    chip_masks = list(range(2, tiles, 2))
    half, mirror = faces // 2, tiles - 2
    peer = swapped(other, "tile", 1)
    turned_near, turned_far = peer[hidden : hidden + 48], peer[hidden + 48 :]

    def half_taps(h, after):
        return call(
            lambda *refs: taps_kernel(h, *refs),
            [shape((56, LANES), F32), sign],
            [],
            3_500_000_000,
            (grad, pad),
            after=after,
        )

    riders = {1: [plain_near, turned_near], half: [plain_far, turned_far]}
    total = (mine + peer[:hidden].astype(F32)).astype(BF16)
    got, rode = scatter_start(total, "face", face_masks, lax.axis_index("face"), riders)
    taps0, token = half_taps(0, (turned_near,))
    share = ordered(tree_sum(got), token)
    plain_near, turned_near = rode[1][:48], rode[1][48:]
    plain_far, turned_far = rode[half][:48], rode[half][48:]
    riders = {mirror: [turned_near, turned_far]}
    got, rode = scatter_start(share, "tile", chip_masks, lax.axis_index("tile") >> 1, riders)
    taps1, token = half_taps(1, (got[1],))
    share = ordered(tree_sum(got), token).astype(BF16)
    columns = (plain_near, rode[mirror][:48], plain_far, rode[mirror][48:])
    small = jnp.concatenate(
        [
            jnp.concatenate([taps0[:49], taps1[:49]], 1),
            bias_out.reshape(hidden // channels, channels),
            vecs[0:5],
            jnp.zeros((SMALL - 54 - hidden // channels, channels), F32),
        ],
        0,
    )
    def half_inner(h, after):
        return call(
            lambda *refs: inner_kernel(h, *refs),
            [shape((rows * (cols + SUB), LANES), F32), sign],
            [],
            2_100_000_000,
            (grad, taps),
            after=after,
        )

    got = gather_start(share, small, "tile", chip_masks)
    within, across, token = call(
        rims_kernel,
        [shape((halves, 3, cols, LANES), BF16)] * 2 + [sign],
        [pltpu.VMEM((6 * cols, LANES), F32), pltpu.VMEM((16, LANES), F32)],
        900_000_000,
        (rim, *columns, edge_match),
        smem=1,
    )
    inner0, token = half_inner(0, (token, got[0]))
    arrived = row_swap(within, across)
    pieces, small = gather_done(share, small, got)
    small = ordered(small, token)
    got = gather_start(pieces, small, "face", face_masks)
    inner1, token = half_inner(1, (got[0], arrived[1]))
    pieces, small = gather_done(pieces, small, got)
    small = ordered(small, token).astype(BF16)
    peer = swapped(jnp.concatenate([pieces, small], 0), "tile", 1)
    (grad_fields,) = call(
        fields_kernel,
        [shape(band.shape, BF16)],
        [pltpu.VMEM((cells, LANES), F32), pltpu.VMEM((16, LANES), F32)],
        2_000_000_000,
        (inner0, inner1, *arrived, *columns, cot, edge_match),
        smem=1,
    )
    small = small.astype(F32) + peer[hidden:].astype(F32)

    factor = 1.0 / math.sqrt(faces * tiles * cells)

    def finish(*refs):
        finish_kernel(factor, faces, tiles // 2, *refs)

    g_expand, g_reduce, g_taps, g_bias, g_vecs = call(
        finish,
        [
            shape((channels, hidden), F32),
            shape((hidden, channels), F32),
            shape((7, 7, channels), F32),
            shape((1, hidden), F32),
            shape((5, channels), F32),
        ],
        [],
        2_000_000_000,
        (pieces, peer[:hidden], small),
    )
    return (
        result[None],
        grad_fields[None],
        g_taps,
        g_expand,
        g_reduce,
        g_bias.reshape(hidden),
        g_vecs,
    )


def solution(mesh):
    return jax.shard_map(
        shards,
        mesh=mesh,
        in_specs=(P("face", "tile"), P("face", "tile")) + (P(),) * 10,
        out_specs=(P("face", "tile"), P("face", "tile")) + (P(),) * 5,
        check_vma=False,
    )
```

time: 132 us -> 87.2 us (0.66)
  local copies, waits for them, and re-layouts: 18.1 us -> 2.7 us
  starting transfers between devices: 46.5 us -> 31.5 us
  waiting for transfers between devices: 28.8 us -> 20.1 us
  other arithmetic: 6.88 us -> 2.19 us
  between operations: 3.38 us -> 1.08 us
  Pallas kernels: 27.9 us -> 29.4 us
    ppermute x12 -> x6, starting transfers between devices: 24.7 us -> 8.8 us  [the longest x4 7.48 us: face_swap(): return lax.ppermute(x, ('face', 'tile'), pairs)]
    ppermute x23 -> x16, waiting for transfers between devices: 25.4 us -> 18.4 us  [swapped(): lax.ppermute(x, axis, [(i, i ^ mask) for i in range(lax.axis_size(axis))])]
    unnamed x40 -> x46, local copies, waits for them, and re-layouts: 6.42 us -> 1.57 us
    slice x11 -> x8, local copies, waits for them, and re-layouts: 4.01 us -> 0.91 us  [the longest x1 0.85 us: shards(): turned_near, turned_far = (peer[hidden:hidden + 48], peer[hidden + 48:])]
    dynamic_slice x6 -> x0, local copies, waits for them, and re-layouts: 2.23 us -> none  [the longest x1 1.34 us: partner_swap(): reverse = own[side, 2] == 1]
    add x13 -> x3, other arithmetic: 2.24 us -> 0.12 us  [the longest x1 0.07 us: tree_sum(): parts = [parts[i] + parts[i + 1] for i in range(0, len(parts), 2)]]
    reshape x4 -> x0, local copies, waits for them, and re-layouts: 2.07 us -> none  [the longest x1 1.09 us: shards(): g_expand.reshape(hidden // 256, 256, 256).transpose(1, 0, 2)]
    ppermute x12 -> x6, waiting for transfers between devices: 3.39 us -> 1.69 us  [the longest x4 1.69 us: face_swap(): return lax.ppermute(x, ('face', 'tile'), pairs)]
  transfers between devices with their start and end apart: 35 -> 22, of which waited for: 20 -> 10; matrix products, arithmetic and copies ran while one was open for 11% -> 0% of each run, Pallas kernels for 0% -> 19%
where the time goes in v2:
time: 87.2 us; the launch traced here: 86.9 us
  starting transfers between devices  31.5 us (36%)
  Pallas kernels  29.4 us (34%)
  waiting for transfers between devices  20.1 us (23%)
  local copies, waits for them, and re-layouts  2.7 us (3%)
  other arithmetic  2.19 us (3%)
  between operations  1.08 us (1%)
    pallas_call x11, Pallas kernels, call(): pl.pallas_call(run, out_shape=outs, in_specs=[vmem] * (count - smem) + [s...  29.4 us
    ppermute x16, starting transfers between devices, swapped(): lax.ppermute(x, axis, [(i, i ^ mask) for i in range(lax.axis_size(axis))])  22.7 us
    ppermute x16, waiting for transfers between devices, swapped(): lax.ppermute(x, axis, [(i, i ^ mask) for i in range(lax.axis_size(axis))])  18.4 us
    ppermute x4, starting transfers between devices, face_swap(): return lax.ppermute(x, ('face', 'tile'), pairs)  7.48 us
  transfers between devices with their start and end apart: 22, of which 10 were waited for; matrix products, arithmetic and copies ran while one was open for 0% of the time, Pallas kernels for 19%

profile of v2, /device:TPU:0, one launch (start us, length us, event | category | flops | bytes accessed | tf_op | source)
XLA Modules:
  0.0 86.9 jit_solution(7546315337628515739)
XLA Ops:
  0.6 1.0 %copy-done = bf16[1,8,128,256]{3,2,1,0:T(8,128)(2,1)S(1)} copy-done((bf16[1,8,128,256]{3,2,1,0:T(8,128)(2,1)S(1)}, bf16[1,8,128,256]{3,2,1,0:T(8,128)(2,1)}, u32[]{:S(2)}) %copy-start) | copy-done | bytes 524312
  1.7 0.5 collective-permute-start
  2.2 0.7 collective-permute-start.1
  2.9 0.1 copy.19.refs_3_.refs_17_.refs_5_.refs_9_
  3.0 0.3 collective-permute-done.refs_1_
  3.3 0.7 shard_map.172
  4.0 2.9 %collective-permute-start.2 = (bf16[48,256]{1,0:T(8,128)(2,1)S(1)}, bf16[48,256]{1,0:T(8,128)(2,1)S(1)}, u32[]{:S(2)}, u32[]{:S(2)}) collective-permute-start(bf16[48,256]{1,0:T(8,128)(2,1)S(1)} %get-tuple-element.45.refs_3_), channel_id=1, source_target_pairs={{0,8},{1,9},{2,10},{3,11},{4,12},{5,13},{6,14},{7,15},{8,0},{9,1},... | collective-permute-start | bytes 73736 | tf_op jit(solution)/shard_map/ppermute | solution.py:533
  6.9 3.0 %collective-permute-start.3 = (bf16[48,256]{1,0:T(8,128)(2,1)S(1)}, bf16[48,256]{1,0:T(8,128)(2,1)S(1)}, u32[]{:S(2)}, u32[]{:S(2)}) collective-permute-start(bf16[48,256]{1,0:T(8,128)(2,1)S(1)} %get-tuple-element.46), channel_id=1, source_target_pairs={{0,15},{1,14},{2,13},{3,12},{4,11},{5,10},{6,9},{7,8},{8,7},{9,6},... | collective-permute-start | bytes 73736 | tf_op jit(solution)/shard_map/ppermute | solution.py:533
  10.0 1.5 %collective-permute-start.4 = (bf16[48,256]{1,0:T(8,128)(2,1)S(1)}, bf16[48,256]{1,0:T(8,128)(2,1)S(1)}, u32[]{:S(2)}, u32[]{:S(2)}) collective-permute-start(bf16[48,256]{1,0:T(8,128)(2,1)S(1)} %get-tuple-element.47), channel_id=1, source_target_pairs={{0,16},{1,17},{2,18},{3,19},{4,20},{5,21},{6,22},{7,23},{8,24},{9,... | collective-permute-start | bytes 73736 | tf_op jit(solution)/shard_map/ppermute | solution.py:533
  11.6 4.1 %shard_map.173 = (f32[2176,128]{1,0:T(8,128)S(1)}, f32[2,50,8,128]{3,2,1,0:T(8,128)S(1)}) custom-call(bf16[8,128,256]{2,1,0:T(8,128)(2,1)S(1)} %bitcast.52, bf16[7,7,256]{2,1,0:T(8,128)(2,1)S(1)} %copy-done.5, f32[1,256]{1,0:T(1,128)S(1)} %bitcast.57, bf16[48,256]{1,0:T(8,128)(2,1)S(1)} %get-tuple-element.45.refs_3_), custom_call_target="tpu_custom_call" | custom-call | flops 4499999744 | bytes 1048576 | tf_op jit(solution)/shard_map/pallas_call | solution.py:35
  15.8 1.7 %collective-permute-done.5.refs_6_ = bf16[48,256]{1,0:T(8,128)(2,1)S(1)} collective-permute-done((bf16[48,256]{1,0:T(8,128)(2,1)S(1)}, bf16[48,256]{1,0:T(8,128)(2,1)S(1)}, u32[]{:S(2)}, u32[]{:S(2)}) %collective-permute-start.5) | collective-permute-done | bytes 24608 | tf_op jit(solution)/shard_map/ppermute | solution.py:533
  17.5 10.4 %shard_map.174 = (bf16[8,128,256]{2,1,0:T(8,128)(2,1)}, f32[4256,128]{1,0:T(8,128)}, f32[2312,128]{1,0:T(8,128)}, f32[1024,256]{1,0:T(8,128)S(1)}, bf16[1120,256...) custom-call(bf16[8,128,256]{2,1,0:T(8,128)(2,1)S(1)} %bitcast.53, ...), custom_call_target="tpu_custom_call" | custom-call | flops 12000000000 | bytes 1048576 | tf_op jit(solution)/shard_map/pallas_call | solution.py:35
  27.9 6.0 %collective-permute-start.6 = (bf16[1120,256]{1,0:T(8,128)(2,1)S(1)}, bf16[1120,256]{1,0:T(8,128)(2,1)}, u32[]{:S(2)}, u32[]{:S(2)}) collective-permute-start(bf16[1120,256]{1,0:T(8,128)(2,1)S(1)} %get-tuple-element.55), channel_id=1, source_target_pairs={{0,1},{1,0},{2,3},{3,2},{4,5},{5,4},{6,7},{7,6},{8,9},{9,8},{10,11... | collective-permute-start | bytes 1720328 | tf_op jit(solution)/shard_map/ppermute | solution.py:569
  33.9 1.7 %collective-permute-done.6 = bf16[1120,256]{1,0:T(8,128)(2,1)} collective-permute-done((bf16[1120,256]{1,0:T(8,128)(2,1)S(1)}, bf16[1120,256]{1,0:T(8,128)(2,1)}, u32[]{:S(2)}, u32[]{:S(2)}) %collective-permute-start.6) | collective-permute-done | bytes 573472 | tf_op jit(solution)/shard_map/ppermute | solution.py:569
  35.6 1.3 %add_convert_fusion = bf16[1024,256]{1,0:T(8,128)(2,1)S(1)} fusion(f32[1024,256]{1,0:T(8,128)S(1)} %get-tuple-element.54, bf16[1120,256]{1,0:T(8,128)(2,1)} %collective-permute-done.6), kind=kLoop, calls=%fused_computation | loop fusion | flops 786432 | bytes 2097152 | tf_op jit(solution)/shard_map/convert_element_type | solution.py:729
  37.0 0.8 fusion.11
  37.9 0.6 collective-permute-start.8
  38.5 1.6 %collective-permute-start.7 = (bf16[352,256]{1,0:T(8,128)(2,1)S(1)}, bf16[352,256]{1,0:T(8,128)(2,1)S(1)}, u32[]{:S(2)}, u32[]{:S(2)}) collective-permute-start(bf16[352,256]{1,0:T(8,128)(2,1)S(1)} %pad_maximum_fusion), channel_id=1, source_target_pairs={{0,8},{8,0},{16,24},{24,16},{1,9},{9,1},{17,25},{25,17},{2,10},{10... | collective-permute-start | bytes 540680 | tf_op jit(solution)/shard_map/ppermute | solution.py:569
  40.0 1.5 %collective-permute-start.9 = (bf16[256,256]{1,0:T(8,128)(2,1)S(1)}, bf16[256,256]{1,0:T(8,128)(2,1)S(1)}, u32[]{:S(2)}, u32[]{:S(2)}) collective-permute-start(bf16[256,256]{1,0:T(8,128)(2,1)S(1)} %get-tuple-element.85), channel_id=1, source_target_pairs={{0,24},{8,16},{16,8},{24,0},{1,25},{9,17},{17,9},{25,1},{2,26},{10... | collective-permute-start | bytes 393224 | tf_op jit(solution)/shard_map/ppermute | solution.py:569
  41.5 3.0 %shard_map.175 = (f32[56,128]{1,0:T(8,128)S(1)}, f32[8,128]{1,0:T(8,128)S(1)}) custom-call(f32[2312,128]{1,0:T(8,128)S(1)} %copy-done.12, f32[4256,128]{1,0:T(8,128)S(1)} %copy-done.14, bf16[48,256]{1,0:T(8,128)(2,1)S(1)} %get-tuple-element.84.refs_2_), custom_call_target="tpu_custom_call" | custom-call | flops 3500000000 | bytes 1048576 | tf_op jit(solution)/shard_map/pallas_call | solution.py:35
  44.6 4.3 %collective-permute-done.9 = bf16[256,256]{1,0:T(8,128)(2,1)S(1)} collective-permute-done((bf16[256,256]{1,0:T(8,128)(2,1)S(1)}, bf16[256,256]{1,0:T(8,128)(2,1)S(1)}, u32[]{:S(2)}, u32[]{:S(2)}) %collective-permute-start.9) | collective-permute-done | bytes 131104 | tf_op jit(solution)/shard_map/ppermute | solution.py:569
  49.0 0.1 collective-permute-start.11
  49.1 1.9 %collective-permute-start.10 = (bf16[160,256]{1,0:T(8,128)(2,1)S(1)}, bf16[160,256]{1,0:T(8,128)(2,1)S(1)}, u32[]{:S(2)}, u32[]{:S(2)}) collective-permute-start(bf16[160,256]{1,0:T(8,128)(2,1)S(1)} %pad_maximum_fusion.2), channel_id=1, source_target_pairs={{0,6},{1,7},{2,4},{3,5},{4,2},{5,3},{6,0},{7,1},{8,14},{9,15},{10,... | collective-permute-start | bytes 245768 | tf_op jit(solution)/shard_map/ppermute | solution.py:569
  51.0 1.6 %collective-permute-start.12 = (bf16[64,256]{1,0:T(8,128)(2,1)S(1)}, bf16[64,256]{1,0:T(8,128)(2,1)S(1)}, u32[]{:S(2)}, u32[]{:S(2)}) collective-permute-start(bf16[64,256]{1,0:T(8,128)(2,1)S(1)} %get-tuple-element.88), channel_id=1, source_target_pairs={{0,4},{1,5},{2,6},{3,7},{4,0},{5,1},{6,2},{7,3},{8,12},{9,13},{10,... | collective-permute-start | bytes 98312 | tf_op jit(solution)/shard_map/ppermute | solution.py:569
  52.7 1.2 %collective-permute-done.11.refs_2_ = bf16[64,256]{1,0:T(8,128)(2,1)S(1)} collective-permute-done((bf16[64,256]{1,0:T(8,128)(2,1)S(1)}, bf16[64,256]{1,0:T(8,128)(2,1)S(1)}, u32[]{:S(2)}, u32[]{:S(2)}) %collective-permute-start.11) | collective-permute-done | bytes 32800 | tf_op jit(solution)/shard_map/ppermute | solution.py:569
  53.9 3.1 %shard_map.177 = (f32[56,128]{1,0:T(8,128)S(1)}, f32[8,128]{1,0:T(8,128)S(1)}) custom-call(f32[2312,128]{1,0:T(8,128)S(1)} %copy-done.12, f32[4256,128]{1,0:T(8,128)S(1)} %copy-done.14, bf16[64,256]{1,0:T(8,128)(2,1)S(1)} %collective-permute-done.11.refs_2_), custom_call_target="tpu_custom_call" | custom-call | flops 3500000000 | bytes 1048576 | tf_op jit(solution)/shard_map/pallas_call | solution.py:35
  57.0 0.1 collective-permute-done.12
  57.1 0.6 constant_dynamic-update-slice_fusion.13
  57.8 0.1 concatenate.38
  57.9 0.3 collective-permute-start.13
  58.1 2.1 %collective-permute-start.14 = (bf16[128,256]{1,0:T(8,128)(2,1)S(1)}, bf16[128,256]{1,0:T(8,128)(2,1)S(1)}, u32[]{:S(2)}, u32[]{:S(2)}) collective-permute-start(bf16[128,256]{1,0:T(8,128)(2,1)S(1)} %concatenate.38), channel_id=1, source_target_pairs={{0,4},{1,5},{2,6},{3,7},{4,0},{5,1},{6,2},{7,3},{8,12},{9,13},{10,... | collective-permute-start | bytes 196616 | tf_op jit(solution)/shard_map/ppermute | solution.py:569
  60.2 2.1 %collective-permute-start.15 = (bf16[128,256]{1,0:T(8,128)(2,1)S(1)}, bf16[128,256]{1,0:T(8,128)(2,1)S(1)}, u32[]{:S(2)}, u32[]{:S(2)}) collective-permute-start(bf16[128,256]{1,0:T(8,128)(2,1)S(1)} %concatenate.38), channel_id=1, source_target_pairs={{0,6},{1,7},{2,4},{3,5},{4,2},{5,3},{6,0},{7,1},{8,14},{9,15},{10,... | collective-permute-start | bytes 196616 | tf_op jit(solution)/shard_map/ppermute | solution.py:569
  62.4 0.8 shard_map.176
  63.1 0.3 copy-done.18
  63.4 1.3 %collective-permute-done.14 = bf16[128,256]{1,0:T(8,128)(2,1)S(1)} collective-permute-done((bf16[128,256]{1,0:T(8,128)(2,1)S(1)}, bf16[128,256]{1,0:T(8,128)(2,1)S(1)}, u32[]{:S(2)}, u32[]{:S(2)}) %collective-permute-start.14) | collective-permute-done | bytes 65568 | tf_op jit(solution)/shard_map/ppermute | solution.py:569
  64.7 2.0 %shard_map.178 = (f32[1088,128]{1,0:T(8,128)S(1)}, f32[8,128]{1,0:T(8,128)S(1)}) custom-call(f32[2312,128]{1,0:T(8,128)S(1)} %copy-done.13, f32[2,50,8,128]{3,2,1,0:T(8,128)S(1)} %copy-done.16, f32[8,128]{1,0:T(8,128)S(1)} %get-tuple-element.60.refs_2_, bf16[128,256]{1,0:T(8,128)(2,1)S(1)} %collective-permute-done.13.refs_3_), custom_call_target="tpu_custom_call" | custom-call | flops 2100000000 | bytes 1048576 | tf_op jit(solution)/shard_map/pallas_call | solution.py:35
  66.8 1.5 %collective-permute-start.16 = (bf16[320,256]{1,0:T(8,128)(2,1)S(1)}, bf16[320,256]{1,0:T(8,128)(2,1)S(1)}, u32[]{:S(2)}, u32[]{:S(2)}) collective-permute-start(bf16[320,256]{1,0:T(8,128)(2,1)S(1)} %get-tuple-element.105), channel_id=1, source_target_pairs={{0,8},{8,0},{16,24},{24,16},{1,9},{9,1},{17,25},{25,17},{2,10},{10... | collective-permute-start | bytes 491528 | tf_op jit(solution)/shard_map/ppermute | solution.py:569
  68.4 0.7 collective-permute-start.17
  69.0 1.1 %collective-permute-start.19 = (bf16[320,256]{1,0:T(8,128)(2,1)S(1)}, bf16[320,256]{1,0:T(8,128)(2,1)S(1)}, u32[]{:S(2)}, u32[]{:S(2)}) collective-permute-start(bf16[320,256]{1,0:T(8,128)(2,1)S(1)} %get-tuple-element.105), channel_id=1, source_target_pairs={{0,16},{8,24},{16,0},{24,8},{1,17},{9,25},{17,1},{25,9},{2,18},{10... | collective-permute-start | bytes 491528 | tf_op jit(solution)/shard_map/ppermute | solution.py:569
  70.2 1.0 %collective-permute-start.20 = (bf16[320,256]{1,0:T(8,128)(2,1)S(1)}, bf16[320,256]{1,0:T(8,128)(2,1)S(1)}, u32[]{:S(2)}, u32[]{:S(2)}) collective-permute-start(bf16[320,256]{1,0:T(8,128)(2,1)S(1)} %get-tuple-element.105), channel_id=1, source_target_pairs={{0,24},{8,16},{16,8},{24,0},{1,25},{9,17},{17,9},{25,1},{2,26},{10... | collective-permute-start | bytes 491528 | tf_op jit(solution)/shard_map/ppermute | solution.py:569
  71.1 1.1 %collective-permute-done.16.refs_2_ = bf16[320,256]{1,0:T(8,128)(2,1)S(1)} collective-permute-done((bf16[320,256]{1,0:T(8,128)(2,1)S(1)}, bf16[320,256]{1,0:T(8,128)(2,1)S(1)}, u32[]{:S(2)}, u32[]{:S(2)}) %collective-permute-start.16) | collective-permute-done | bytes 163872 | tf_op jit(solution)/shard_map/ppermute | solution.py:569
  72.2 6.6 %collective-permute-done.19 = bf16[320,256]{1,0:T(8,128)(2,1)S(1)} collective-permute-done((bf16[320,256]{1,0:T(8,128)(2,1)S(1)}, bf16[320,256]{1,0:T(8,128)(2,1)S(1)}, u32[]{:S(2)}, u32[]{:S(2)}) %collective-permute-start.19) | collective-permute-done | bytes 163872 | tf_op jit(solution)/shard_map/ppermute | solution.py:569
  78.8 2.0 %shard_map.179 = (f32[1088,128]{1,0:T(8,128)S(1)}, f32[8,128]{1,0:T(8,128)S(1)}) custom-call(f32[2312,128]{1,0:T(8,128)S(1)} %copy-done.13, f32[2,50,8,128]{3,2,1,0:T(8,128)S(1)} %copy-done.16, bf16[320,256]{1,0:T(8,128)(2,1)S(1)} %collective-permute-done.16.refs_2_, bf16[2,3,128,128]{3,2,1,0:T(8,128)(2,1)S(1)} %collective-permute-done.17.refs_3_), custom_call_target="tpu_custom_call" | custom-call | flops 2100000000 | bytes 1048576 | tf_op jit(solution)/shard_map/pallas_call | solution.py:35
  80.9 0.8 collective-permute-start.21
  81.7 0.1 collective-permute-start.18
  81.8 1.8 %collective-permute-done.18.refs_2_ = bf16[2,3,128,128]{3,2,1,0:T(8,128)(2,1)S(1)} collective-permute-done((bf16[2,3,128,128]{3,2,1,0:T(8,128)(2,1)S(1)}, bf16[2,3,128,128]{3,2,1,0:T(8,128)(2,1)S(1)}, u32[]{:S(2)}, u32[]{:S(2)}) %collective-permute-start.18) | collective-permute-done | bytes 196640 | tf_op jit(solution)/shard_map/ppermute | solution.py:569
  83.6 1.7 %shard_map.180 = bf16[8,128,256]{2,1,0:T(8,128)(2,1)} custom-call(f32[1088,128]{1,0:T(8,128)S(1)} %get-tuple-element.66.refs_0_, f32[1088,128]{1,0:T(8,128)S(1)} %get-tuple-element.69.refs_1_, bf16[2,3,128,128]{3,2,1,0:T(8,128)(2,1)S(1)} %collective-permute-done.18.refs_2_, bf16[2,3,128,128]{3,2,1,0:T(8,128)(2,1)S(1)} %collective-permute-done.17.refs_3_, ...), custom_call_target="tpu_custom_call" | custom-call | flops 2000000000 | bytes 1048576 | tf_op jit(solution)/shard_map/pallas_call | solution.py:35
  85.3 1.6 %shard_map.181 = (f32[256,1024]{1,0:T(8,128)}, f32[1024,256]{1,0:T(8,128)}, f32[7,7,256]{2,1,0:T(8,128)}, f32[1,1024]{1,0:T(1,128)}, f32[5,256]{1,0:T(8,128)}) custom-call(bf16[1024,256]{1,0:T(8,128)(2,1)S(1)} %get-tuple-element.96.refs_0_, bf16[1024,256]{1,0:T(8,128)(2,1)S(1)} %slice.155.refs_1_, f32[64,256]{1,0:T(8,128)S(1)} %convert_add_fusion.1.refs_2_), custom_call_target="tpu_custom_call" | custom-call | flops 2000000000 | bytes 1048576 | tf_op jit(solution)/shard_map/pallas_call | solution.py:35
  (79 shorter events, 0.7 us)
Async XLA Ops:
  0.6 1.0 %copy-start = (bf16[1,8,128,256]{3,2,1,0:T(8,128)(2,1)S(1)}, bf16[1,8,128,256]{3,2,1,0:T(8,128)(2,1)}, u32[]{:S(2)}) copy-start(bf16[1,8,128,256]{3,2,1,0:T(8,128)(2,1)} %param.12) | copy-start | bytes 1572868
  1.7 1.2 %copy-start.17 = (s32[4,2,3]{0,1,2:T(2,128)S(1)}, s32[4,2,3]{0,1,2:T(2,128)}, u32[]{:S(2)}) copy-start(s32[4,2,3]{0,1,2:T(2,128)} %param.14) | copy-start | bytes 292
  1.7 1.6 %collective-permute-start = (bf16[3,128,256]{2,1,0:T(8,128)(2,1)S(1)}, bf16[3,128,256]{2,1,0:T(8,128)(2,1)S(1)}, u32[]{:S(2)}, u32[]{:S(2)}) collective-permute-start(bf16[3,128,256]{2,1,0:T(8,128)(2,1)S(1)} %get-tuple-element.42), channel_id=1, source_target_pairs={{0,1},{1,0},{2,3},{3,2},{4,5},{5,4},{6,7},{7,6},{8,9},{9,8},{10,11... | collective-permute-start | bytes 589832 | tf_op jit(solution)/shard_map/ppermute | solution.py:569
  2.2 1.1 %collective-permute-start.1 = (bf16[3,128,256]{2,1,0:T(8,128)(2,1)S(1)}, bf16[3,128,256]{2,1,0:T(8,128)(2,1)S(1)}, u32[]{:S(2)}, u32[]{:S(2)}) collective-permute-start(bf16[3,128,256]{2,1,0:T(8,128)(2,1)S(1)} %get-tuple-element.43), channel_id=1, source_target_pairs={{1,2},{3,4},{5,6},{2,1},{4,3},{6,5},{9,10},{11,12},{13,14},{10,9},... | collective-permute-start | bytes 589832 | tf_op jit(solution)/shard_map/ppermute | solution.py:552
  3.3 8.2 %copy-start.1 = (bf16[1,8,128,256]{3,2,1,0:T(8,128)(2,1)S(1)}, bf16[1,8,128,256]{3,2,1,0:T(8,128)(2,1)}, u32[]{:S(2)}) copy-start(bf16[1,8,128,256]{3,2,1,0:T(8,128)(2,1)} %param.12) | copy-start | bytes 1572868
  3.3 8.2 %copy-start.5 = (bf16[7,7,256]{2,1,0:T(8,128)(2,1)S(1)}, bf16[7,7,256]{2,1,0:T(8,128)(2,1)}, u32[]{:S(2)}) copy-start(bf16[7,7,256]{2,1,0:T(8,128)(2,1)} %refs_1_.1) | copy-start | bytes 75268
  3.3 8.2 %copy-start.7 = (f32[256]{0:T(256)S(1)}, f32[256]{0:T(256)}, u32[]{:S(2)}) copy-start(f32[256]{0:T(256)} %param.16) | copy-start | bytes 3076
  4.0 11.7 %collective-permute-start.2 = (bf16[48,256]{1,0:T(8,128)(2,1)S(1)}, bf16[48,256]{1,0:T(8,128)(2,1)S(1)}, u32[]{:S(2)}, u32[]{:S(2)}) collective-permute-start(bf16[48,256]{1,0:T(8,128)(2,1)S(1)} %get-tuple-element.45.refs_3_), channel_id=1, source_target_pairs={{0,8},{1,9},{2,10},{3,11},{4,12},{5,13},{6,14},{7,15},{8,0},{9,1},... | collective-permute-start | bytes 73736 | tf_op jit(solution)/shard_map/ppermute | solution.py:533
  6.9 8.8 %collective-permute-start.3 = (bf16[48,256]{1,0:T(8,128)(2,1)S(1)}, bf16[48,256]{1,0:T(8,128)(2,1)S(1)}, u32[]{:S(2)}, u32[]{:S(2)}) collective-permute-start(bf16[48,256]{1,0:T(8,128)(2,1)S(1)} %get-tuple-element.46), channel_id=1, source_target_pairs={{0,15},{1,14},{2,13},{3,12},{4,11},{5,10},{6,9},{7,8},{8,7},{9,6},... | collective-permute-start | bytes 73736 | tf_op jit(solution)/shard_map/ppermute | solution.py:533
  10.0 5.8 %collective-permute-start.4 = (bf16[48,256]{1,0:T(8,128)(2,1)S(1)}, bf16[48,256]{1,0:T(8,128)(2,1)S(1)}, u32[]{:S(2)}, u32[]{:S(2)}) collective-permute-start(bf16[48,256]{1,0:T(8,128)(2,1)S(1)} %get-tuple-element.47), channel_id=1, source_target_pairs={{0,16},{1,17},{2,18},{3,19},{4,20},{5,21},{6,22},{7,23},{8,24},{9,... | collective-permute-start | bytes 73736 | tf_op jit(solution)/shard_map/ppermute | solution.py:533
  11.5 5.9 %collective-permute-start.5 = (bf16[48,256]{1,0:T(8,128)(2,1)S(1)}, bf16[48,256]{1,0:T(8,128)(2,1)S(1)}, u32[]{:S(2)}, u32[]{:S(2)}) collective-permute-start(bf16[48,256]{1,0:T(8,128)(2,1)S(1)} %get-tuple-element.48), channel_id=1, source_target_pairs={{0,23},{1,22},{2,21},{3,20},{4,19},{5,18},{6,17},{7,16},{8,31},{9,... | collective-permute-start | bytes 73736 | tf_op jit(solution)/shard_map/ppermute | solution.py:533
  11.5 5.9 %copy-start.2 = (bf16[256,1024]{1,0:T(8,128)(2,1)S(1)}, bf16[256,1024]{1,0:T(8,128)(2,1)}, u32[]{:S(2)}) copy-start(bf16[256,1024]{1,0:T(8,128)(2,1)} %refs_14_.1) | copy-start | bytes 1572868
  11.5 5.9 %copy-start.3 = (bf16[1024,256]{1,0:T(8,128)(2,1)S(1)}, bf16[1024,256]{1,0:T(8,128)(2,1)}, u32[]{:S(2)}) copy-start(bf16[1024,256]{1,0:T(8,128)(2,1)} %refs_15_.1) | copy-start | bytes 1572868
  11.5 5.9 %copy-start.4 = (bf16[1,8,128,256]{3,2,1,0:T(8,128)(2,1)S(1)}, bf16[1,8,128,256]{3,2,1,0:T(8,128)(2,1)}, u32[]{:S(2)}) copy-start(bf16[1,8,128,256]{3,2,1,0:T(8,128)(2,1)} %param.13) | copy-start | bytes 1572868
  11.6 5.9 %copy-start.6 = (f32[1024]{0:T(1024)S(1)}, f32[1024]{0:T(1024)}, u32[]{:S(2)}) copy-start(f32[1024]{0:T(1024)} %param.20) | copy-start | bytes 12292
  11.6 5.9 %copy-start.8 = (f32[256]{0:T(256)S(1)}, f32[256]{0:T(256)}, u32[]{:S(2)}) copy-start(f32[256]{0:T(256)} %param.17) | copy-start | bytes 3076
  11.6 5.9 %copy-start.9 = (f32[256]{0:T(256)S(1)}, f32[256]{0:T(256)}, u32[]{:S(2)}) copy-start(f32[256]{0:T(256)} %param.18) | copy-start | bytes 3076
  11.6 5.9 %copy-start.10 = (f32[256]{0:T(256)S(1)}, f32[256]{0:T(256)}, u32[]{:S(2)}) copy-start(f32[256]{0:T(256)} %param.22) | copy-start | bytes 3076
  11.6 5.9 %copy-start.11 = (f32[256]{0:T(256)S(1)}, f32[256]{0:T(256)}, u32[]{:S(2)}) copy-start(f32[256]{0:T(256)} %param.23) | copy-start | bytes 3076
  15.7 12.2 %copy-start.15 = (f32[2,50,8,128]{3,2,1,0:T(8,128)}, f32[2,50,8,128]{3,2,1,0:T(8,128)S(1)}, u32[]{:S(2)}) copy-start(f32[2,50,8,128]{3,2,1,0:T(8,128)S(1)} %get-tuple-element.49.refs_8_.refs_1_) | copy-start | bytes 1228804
  27.9 7.7 %collective-permute-start.6 = (bf16[1120,256]{1,0:T(8,128)(2,1)S(1)}, bf16[1120,256]{1,0:T(8,128)(2,1)}, u32[]{:S(2)}, u32[]{:S(2)}) collective-permute-start(bf16[1120,256]{1,0:T(8,128)(2,1)S(1)} %get-tuple-element.55), channel_id=1, source_target_pairs={{0,1},{1,0},{2,3},{3,2},{4,5},{5,4},{6,7},{7,6},{8,9},{9,8},{10,11... | collective-permute-start | bytes 1720328 | tf_op jit(solution)/shard_map/ppermute | solution.py:569
  35.6 5.9 %copy-start.14 = (f32[4256,128]{1,0:T(8,128)S(1)}, f32[4256,128]{1,0:T(8,128)}, u32[]{:S(2)}) copy-start(f32[4256,128]{1,0:T(8,128)} %get-tuple-element.58.refs_1_) | copy-start | bytes 6537220
  36.9 4.6 %copy-start.12 = (f32[2312,128]{1,0:T(8,128)S(1)}, f32[2312,128]{1,0:T(8,128)}, u32[]{:S(2)}) copy-start(f32[2312,128]{1,0:T(8,128)} %get-tuple-element.52.refs_0_) | copy-start | bytes 3551236
  37.9 11.0 %collective-permute-start.8 = (bf16[352,256]{1,0:T(8,128)(2,1)S(1)}, bf16[352,256]{1,0:T(8,128)(2,1)S(1)}, u32[]{:S(2)}, u32[]{:S(2)}) collective-permute-start(bf16[352,256]{1,0:T(8,128)(2,1)S(1)} %pad_maximum_fusion.1), channel_id=1, source_target_pairs={{0,16},{8,24},{16,0},{24,8},{1,17},{9,25},{17,1},{25,9},{2,18},{10... | collective-permute-start | bytes 540680 | tf_op jit(solution)/shard_map/ppermute | solution.py:569
  38.5 10.4 %collective-permute-start.7 = (bf16[352,256]{1,0:T(8,128)(2,1)S(1)}, bf16[352,256]{1,0:T(8,128)(2,1)S(1)}, u32[]{:S(2)}, u32[]{:S(2)}) collective-permute-start(bf16[352,256]{1,0:T(8,128)(2,1)S(1)} %pad_maximum_fusion), channel_id=1, source_target_pairs={{0,8},{8,0},{16,24},{24,16},{1,9},{9,1},{17,25},{25,17},{2,10},{10... | collective-permute-start | bytes 540680 | tf_op jit(solution)/shard_map/ppermute | solution.py:569
  40.0 8.8 %collective-permute-start.9 = (bf16[256,256]{1,0:T(8,128)(2,1)S(1)}, bf16[256,256]{1,0:T(8,128)(2,1)S(1)}, u32[]{:S(2)}, u32[]{:S(2)}) collective-permute-start(bf16[256,256]{1,0:T(8,128)(2,1)S(1)} %get-tuple-element.85), channel_id=1, source_target_pairs={{0,24},{8,16},{16,8},{24,0},{1,25},{9,17},{17,9},{25,1},{2,26},{10... | collective-permute-start | bytes 393224 | tf_op jit(solution)/shard_map/ppermute | solution.py:569
  49.0 4.9 %collective-permute-start.11 = (bf16[64,256]{1,0:T(8,128)(2,1)S(1)}, bf16[64,256]{1,0:T(8,128)(2,1)S(1)}, u32[]{:S(2)}, u32[]{:S(2)}) collective-permute-start(bf16[64,256]{1,0:T(8,128)(2,1)S(1)} %get-tuple-element.89), channel_id=1, source_target_pairs={{0,2},{1,3},{2,0},{3,1},{4,6},{5,7},{6,4},{7,5},{8,10},{9,11},{10,... | collective-permute-start | bytes 98312 | tf_op jit(solution)/shard_map/ppermute | solution.py:569
  49.1 8.0 %collective-permute-start.10 = (bf16[160,256]{1,0:T(8,128)(2,1)S(1)}, bf16[160,256]{1,0:T(8,128)(2,1)S(1)}, u32[]{:S(2)}, u32[]{:S(2)}) collective-permute-start(bf16[160,256]{1,0:T(8,128)(2,1)S(1)} %pad_maximum_fusion.2), channel_id=1, source_target_pairs={{0,6},{1,7},{2,4},{3,5},{4,2},{5,3},{6,0},{7,1},{8,14},{9,15},{10,... | collective-permute-start | bytes 245768 | tf_op jit(solution)/shard_map/ppermute | solution.py:569
  51.0 6.1 %collective-permute-start.12 = (bf16[64,256]{1,0:T(8,128)(2,1)S(1)}, bf16[64,256]{1,0:T(8,128)(2,1)S(1)}, u32[]{:S(2)}, u32[]{:S(2)}) collective-permute-start(bf16[64,256]{1,0:T(8,128)(2,1)S(1)} %get-tuple-element.88), channel_id=1, source_target_pairs={{0,4},{1,5},{2,6},{3,7},{4,0},{5,1},{6,2},{7,3},{8,12},{9,13},{10,... | collective-permute-start | bytes 98312 | tf_op jit(solution)/shard_map/ppermute | solution.py:569
  57.9 5.2 %collective-permute-start.13 = (bf16[128,256]{1,0:T(8,128)(2,1)S(1)}, bf16[128,256]{1,0:T(8,128)(2,1)S(1)}, u32[]{:S(2)}, u32[]{:S(2)}) collective-permute-start(bf16[128,256]{1,0:T(8,128)(2,1)S(1)} %concatenate.38), channel_id=1, source_target_pairs={{0,2},{1,3},{2,0},{3,1},{4,6},{5,7},{6,4},{7,5},{8,10},{9,11},{10,... | collective-permute-start | bytes 196616 | tf_op jit(solution)/shard_map/ppermute | solution.py:569
  58.1 6.6 %collective-permute-start.14 = (bf16[128,256]{1,0:T(8,128)(2,1)S(1)}, bf16[128,256]{1,0:T(8,128)(2,1)S(1)}, u32[]{:S(2)}, u32[]{:S(2)}) collective-permute-start(bf16[128,256]{1,0:T(8,128)(2,1)S(1)} %concatenate.38), channel_id=1, source_target_pairs={{0,4},{1,5},{2,6},{3,7},{4,0},{5,1},{6,2},{7,3},{8,12},{9,13},{10,... | collective-permute-start | bytes 196616 | tf_op jit(solution)/shard_map/ppermute | solution.py:569
  60.2 6.5 %collective-permute-start.15 = (bf16[128,256]{1,0:T(8,128)(2,1)S(1)}, bf16[128,256]{1,0:T(8,128)(2,1)S(1)}, u32[]{:S(2)}, u32[]{:S(2)}) collective-permute-start(bf16[128,256]{1,0:T(8,128)(2,1)S(1)} %concatenate.38), channel_id=1, source_target_pairs={{0,6},{1,7},{2,4},{3,5},{4,2},{5,3},{6,0},{7,1},{8,14},{9,15},{10,... | collective-permute-start | bytes 196616 | tf_op jit(solution)/shard_map/ppermute | solution.py:569
  62.3 1.1 %copy-start.18 = (bf16[1088,256]{1,0:T(8,128)(2,1)S(1)}, bf16[1088,256]{1,0:T(8,128)(2,1)}, u32[]{:S(2)}) copy-start(bf16[1088,256]{1,0:T(8,128)(2,1)} %get-tuple-element.79) | copy-start | bytes 1671172
  62.3 2.4 %copy-start.13 = (f32[2312,128]{1,0:T(8,128)S(1)}, f32[2312,128]{1,0:T(8,128)}, u32[]{:S(2)}) copy-start(f32[2312,128]{1,0:T(8,128)} %get-tuple-element.52.refs_0_) | copy-start | bytes 3551236
  62.3 2.4 %copy-start.16 = (f32[2,50,8,128]{3,2,1,0:T(8,128)S(1)}, f32[2,50,8,128]{3,2,1,0:T(8,128)}, u32[]{:S(2)}) copy-start(f32[2,50,8,128]{3,2,1,0:T(8,128)} %copy-done.15) | copy-start | bytes 1228804
  66.8 5.4 %collective-permute-start.16 = (bf16[320,256]{1,0:T(8,128)(2,1)S(1)}, bf16[320,256]{1,0:T(8,128)(2,1)S(1)}, u32[]{:S(2)}, u32[]{:S(2)}) collective-permute-start(bf16[320,256]{1,0:T(8,128)(2,1)S(1)} %get-tuple-element.105), channel_id=1, source_target_pairs={{0,8},{8,0},{16,24},{24,16},{1,9},{9,1},{17,25},{25,17},{2,10},{10... | collective-permute-start | bytes 491528 | tf_op jit(solution)/shard_map/ppermute | solution.py:569
  68.4 10.5 %collective-permute-start.17 = (bf16[2,3,128,128]{3,2,1,0:T(8,128)(2,1)S(1)}, bf16[2,3,128,128]{3,2,1,0:T(8,128)(2,1)S(1)}, u32[]{:S(2)}, u32[]{:S(2)}) collective-permute-start(bf16[2,3,128,128]{3,2,1,0:T(8,128)(2,1)S(1)} %get-tuple-element.68), channel_id=1, source_target_pairs={{1,2},{3,4},{5,6},{2,1},{4,3},{6,5},{9,10},{11,12},{13,14},{10,9},... | collective-permute-start | bytes 589832 | tf_op jit(solution)/shard_map/ppermute | solution.py:552
  69.0 9.8 %collective-permute-start.19 = (bf16[320,256]{1,0:T(8,128)(2,1)S(1)}, bf16[320,256]{1,0:T(8,128)(2,1)S(1)}, u32[]{:S(2)}, u32[]{:S(2)}) collective-permute-start(bf16[320,256]{1,0:T(8,128)(2,1)S(1)} %get-tuple-element.105), channel_id=1, source_target_pairs={{0,16},{8,24},{16,0},{24,8},{1,17},{9,25},{17,1},{25,9},{2,18},{10... | collective-permute-start | bytes 491528 | tf_op jit(solution)/shard_map/ppermute | solution.py:569
  70.2 10.7 %collective-permute-start.20 = (bf16[320,256]{1,0:T(8,128)(2,1)S(1)}, bf16[320,256]{1,0:T(8,128)(2,1)S(1)}, u32[]{:S(2)}, u32[]{:S(2)}) collective-permute-start(bf16[320,256]{1,0:T(8,128)(2,1)S(1)} %get-tuple-element.105), channel_id=1, source_target_pairs={{0,24},{8,16},{16,8},{24,0},{1,25},{9,17},{17,9},{25,1},{2,26},{10... | collective-permute-start | bytes 491528 | tf_op jit(solution)/shard_map/ppermute | solution.py:569
  80.9 4.4 %collective-permute-start.21 = (bf16[1088,256]{1,0:T(8,128)(2,1)S(1)}, bf16[1088,256]{1,0:T(8,128)(2,1)S(1)}, u32[]{:S(2)}, u32[]{:S(2)}) collective-permute-start(bf16[1088,256]{1,0:T(8,128)(2,1)S(1)} %get-tuple-element.77), channel_id=1, source_target_pairs={{0,1},{1,0},{2,3},{3,2},{4,5},{5,4},{6,7},{7,6},{8,9},{9,8},{10,11... | collective-permute-start | bytes 1671176 | tf_op jit(solution)/shard_map/ppermute | solution.py:569
  81.7 1.9 %collective-permute-start.18 = (bf16[2,3,128,128]{3,2,1,0:T(8,128)(2,1)S(1)}, bf16[2,3,128,128]{3,2,1,0:T(8,128)(2,1)S(1)}, u32[]{:S(2)}, u32[]{:S(2)}) collective-permute-start(bf16[2,3,128,128]{3,2,1,0:T(8,128)(2,1)S(1)} %get-tuple-element.70), channel_id=1, source_target_pairs={{0,1},{1,0},{2,3},{3,2},{4,5},{5,4},{6,7},{7,6},{8,9},{9,8},{10,11... | collective-permute-start | bytes 589832 | tf_op jit(solution)/shard_map/ppermute | solution.py:569

commit v3 on v2

--- a/solution.py
+++ b/solution.py
@@ -51,13 +51,19 @@
     return ref[pl.ds(start, SUB, stride=groups), :]
 
 
-def gluing(match):
+def gluing(match, flags):
     face = lax.axis_index("face")
     near = jnp.where(match[face, 0, 0] == face ^ 1, 0, 1)
-    return near, match[face, near, 2], match[face, 1 - near, 2]
-
-
-def pack_columns(tile, count, near, held, outs):
+    flags[...] = jnp.zeros_like(flags)
+    for k, value in enumerate((near, match[face, near, 2], match[face, 1 - near, 2])):
+        flags[k : k + 1, :] = jnp.full((1, LANES), value, jnp.int32).astype(F32)
+
+
+def glued(flags):
+    return flags[0:1, :] == 0.0, flags[1:2, :] == 1.0, flags[2:3, :] == 1.0
+
+
+def pack_columns(tile, count, first, held, outs):
     vals = {}
     for side in range(2):
         for h in range(2):
@@ -69,7 +75,6 @@
             for v in range(2):
                 for d in range(3):
                     vals[side, h, v, d] = held[v, pl.ds(tile.column(side, d), 16, stride=SUB), :]
-    first = near == 0
     for h in range(2):
         lane = slice(h * LANES, (h + 1) * LANES)
         for v in range(2):
@@ -80,14 +85,12 @@
                 outs[2 + v][at, lane] = jnp.where(first, east, west).astype(BF16)
 
 
-def unpack_columns(near, turn_near, turn_far, got):
-    first = near == 0
-
+def unpack_columns(first, turn_near, turn_far, got):
     def value(side, h, d):
         lane = slice(h * LANES, (h + 1) * LANES)
         parts = [g[d * 16 : d * 16 + 16, lane].astype(F32) for g in got]
-        one = jnp.where(turn_near == 1, parts[1], parts[0])
-        two = jnp.where(turn_far == 1, parts[3], parts[2])
+        one = jnp.where(turn_near, parts[1], parts[0])
+        two = jnp.where(turn_far, parts[3], parts[2])
         return jnp.where(first, one, two) if side == 0 else jnp.where(first, two, one)
 
     return value
@@ -106,11 +109,12 @@
 
 
 def edges_kernel(columns, within, across, match, *refs):
-    outs, held = refs[:4], refs[4]
+    outs, flags, held = refs[:4], refs[4], refs[5]
+    gluing(match, flags)
     up, down = above_below(within, across)
     rows, _, _ = columns.shape
     _, cols, _ = within.shape
-    near, _, _ = gluing(match)
+    first, _, _ = glued(flags)
 
     def tile(side, h, i):
         lane = slice(h * LANES, (h + 1) * LANES)
@@ -124,7 +128,7 @@
         return v.astype(F32)[0:SUB] if side == 0 else v.astype(F32)[SUB:16]
 
     tile.column = lambda side, d: d if side == 0 else SUB - 1 - d
-    pack_columns(tile, rows + 6, near, held, outs)
+    pack_columns(tile, rows + 6, first, held, outs)
 
 
 def fill_pad(pad, halves, ext, wide, cols, source, which):
@@ -175,9 +179,9 @@
 
 
 def forward_kernel(
-    band, within, across, got0, got1, got2, got3, cot, taps, gain, shift, bias2, scale, bias1, w1, w2, part, match,
-    result_out, pad_out, grad_out, mine, other, plain_near, plain_far, rim, vecs, bias_out,
-    result, pad, grad, conv, normed, act, pre, gbr, tmp, strip, sems,
+    band, within, across, got0, got1, got2, got3, cot, taps, gain, shift, bias2, scale, bias1, w1, w2, part, flags,
+    result_out, pad_out, grad_out, mine, other, plain_near, plain_far, rim_out, vecs, bias_out,
+    rim, result, pad, grad, conv, normed, act, pre, gbr, tmp, strip, sems,
 ):
     rows, cols, channels = band.shape
     halves = channels // LANES
@@ -188,8 +192,8 @@
     cpitch = groups * SUB
     hidden = w1.shape[1]
 
-    near, turn_near, turn_far = gluing(match)
-    arrived = unpack_columns(near, turn_near, turn_far, (got0, got1, got2, got3))
+    first, turn_near, turn_far = glued(flags)
+    arrived = unpack_columns(first, turn_near, turn_far, (got0, got1, got2, got3))
 
     up, down = above_below(within, across)
 
@@ -327,14 +331,6 @@
     keep_result = pltpu.make_async_copy(result, result_out, sems.at[2])
     keep_result.start()
 
-    even = (lax.axis_index("tile") & 1) == 0
-    for n in range(tiles):
-        hid = slice(n * 256, (n + 1) * 256)
-        g_expand = dot(normed[...], pre[:, hid], ((0,), (0,)))
-        g_reduce = dot(act[:, hid], gbr[...], ((0,), (0,)))
-        mine[hid, :] = jnp.where(even, g_expand, g_reduce)
-        other[hid, :] = jnp.where(even, g_reduce, g_expand).astype(BF16)
-
     def rim_half(h, carry):
         for k in range(6):
             acc = spread_row(grad, taps, h, k if k < 3 else rows + k, rows, pitch, groups)
@@ -343,7 +339,8 @@
         return carry
 
     lax.fori_loop(0, halves, rim_half, 0)
-    first = near == 0
+    keep_rim = pltpu.make_async_copy(rim, rim_out, sems.at[3])
+    keep_rim.start()
     strip[...] = jnp.zeros_like(strip)
     for h in range(halves):
         lane = slice(h * LANES, (h + 1) * LANES)
@@ -377,9 +374,18 @@
                 else:
                     plain_near[16 * d : 16 * d + 16, lane] = one
                     plain_far[16 * d : 16 * d + 16, lane] = two
+
+    even = (lax.axis_index("tile") & 1) == 0
+    for n in range(tiles):
+        hid = slice(n * 256, (n + 1) * 256)
+        g_expand = dot(normed[...], pre[:, hid], ((0,), (0,)))
+        g_reduce = dot(act[:, hid], gbr[...], ((0,), (0,)))
+        mine[hid, :] = jnp.where(even, g_expand, g_reduce)
+        other[hid, :] = jnp.where(even, g_reduce, g_expand).astype(BF16)
     keep_pad.wait()
     keep_grad.wait()
     keep_result.wait()
+    keep_rim.wait()
 
 
 def spread_row(grad, taps, h, o, rows, pitch, groups):
@@ -447,13 +453,13 @@
     some(6, 1)
 
 
-def rims_kernel(rim, got0, got1, got2, got3, match, within, across, token, total, held):
+def rims_kernel(rim, got0, got1, got2, got3, flags, within, across, token, total, held):
     token[...] = jnp.zeros_like(token)
     halves, _, cols, _ = within.shape
     even = (lax.axis_index("tile") & 1) == 0
     cpitch = rim.shape[0] // (halves * 6)
-    near, turn_near, turn_far = gluing(match)
-    arrived = unpack_columns(near, turn_near, turn_far, (got0, got1, got2, got3))
+    first, turn_near, turn_far = glued(flags)
+    arrived = unpack_columns(first, turn_near, turn_far, (got0, got1, got2, got3))
     for h in range(halves):
         for k in range(6):
             total[k * cols : (k + 1) * cols, :] = rim[
@@ -473,13 +479,14 @@
             across[h, k] = jnp.where(even, top, bottom)
 
 
-def fields_kernel(inner0, inner1, within, across, got0, got1, got2, got3, cot, match, out, total, held):
+def fields_kernel(inner0, inner1, within, across, got0, got1, got2, got3, cot, flags, out, token, total, held):
+    token[...] = jnp.zeros_like(token)
     rows, cols, channels = cot.shape
     halves = channels // LANES
     cpitch = inner0.shape[0] // rows
     from_up, from_down = above_below(within, across)
-    near, turn_near, turn_far = gluing(match)
-    arrived = unpack_columns(near, turn_near, turn_far, (got0, got1, got2, got3))
+    first, turn_near, turn_far = glued(flags)
+    arrived = unpack_columns(first, turn_near, turn_far, (got0, got1, got2, got3))
     for h in range(halves):
         lane = slice(h * LANES, (h + 1) * LANES)
         for r in range(rows):
@@ -499,15 +506,89 @@
             out[r, :, lane] = total[r * cols : (r + 1) * cols, :].astype(BF16)
 
 
-def finish_kernel(factor, faces, chips, mine, peer, small, expand, reduce, g_taps, g_bias, vecs):
+def merge_kernel(masks, half, mine, peer, plain_near, plain_far, flags, own, token, *messages):
+    _, turn_near, turn_far = glued(flags)
+    token[...] = jnp.zeros_like(token)
+    hidden = mine.shape[0]
+    count = own.shape[0]
+    face = lax.axis_index("face")
+
+    def share(mask):
+        at = pl.ds(pl.multiple_of((face ^ mask) * count, count), count)
+        return mine[at, :] + peer[at, :].astype(F32)
+
+    def choose(turn, at, plain, message):
+        for h in range(2):
+            lane = slice(h * LANES, (h + 1) * LANES)
+            turned = peer[at : at + 48, lane].astype(F32)
+            message[count : count + 48, lane] = jnp.where(
+                turn, turned, plain[:, lane].astype(F32)
+            ).astype(BF16)
+
+    own[...] = share(0)
+    for mask, message in zip(masks, messages):
+        message[0:count, :] = share(mask).astype(BF16)
+        if mask == 1:
+            choose(turn_near, hidden, plain_near, message)
+        if mask == half:
+            choose(turn_far, hidden + 48, plain_far, message)
+
+
+def deal_kernel(masks, mirror, near, far, own, *refs):
+    count = own.shape[0]
+    got, (part, token, *messages), total = refs[: len(refs) - 3 - len(masks)], refs[
+        len(refs) - 3 - len(masks) : -1
+    ], refs[-1]
+    token[...] = jnp.zeros_like(token)
+    size = part.shape[0]
+    chip = lax.axis_index("tile") >> 1
+    total[...] = tree_sum([own[...]] + [g[0:count, :] for g in got])
+
+    def share(place):
+        return total[pl.ds(pl.multiple_of(place * size, size), size), :]
+
+    part[...] = share(chip)
+    for mask, message in zip(masks, messages):
+        at = 0
+        if mask == mirror:
+            message[0:48, :] = got[near][count:, :]
+            message[48:96, :] = got[far][count:, :]
+            at = 96
+        message[at : at + size, :] = share(chip ^ (mask >> 1)).astype(BF16)
+
+
+def pack_shares_kernel(own, *refs):
+    *got, taps0, taps1, bias, vecs, out, held = refs
+    count, channels = own.shape
+    held[...] = jnp.zeros_like(held)
+    held[0:49, 0:LANES] = taps0[0:49, :]
+    held[0:49, LANES : 2 * LANES] = taps1[0:49, :]
+    parts = bias.shape[1] // channels
+    for n in range(parts):
+        held[49 + n : 50 + n, :] = bias[:, n * channels : (n + 1) * channels]
+    held[49 + parts : 54 + parts, :] = vecs[0:5, :]
+    out[0:SMALL, :] = held[...].astype(BF16)
+    out[SMALL:, :] = tree_sum([own[...]] + [g[0:count, :] for g in got]).astype(BF16)
+
+
+def pack_pieces_kernel(own, *refs):
+    *got, out = refs
+    parts = [own[...].astype(F32)] + [g[...].astype(F32) for g in got]
+    out[0:SMALL, :] = tree_sum([p[0:SMALL] for p in parts]).astype(BF16)
+    out[SMALL:, :] = jnp.concatenate([p[SMALL:] for p in parts], 0).astype(BF16)
+
+
+def finish_kernel(factor, faces, chips, mine, peer, expand, reduce, g_taps, g_bias, vecs):
     hidden, channels = reduce.shape
     count = hidden // (faces * chips)
     face = lax.axis_index("face")
     chip = lax.axis_index("tile") >> 1
     even = (lax.axis_index("tile") & 1) == 0
+    small = mine[0:SMALL, :].astype(F32) + peer[0:SMALL, :].astype(F32)
+    small = small * factor
     for f in range(faces):
         for z in range(chips):
-            at = (f * chips + z) * count
+            at = SMALL + (f * chips + z) * count
             own = mine[at : at + count, :].astype(F32) * factor
             got = peer[at : at + count, :].astype(F32) * factor
             to = ((face ^ f) * chips + (chip ^ z)) * count
@@ -516,11 +597,11 @@
             col = pl.multiple_of((to // channels) * channels, channels)
             expand[pl.ds(row, count), pl.ds(col, channels)] = jnp.where(even, own, got)
     for a in range(7):
-        g_taps[a] = small[a * 7 : a * 7 + 7, :] * factor
+        g_taps[a] = small[a * 7 : a * 7 + 7, :]
     for n in range(hidden // channels):
-        g_bias[:, n * channels : (n + 1) * channels] = small[49 + n : 50 + n, :] * factor
+        g_bias[:, n * channels : (n + 1) * channels] = small[49 + n : 50 + n, :]
     first = 49 + hidden // channels
-    vecs[...] = small[first : first + 5, :] * factor
+    vecs[...] = small[first : first + 5, :]
 
 
 def face_swap(x, mask, turned=False):
@@ -576,37 +657,9 @@
     return parts[0]
 
 
-def joined(x, riders):
-    return jnp.concatenate([x] + list(riders), 0) if riders else x
-
-
-def scatter_start(x, axis, masks, index, riders):
-    shares = x.reshape((len(masks) + 1, x.shape[0] // (len(masks) + 1)) + x.shape[1:])
-    step = masks[0]
-    cut = shares.shape[1]
-    own = lax.dynamic_index_in_dim(shares, index, 0, keepdims=False)
-    sent = [
-        lax.dynamic_index_in_dim(shares, index ^ (m // step), 0, keepdims=False).astype(BF16)
-        for m in masks
-    ]
-    got = [swapped(joined(v, riders.get(m)), axis, m) for v, m in zip(sent, masks)]
-    return [own] + [g[:cut] for g in got], {m: got[masks.index(m)][cut:] for m in riders}
-
-
-def gather_start(x, small, axis, masks):
-    sent = jnp.concatenate([x, small.astype(BF16)], 0)
-    return [swapped(sent, axis, m) for m in masks]
-
-
-def gather_done(x, small, got):
-    cut = x.shape[0]
-    pieces = jnp.concatenate([x] + [g[:cut] for g in got], 0)
-    return pieces, tree_sum([small.astype(BF16)] + [g[cut:] for g in got])
-
-
-def ordered(x, token):
-    blocks = x.reshape(x.shape[0] // SUB, SUB, x.shape[1] // LANES, LANES)
-    return (blocks + token[None, :, None, :]).reshape(x.shape)
+def gathered(x, axis, masks):
+    got = [swapped(x, axis, m) for m in masks]
+    return [x] + [got[masks.index(m)] for m in sorted(masks)]
 
 
 def shards(
@@ -635,6 +688,7 @@
     faces, tiles = lax.axis_size("face"), lax.axis_size("tile")
     shape = jax.ShapeDtypeStruct
     strips = [shape((48, channels), BF16)] * 4
+    sign = shape((SUB, LANES), F32)
 
     *rim_rows, columns = call(
         ends_kernel,
@@ -648,9 +702,9 @@
         (band,),
     )
     beside = row_swap(*rim_rows)
-    sides = call(
+    *sides, flags = call(
         edges_kernel,
-        strips,
+        strips + [sign],
         [pltpu.VMEM((2, 16 * SUB, LANES), F32)],
         900_000_000,
         (columns, *beside, edge_match),
@@ -670,7 +724,6 @@
         after=(sides[0],),
     )
     part, taps = kept(part), kept(taps)
-    sign = shape((SUB, LANES), F32)
     result, pad, grad, mine, other, plain_near, plain_far, rim, vecs, bias_out = call(
         forward_kernel,
         [
@@ -681,11 +734,12 @@
             shape((hidden + 96, channels), BF16),
             shape((48, channels), BF16),
             shape((48, channels), BF16),
-            shape((halves * 6 * (cols + SUB), LANES), F32),
+            pltpu.HBM((halves * 6 * (cols + SUB), LANES), F32),
             shape((8, channels), F32),
             shape((1, hidden), F32),
         ],
         [
+            pltpu.VMEM((halves * 6 * (cols + SUB), LANES), F32),
             pltpu.VMEM(band.shape, BF16),
             pltpu.VMEM((halves * ext * wide, LANES), F32),
             pltpu.VMEM((halves * rows * pitch + SUB, LANES), F32),
@@ -696,93 +750,115 @@
             pltpu.VMEM((cells, channels), BF16),
             pltpu.VMEM((2 * cols, channels), F32),
             pltpu.VMEM((12 * 32, LANES), F32),
-            pltpu.SemaphoreType.DMA((3,)),
+            pltpu.SemaphoreType.DMA((4,)),
         ],
         12_000_000_000,
         (
             band, *beside, *got, cot, taps, norm_gain[None], norm_bias[None], reduce_bias[None],
             layer_scale[None], expand_bias.reshape(1, hidden), expand_weight, reduce_weight, part,
-            edge_match,
+            flags,
         ),
-        smem=1,
         limit=20,
-        left=(0, 1, 2),
-    )
-
-    face_masks = list(range(1, faces))
+        left=(0, 1, 2, 7),
+    )
+
+    face_masks = list(range(faces - 1, 0, -1))
     chip_masks = list(range(2, tiles, 2))
     half, mirror = faces // 2, tiles - 2
     peer = swapped(other, "tile", 1)
-    turned_near, turned_far = peer[hidden : hidden + 48], peer[hidden + 48 :]
+    count = hidden // faces
+    own, merged, *messages = call(
+        lambda *refs: merge_kernel(face_masks, half, *refs),
+        [shape((count, channels), F32), sign]
+        + [shape((count + 48 * (m in (1, half)), channels), BF16) for m in face_masks],
+        [],
+        500_000_000,
+        (mine, peer, plain_near, plain_far, flags),
+    )
 
     def half_taps(h, after):
         return call(
             lambda *refs: taps_kernel(h, *refs),
             [shape((56, LANES), F32), sign],
             [],
-            3_500_000_000,
+            3_500_000_000 if h == 0 else 300_000_000,
             (grad, pad),
             after=after,
         )
 
-    riders = {1: [plain_near, turned_near], half: [plain_far, turned_far]}
-    total = (mine + peer[:hidden].astype(F32)).astype(BF16)
-    got, rode = scatter_start(total, "face", face_masks, lax.axis_index("face"), riders)
-    taps0, token = half_taps(0, (turned_near,))
-    share = ordered(tree_sum(got), token)
-    plain_near, turned_near = rode[1][:48], rode[1][48:]
-    plain_far, turned_far = rode[half][:48], rode[half][48:]
-    riders = {mirror: [turned_near, turned_far]}
-    got, rode = scatter_start(share, "tile", chip_masks, lax.axis_index("tile") >> 1, riders)
-    taps1, token = half_taps(1, (got[1],))
-    share = ordered(tree_sum(got), token).astype(BF16)
-    columns = (plain_near, rode[mirror][:48], plain_far, rode[mirror][48:])
-    small = jnp.concatenate(
-        [
-            jnp.concatenate([taps0[:49], taps1[:49]], 1),
-            bias_out.reshape(hidden // channels, channels),
-            vecs[0:5],
-            jnp.zeros((SMALL - 54 - hidden // channels, channels), F32),
-        ],
-        0,
-    )
     def half_inner(h, after):
         return call(
             lambda *refs: inner_kernel(h, *refs),
             [shape((rows * (cols + SUB), LANES), F32), sign],
             [],
-            2_100_000_000,
+            2_100_000_000 if h == 0 else 200_000_000,
             (grad, taps),
             after=after,
         )
 
-    got = gather_start(share, small, "tile", chip_masks)
+    got = [swapped(v, "face", m) for v, m in zip(messages, face_masks)]
+    rode = {m: got[face_masks.index(m)][count:] for m in (1, half)}
+    inner0, token = half_inner(0, (merged,))
+    taps0, token = half_taps(0, (token,))
+    rows_z, rows_f = hidden // (faces * (tiles // 2)), hidden // faces
+    got = got[::-1]
+    part, dealt, *messages = call(
+        lambda *refs: deal_kernel(chip_masks, mirror, 0, half - 1, *refs),
+        [shape((rows_z, channels), F32), sign]
+        + [shape((rows_z + 96 * (m == mirror), channels), BF16) for m in chip_masks],
+        [pltpu.VMEM((rows_f, channels), F32)],
+        100_000_000,
+        (own, *got),
+        after=(token,),
+    )
+    straight = rode
+    got = [swapped(v, "tile", m) for v, m in zip(messages, chip_masks)]
+    strips_got = got[chip_masks.index(mirror)]
+    got = [g[96:] if m == mirror else g for g, m in zip(got, chip_masks)]
+    columns = (straight[1], strips_got[0:48], straight[half], strips_got[48:96])
+    taps1, _ = half_taps(1, (dealt,))
+    (share,) = call(
+        pack_shares_kernel,
+        [shape((SMALL + rows_z, channels), BF16)],
+        [pltpu.VMEM((SMALL, channels), F32)],
+        1_000_000,
+        (part, *got, taps0, taps1, bias_out, vecs),
+    )
+    got = gathered(share, "tile", chip_masks)
     within, across, token = call(
         rims_kernel,
         [shape((halves, 3, cols, LANES), BF16)] * 2 + [sign],
         [pltpu.VMEM((6 * cols, LANES), F32), pltpu.VMEM((16, LANES), F32)],
         900_000_000,
-        (rim, *columns, edge_match),
-        smem=1,
-    )
-    inner0, token = half_inner(0, (token, got[0]))
+        (rim, *columns, flags),
+    )
     arrived = row_swap(within, across)
-    pieces, small = gather_done(share, small, got)
-    small = ordered(small, token)
-    got = gather_start(pieces, small, "face", face_masks)
-    inner1, token = half_inner(1, (got[0], arrived[1]))
-    pieces, small = gather_done(pieces, small, got)
-    small = ordered(small, token).astype(BF16)
-    peer = swapped(jnp.concatenate([pieces, small], 0), "tile", 1)
-    (grad_fields,) = call(
+    (pieces,) = call(
+        pack_pieces_kernel,
+        [shape((SMALL + rows_f, channels), BF16)],
+        [],
+        1_000_000,
+        tuple(got),
+        after=(token,),
+    )
+    got = gathered(pieces, "face", face_masks)
+    inner1, _ = half_inner(1, (pieces,))
+    grad_fields, token = call(
         fields_kernel,
-        [shape(band.shape, BF16)],
+        [shape(band.shape, BF16), sign],
         [pltpu.VMEM((cells, LANES), F32), pltpu.VMEM((16, LANES), F32)],
-        2_000_000_000,
-        (inner0, inner1, *arrived, *columns, cot, edge_match),
-        smem=1,
-    )
-    small = small.astype(F32) + peer[hidden:].astype(F32)
+        200_000_000,
+        (inner0, inner1, *arrived, *columns, cot, flags),
+    )
+    (pieces,) = call(
+        pack_pieces_kernel,
+        [shape((SMALL + hidden, channels), BF16)],
+        [],
+        1_000_000,
+        tuple(got),
+        after=(token,),
+    )
+    peer = swapped(pieces, "tile", 1)
 
     factor = 1.0 / math.sqrt(faces * tiles * cells)
 
@@ -800,7 +876,7 @@
         ],
         [],
         2_000_000_000,
-        (pieces, peer[:hidden], small),
+        (pieces, peer),
     )
     return (
         result[None],

time: 87.2 us -> 74.6 us (0.86)
  waiting for transfers between devices: 20.1 us -> 12.7 us
  other arithmetic: 2.19 us -> 0 us
  Pallas kernels: 29.4 us -> 27.9 us
  local copies, waits for them, and re-layouts: 2.7 us -> 1.22 us
    ppermute x16, waiting for transfers between devices: 18.4 us -> 11.5 us  [swapped(): lax.ppermute(x, axis, [(i, i ^ mask) for i in range(lax.axis_size(axis))])]
    pallas_call x11 -> x16, Pallas kernels: 29.4 us -> 27.9 us  [call(): pl.pallas_call(run, out_shape=outs, in_specs=[vmem] * (count - smem) + [s...]
    convert_element_type x1 -> x0, other arithmetic: 1.3 us -> none  [shards(): total = (mine + peer[:hidden].astype(F32)).astype(BF16)]
    slice x8 -> x4, local copies, waits for them, and re-layouts: 0.91 us -> 0.01 us  [the longest x2 0.01 us: shards(): rode = {m: got[face_masks.index(m)][count:] for m in (1, half)}]
  transfers between devices with their start and end apart: 22 -> 22, of which waited for: 10 -> 10; matrix products, arithmetic and copies ran while one was open for 0% -> 0% of each run, Pallas kernels for 19% -> 21%
where the time goes in v3:
time: 74.6 us; the launch traced here: 74.4 us
  starting transfers between devices  31.6 us (42%)
  Pallas kernels  27.9 us (37%)
  waiting for transfers between devices  12.7 us (17%)
  local copies, waits for them, and re-layouts  1.22 us (2%)
  between operations  0.95 us (1%)
    pallas_call x16, Pallas kernels, call(): pl.pallas_call(run, out_shape=outs, in_specs=[vmem] * (count - smem) + [s...  27.9 us
    ppermute x16, starting transfers between devices, swapped(): lax.ppermute(x, axis, [(i, i ^ mask) for i in range(lax.axis_size(axis))])  22.3 us
    ppermute x16, waiting for transfers between devices, swapped(): lax.ppermute(x, axis, [(i, i ^ mask) for i in range(lax.axis_size(axis))])  11.5 us
    ppermute x4, starting transfers between devices, face_swap(): return lax.ppermute(x, ('face', 'tile'), pairs)  7.76 us
    ppermute x2, starting transfers between devices, row_swap(): lax.ppermute(across, 'tile', pairs + [(j, i) for i, j in pairs])  1.51 us
  transfers between devices with their start and end apart: 22, of which 10 were waited for; matrix products, arithmetic and copies ran while one was open for 0% of the time, Pallas kernels for 21%

profile of v3, /device:TPU:0, one launch (start us, length us, event | category | flops | bytes accessed | tf_op | source)
XLA Modules:
  0.0 74.4 jit_solution(11716712859443425236)
XLA Ops:
  0.6 1.0 %copy-done.3 = bf16[1,8,128,256]{3,2,1,0:T(8,128)(2,1)S(1)} copy-done((bf16[1,8,128,256]{3,2,1,0:T(8,128)(2,1)S(1)}, bf16[1,8,128,256]{3,2,1,0:T(8,128)(2,1)}, u32[]{:S(2)}) %copy-start.3) | copy-done | bytes 524312
  1.7 0.5 collective-permute-start
  2.2 0.7 collective-permute-start.1
  2.9 0.1 copy.19.refs_3_
  3.0 0.3 collective-permute-done.refs_1_
  3.3 0.7 shard_map.172
  4.0 5.7 %collective-permute-start.3 = (bf16[48,256]{1,0:T(8,128)(2,1)S(1)}, bf16[48,256]{1,0:T(8,128)(2,1)S(1)}, u32[]{:S(2)}, u32[]{:S(2)}) collective-permute-start(bf16[48,256]{1,0:T(8,128)(2,1)S(1)} %get-tuple-element.57), channel_id=1, source_target_pairs={{0,15},{1,14},{2,13},{3,12},{4,11},{5,10},{6,9},{7,8},{8,7},{9,6},... | collective-permute-start | bytes 73736 | tf_op jit(solution)/shard_map/ppermute | solution.py:614
  9.7 1.5 %collective-permute-start.4 = (bf16[48,256]{1,0:T(8,128)(2,1)S(1)}, bf16[48,256]{1,0:T(8,128)(2,1)S(1)}, u32[]{:S(2)}, u32[]{:S(2)}) collective-permute-start(bf16[48,256]{1,0:T(8,128)(2,1)S(1)} %get-tuple-element.58), channel_id=1, source_target_pairs={{0,16},{1,17},{2,18},{3,19},{4,20},{5,21},{6,22},{7,23},{8,24},{9,... | collective-permute-start | bytes 73736 | tf_op jit(solution)/shard_map/ppermute | solution.py:614
  11.2 0.5 collective-permute-start.2
  11.8 0.0 copy-start.5
  11.8 0.0 copy-start.10
  11.8 0.0 copy-start.11
  11.9 0.0 copy-start.13
  11.9 4.1 %shard_map.173 = (f32[2176,128]{1,0:T(8,128)S(1)}, f32[2,50,8,128]{3,2,1,0:T(8,128)S(1)}) custom-call(bf16[8,128,256]{2,1,0:T(8,128)(2,1)S(1)} %bitcast.14, bf16[7,7,256]{2,1,0:T(8,128)(2,1)S(1)} %copy-done.7, f32[1,256]{1,0:T(1,128)S(1)} %bitcast.17, bf16[48,256]{1,0:T(8,128)(2,1)S(1)} %get-tuple-element.56.refs_3_), custom_call_target="tpu_custom_call" | custom-call | flops 4499999744 | bytes 1048576 | tf_op jit(solution)/shard_map/pallas_call | solution.py:35
  16.0 1.3 %collective-permute-done.5.refs_6_ = bf16[48,256]{1,0:T(8,128)(2,1)S(1)} collective-permute-done((bf16[48,256]{1,0:T(8,128)(2,1)S(1)}, bf16[48,256]{1,0:T(8,128)(2,1)S(1)}, u32[]{:S(2)}, u32[]{:S(2)}) %collective-permute-start.5) | collective-permute-done | bytes 24608 | tf_op jit(solution)/shard_map/ppermute | solution.py:614
  17.4 9.7 %shard_map.174 = (bf16[8,128,256]{2,1,0:T(8,128)(2,1)}, f32[4256,128]{1,0:T(8,128)}, f32[2312,128]{1,0:T(8,128)}, f32[1024,256]{1,0:T(8,128)S(1)}, bf16[1120,256...) custom-call(bf16[8,128,256]{2,1,0:T(8,128)(2,1)S(1)} %bitcast.15, ...), custom_call_target="tpu_custom_call" | custom-call | flops 12000000000 | bytes 1048576 | tf_op jit(solution)/shard_map/pallas_call | solution.py:35
  27.1 5.6 %collective-permute-start.6 = (bf16[1120,256]{1,0:T(8,128)(2,1)S(1)}, bf16[1120,256]{1,0:T(8,128)(2,1)S(1)}, u32[]{:S(2)}, u32[]{:S(2)}) collective-permute-start(bf16[1120,256]{1,0:T(8,128)(2,1)S(1)} %get-tuple-element.66), channel_id=1, source_target_pairs={{0,1},{1,0},{2,3},{3,2},{4,5},{5,4},{6,7},{7,6},{8,9},{9,8},{10,11... | collective-permute-start | bytes 1720328 | tf_op jit(solution)/shard_map/ppermute | solution.py:650
  32.7 1.6 %collective-permute-done.6.refs_1_ = bf16[1120,256]{1,0:T(8,128)(2,1)S(1)} collective-permute-done((bf16[1120,256]{1,0:T(8,128)(2,1)S(1)}, bf16[1120,256]{1,0:T(8,128)(2,1)S(1)}, u32[]{:S(2)}, u32[]{:S(2)}) %collective-permute-start.6) | collective-permute-done | bytes 573472 | tf_op jit(solution)/shard_map/ppermute | solution.py:650
  34.3 0.1 shard_map.175
  34.5 2.2 %collective-permute-start.9 = (bf16[256,256]{1,0:T(8,128)(2,1)S(1)}, bf16[256,256]{1,0:T(8,128)(2,1)S(1)}, u32[]{:S(2)}, u32[]{:S(2)}) collective-permute-start(bf16[256,256]{1,0:T(8,128)(2,1)S(1)} %get-tuple-element.74), channel_id=1, source_target_pairs={{0,24},{8,16},{16,8},{24,0},{1,25},{9,17},{17,9},{25,1},{2,26},{10... | collective-permute-start | bytes 393224 | tf_op jit(solution)/shard_map/ppermute | solution.py:650
  36.7 0.3 collective-permute-start.7
  37.0 1.1 %collective-permute-start.8 = (bf16[304,256]{1,0:T(8,128)(2,1)S(1)}, bf16[304,256]{1,0:T(8,128)(2,1)S(1)}, u32[]{:S(2)}, u32[]{:S(2)}) collective-permute-start(bf16[304,256]{1,0:T(8,128)(2,1)S(1)} %get-tuple-element.73), channel_id=1, source_target_pairs={{0,16},{8,24},{16,0},{24,8},{1,17},{9,25},{17,1},{25,9},{2,18},{10... | collective-permute-start | bytes 466952 | tf_op jit(solution)/shard_map/ppermute | solution.py:650
  38.0 2.0 %shard_map.176 = (f32[1088,128]{1,0:T(8,128)S(1)}, f32[8,128]{1,0:T(8,128)S(1)}) custom-call(f32[2312,128]{1,0:T(8,128)S(1)} %copy-done, f32[2,50,8,128]{3,2,1,0:T(8,128)S(1)} %get-tuple-element.60.refs_8_.refs_1_, f32[8,128]{1,0:T(8,128)S(1)} %get-tuple-element.69.refs_2_), custom_call_target="tpu_custom_call" | custom-call | flops 2100000000 | bytes 1048576 | tf_op jit(solution)/shard_map/pallas_call | solution.py:35
  40.1 3.1 %shard_map.177 = (f32[56,128]{1,0:T(8,128)S(1)}, f32[8,128]{1,0:T(8,128)S(1)}) custom-call(f32[2312,128]{1,0:T(8,128)S(1)} %copy-done, f32[4256,128]{1,0:T(8,128)S(1)} %copy-done.1, f32[8,128]{1,0:T(8,128)S(1)} %get-tuple-element.76.refs_2_), custom_call_target="tpu_custom_call" | custom-call | flops 3500000000 | bytes 1048576 | tf_op jit(solution)/shard_map/pallas_call | solution.py:35
  43.1 0.9 %collective-permute-done.7.refs_1_ = bf16[304,256]{1,0:T(8,128)(2,1)S(1)} collective-permute-done((bf16[304,256]{1,0:T(8,128)(2,1)S(1)}, bf16[304,256]{1,0:T(8,128)(2,1)S(1)}, u32[]{:S(2)}, u32[]{:S(2)}) %collective-permute-start.7) | collective-permute-done | bytes 155680 | tf_op jit(solution)/shard_map/ppermute | solution.py:650
  44.0 0.5 collective-permute-done.8.refs_2_
  44.5 0.1 shard_map.178
  44.7 2.5 %collective-permute-start.12 = (bf16[160,256]{1,0:T(8,128)(2,1)S(1)}, bf16[160,256]{1,0:T(8,128)(2,1)S(1)}, u32[]{:S(2)}, u32[]{:S(2)}) collective-permute-start(bf16[160,256]{1,0:T(8,128)(2,1)S(1)} %get-tuple-element.81), channel_id=1, source_target_pairs={{0,6},{1,7},{2,4},{3,5},{4,2},{5,3},{6,0},{7,1},{8,14},{9,15},{10,... | collective-permute-start | bytes 245768 | tf_op jit(solution)/shard_map/ppermute | solution.py:650
  47.1 2.0 %collective-permute-start.11 = (bf16[64,256]{1,0:T(8,128)(2,1)S(1)}, bf16[64,256]{1,0:T(8,128)(2,1)S(1)}, u32[]{:S(2)}, u32[]{:S(2)}) collective-permute-start(bf16[64,256]{1,0:T(8,128)(2,1)S(1)} %get-tuple-element.80), channel_id=1, source_target_pairs={{0,4},{1,5},{2,6},{3,7},{4,0},{5,1},{6,2},{7,3},{8,12},{9,13},{10,... | collective-permute-start | bytes 98312 | tf_op jit(solution)/shard_map/ppermute | solution.py:650
  49.1 3.1 %shard_map.179 = (f32[56,128]{1,0:T(8,128)S(1)}, f32[8,128]{1,0:T(8,128)}) custom-call(f32[2312,128]{1,0:T(8,128)S(1)} %copy-done, f32[4256,128]{1,0:T(8,128)S(1)} %copy-done.1, f32[8,128]{1,0:T(8,128)S(1)} %get-tuple-element.83.refs_2_), custom_call_target="tpu_custom_call" | custom-call | flops 300000000 | bytes 1048576 | tf_op jit(solution)/shard_map/pallas_call | solution.py:35
  52.3 2.5 %collective-permute-start.15 = (bf16[128,256]{1,0:T(8,128)(2,1)S(1)}, bf16[128,256]{1,0:T(8,128)(2,1)S(1)}, u32[]{:S(2)}, u32[]{:S(2)}) collective-permute-start(bf16[128,256]{1,0:T(8,128)(2,1)S(1)} %shard_map.180.refs_0_), channel_id=1, source_target_pairs={{0,6},{1,7},{2,4},{3,5},{4,2},{5,3},{6,0},{7,1},{8,14},{9,15},{10,... | collective-permute-start | bytes 196616 | tf_op jit(solution)/shard_map/ppermute | solution.py:650
  54.8 0.8 %collective-permute-start.14 = (bf16[128,256]{1,0:T(8,128)(2,1)S(1)}, bf16[128,256]{1,0:T(8,128)(2,1)S(1)}, u32[]{:S(2)}, u32[]{:S(2)}) collective-permute-start(bf16[128,256]{1,0:T(8,128)(2,1)S(1)} %shard_map.180.refs_0_), channel_id=1, source_target_pairs={{0,4},{1,5},{2,6},{3,7},{4,0},{5,1},{6,2},{7,3},{8,12},{9,13},{10,... | collective-permute-start | bytes 196616 | tf_op jit(solution)/shard_map/ppermute | solution.py:650
  55.5 1.2 %collective-permute-start.13 = (bf16[128,256]{1,0:T(8,128)(2,1)S(1)}, bf16[128,256]{1,0:T(8,128)(2,1)S(1)}, u32[]{:S(2)}, u32[]{:S(2)}) collective-permute-start(bf16[128,256]{1,0:T(8,128)(2,1)S(1)} %shard_map.180.refs_0_), channel_id=1, source_target_pairs={{0,2},{1,3},{2,0},{3,1},{4,6},{5,7},{6,4},{7,5},{8,10},{9,11},{10,... | collective-permute-start | bytes 196616 | tf_op jit(solution)/shard_map/ppermute | solution.py:650
  56.7 0.2 shard_map.181
  56.9 0.1 collective-permute-start.16
  57.0 0.9 %collective-permute-start.17 = (bf16[2,3,128,128]{3,2,1,0:T(8,128)(2,1)S(1)}, bf16[2,3,128,128]{3,2,1,0:T(8,128)(2,1)S(1)}, u32[]{:S(2)}, u32[]{:S(2)}) collective-permute-start(bf16[2,3,128,128]{3,2,1,0:T(8,128)(2,1)S(1)} %get-tuple-element.91), channel_id=1, source_target_pairs={{1,2},{3,4},{5,6},{2,1},{4,3},{6,5},{9,10},{11,12},{13,14},{10,9},... | collective-permute-start | bytes 589832 | tf_op jit(solution)/shard_map/ppermute | solution.py:633
  57.8 1.1 %collective-permute-done.15.refs_3_ = bf16[128,256]{1,0:T(8,128)(2,1)S(1)} collective-permute-done((bf16[128,256]{1,0:T(8,128)(2,1)S(1)}, bf16[128,256]{1,0:T(8,128)(2,1)S(1)}, u32[]{:S(2)}, u32[]{:S(2)}) %collective-permute-start.15) | collective-permute-done | bytes 65568 | tf_op jit(solution)/shard_map/ppermute | solution.py:650
  59.0 2.1 %collective-permute-done.14.refs_2_ = bf16[128,256]{1,0:T(8,128)(2,1)S(1)} collective-permute-done((bf16[128,256]{1,0:T(8,128)(2,1)S(1)}, bf16[128,256]{1,0:T(8,128)(2,1)S(1)}, u32[]{:S(2)}, u32[]{:S(2)}) %collective-permute-start.14) | collective-permute-done | bytes 65568 | tf_op jit(solution)/shard_map/ppermute | solution.py:650
  61.1 2.1 %collective-permute-start.20 = (bf16[320,256]{1,0:T(8,128)(2,1)S(1)}, bf16[320,256]{1,0:T(8,128)(2,1)S(1)}, u32[]{:S(2)}, u32[]{:S(2)}) collective-permute-start(bf16[320,256]{1,0:T(8,128)(2,1)S(1)} %shard_map.182.refs_2_.refs_0_), channel_id=1, source_target_pairs={{0,24},{8,16},{16,8},{24,0},{1,25},{9,17},{17,9},{25,1},{2,26},{10... | collective-permute-start | bytes 491528 | tf_op jit(solution)/shard_map/ppermute | solution.py:650
  63.2 0.4 collective-permute-start.19
  63.5 1.1 %collective-permute-start.18 = (bf16[320,256]{1,0:T(8,128)(2,1)S(1)}, bf16[320,256]{1,0:T(8,128)(2,1)S(1)}, u32[]{:S(2)}, u32[]{:S(2)}) collective-permute-start(bf16[320,256]{1,0:T(8,128)(2,1)S(1)} %shard_map.182.refs_2_.refs_0_), channel_id=1, source_target_pairs={{0,8},{8,0},{16,24},{24,16},{1,9},{9,1},{17,25},{25,17},{2,10},{10... | collective-permute-start | bytes 491528 | tf_op jit(solution)/shard_map/ppermute | solution.py:650
  64.7 2.0 %shard_map.183 = (f32[1088,128]{1,0:T(8,128)S(1)}, f32[8,128]{1,0:T(8,128)}) custom-call(f32[2312,128]{1,0:T(8,128)S(1)} %copy-done, f32[2,50,8,128]{3,2,1,0:T(8,128)S(1)} %get-tuple-element.60.refs_8_.refs_1_, bf16[320,256]{1,0:T(8,128)(2,1)S(1)} %shard_map.182.refs_2_.refs_0_), custom_call_target="tpu_custom_call" | custom-call | flops 200000000 | bytes 1048576 | tf_op jit(solution)/shard_map/pallas_call | solution.py:35
  66.7 1.1 %shard_map.184 = (bf16[8,128,256]{2,1,0:T(8,128)(2,1)}, f32[8,128]{1,0:T(8,128)S(1)}) custom-call(f32[1088,128]{1,0:T(8,128)S(1)} %get-tuple-element.70.refs_0_, f32[1088,128]{1,0:T(8,128)S(1)} %get-tuple-element.89.refs_1_, bf16[2,3,128,128]{3,2,1,0:T(8,128)(2,1)S(1)} %collective-permute-done.16.refs_2_, ...), custom_call_target="tpu_custom_call" | custom-call | flops 200000000 | bytes 1048576 | tf_op jit(solution)/shard_map/pallas_call | solution.py:35
  67.9 1.0 %collective-permute-done.20.refs_3_ = bf16[320,256]{1,0:T(8,128)(2,1)S(1)} collective-permute-done((bf16[320,256]{1,0:T(8,128)(2,1)S(1)}, bf16[320,256]{1,0:T(8,128)(2,1)S(1)}, u32[]{:S(2)}, u32[]{:S(2)}) %collective-permute-start.20) | collective-permute-done | bytes 163872 | tf_op jit(solution)/shard_map/ppermute | solution.py:650
  68.9 1.9 %collective-permute-done.19.refs_2_ = bf16[320,256]{1,0:T(8,128)(2,1)S(1)} collective-permute-done((bf16[320,256]{1,0:T(8,128)(2,1)S(1)}, bf16[320,256]{1,0:T(8,128)(2,1)S(1)}, u32[]{:S(2)}, u32[]{:S(2)}) %collective-permute-start.19) | collective-permute-done | bytes 163872 | tf_op jit(solution)/shard_map/ppermute | solution.py:650
  70.8 0.1 collective-permute-start.21
  70.9 1.9 %collective-permute-done.21.refs_1_ = bf16[1088,256]{1,0:T(8,128)(2,1)S(1)} collective-permute-done((bf16[1088,256]{1,0:T(8,128)(2,1)S(1)}, bf16[1088,256]{1,0:T(8,128)(2,1)S(1)}, u32[]{:S(2)}, u32[]{:S(2)}) %collective-permute-start.21) | collective-permute-done | bytes 557088 | tf_op jit(solution)/shard_map/ppermute | solution.py:650
  72.9 1.6 %shard_map.186 = (f32[256,1024]{1,0:T(8,128)}, f32[1024,256]{1,0:T(8,128)}, f32[7,7,256]{2,1,0:T(8,128)}, f32[1,1024]{1,0:T(1,128)}, f32[5,256]{1,0:T(8,128)}) custom-call(bf16[1088,256]{1,0:T(8,128)(2,1)S(1)} %shard_map.185.refs_0_, bf16[1088,256]{1,0:T(8,128)(2,1)S(1)} %collective-permute-done.21.refs_1_), custom_call_target="tpu_custom_call" | custom-call | flops 2000000000 | bytes 1048576 | tf_op jit(solution)/shard_map/pallas_call | solution.py:35
  (49 shorter events, 0.2 us)
Async XLA Ops:
  0.6 1.0 %copy-start.3 = (bf16[1,8,128,256]{3,2,1,0:T(8,128)(2,1)S(1)}, bf16[1,8,128,256]{3,2,1,0:T(8,128)(2,1)}, u32[]{:S(2)}) copy-start(bf16[1,8,128,256]{3,2,1,0:T(8,128)(2,1)} %param.12) | copy-start | bytes 1572868
  1.7 1.2 %copy-start.15 = (s32[4,2,3]{0,1,2:T(2,128)S(1)}, s32[4,2,3]{0,1,2:T(2,128)}, u32[]{:S(2)}) copy-start(s32[4,2,3]{0,1,2:T(2,128)} %param.14) | copy-start | bytes 292
  1.7 1.6 %collective-permute-start = (bf16[3,128,256]{2,1,0:T(8,128)(2,1)S(1)}, bf16[3,128,256]{2,1,0:T(8,128)(2,1)S(1)}, u32[]{:S(2)}, u32[]{:S(2)}) collective-permute-start(bf16[3,128,256]{2,1,0:T(8,128)(2,1)S(1)} %get-tuple-element.53), channel_id=1, source_target_pairs={{0,1},{1,0},{2,3},{3,2},{4,5},{5,4},{6,7},{7,6},{8,9},{9,8},{10,11... | collective-permute-start | bytes 589832 | tf_op jit(solution)/shard_map/ppermute | solution.py:650
  2.2 1.1 %collective-permute-start.1 = (bf16[3,128,256]{2,1,0:T(8,128)(2,1)S(1)}, bf16[3,128,256]{2,1,0:T(8,128)(2,1)S(1)}, u32[]{:S(2)}, u32[]{:S(2)}) collective-permute-start(bf16[3,128,256]{2,1,0:T(8,128)(2,1)S(1)} %get-tuple-element.54), channel_id=1, source_target_pairs={{1,2},{3,4},{5,6},{2,1},{4,3},{6,5},{9,10},{11,12},{13,14},{10,9},... | collective-permute-start | bytes 589832 | tf_op jit(solution)/shard_map/ppermute | solution.py:633
  3.3 8.5 %copy-start.4 = (bf16[1,8,128,256]{3,2,1,0:T(8,128)(2,1)S(1)}, bf16[1,8,128,256]{3,2,1,0:T(8,128)(2,1)}, u32[]{:S(2)}) copy-start(bf16[1,8,128,256]{3,2,1,0:T(8,128)(2,1)} %param.12) | copy-start | bytes 1572868
  3.3 8.5 %copy-start.7 = (bf16[7,7,256]{2,1,0:T(8,128)(2,1)S(1)}, bf16[7,7,256]{2,1,0:T(8,128)(2,1)}, u32[]{:S(2)}) copy-start(bf16[7,7,256]{2,1,0:T(8,128)(2,1)} %refs_1_.1) | copy-start | bytes 75268
  3.3 8.5 %copy-start.9 = (f32[256]{0:T(256)S(1)}, f32[256]{0:T(256)}, u32[]{:S(2)}) copy-start(f32[256]{0:T(256)} %param.16) | copy-start | bytes 3076
  4.0 12.0 %collective-permute-start.3 = (bf16[48,256]{1,0:T(8,128)(2,1)S(1)}, bf16[48,256]{1,0:T(8,128)(2,1)S(1)}, u32[]{:S(2)}, u32[]{:S(2)}) collective-permute-start(bf16[48,256]{1,0:T(8,128)(2,1)S(1)} %get-tuple-element.57), channel_id=1, source_target_pairs={{0,15},{1,14},{2,13},{3,12},{4,11},{5,10},{6,9},{7,8},{8,7},{9,6},... | collective-permute-start | bytes 73736 | tf_op jit(solution)/shard_map/ppermute | solution.py:614
  9.7 6.3 %collective-permute-start.4 = (bf16[48,256]{1,0:T(8,128)(2,1)S(1)}, bf16[48,256]{1,0:T(8,128)(2,1)S(1)}, u32[]{:S(2)}, u32[]{:S(2)}) collective-permute-start(bf16[48,256]{1,0:T(8,128)(2,1)S(1)} %get-tuple-element.58), channel_id=1, source_target_pairs={{0,16},{1,17},{2,18},{3,19},{4,20},{5,21},{6,22},{7,23},{8,24},{9,... | collective-permute-start | bytes 73736 | tf_op jit(solution)/shard_map/ppermute | solution.py:614
  11.2 6.0 %collective-permute-start.5 = (bf16[48,256]{1,0:T(8,128)(2,1)S(1)}, bf16[48,256]{1,0:T(8,128)(2,1)S(1)}, u32[]{:S(2)}, u32[]{:S(2)}) collective-permute-start(bf16[48,256]{1,0:T(8,128)(2,1)S(1)} %get-tuple-element.59), channel_id=1, source_target_pairs={{0,23},{1,22},{2,21},{3,20},{4,19},{5,18},{6,17},{7,16},{8,31},{9,... | collective-permute-start | bytes 73736 | tf_op jit(solution)/shard_map/ppermute | solution.py:614
  11.2 6.0 %collective-permute-start.2 = (bf16[48,256]{1,0:T(8,128)(2,1)S(1)}, bf16[48,256]{1,0:T(8,128)(2,1)S(1)}, u32[]{:S(2)}, u32[]{:S(2)}) collective-permute-start(bf16[48,256]{1,0:T(8,128)(2,1)S(1)} %get-tuple-element.56.refs_3_), channel_id=1, source_target_pairs={{0,8},{1,9},{2,10},{3,11},{4,12},{5,13},{6,14},{7,15},{8,0},{9,1},... | collective-permute-start | bytes 73736 | tf_op jit(solution)/shard_map/ppermute | solution.py:614
  11.8 5.5 %copy-start.2 = (bf16[1,8,128,256]{3,2,1,0:T(8,128)(2,1)S(1)}, bf16[1,8,128,256]{3,2,1,0:T(8,128)(2,1)}, u32[]{:S(2)}) copy-start(bf16[1,8,128,256]{3,2,1,0:T(8,128)(2,1)} %param.13) | copy-start | bytes 1572868
  11.8 5.5 %copy-start.5 = (bf16[256,1024]{1,0:T(8,128)(2,1)S(1)}, bf16[256,1024]{1,0:T(8,128)(2,1)}, u32[]{:S(2)}) copy-start(bf16[256,1024]{1,0:T(8,128)(2,1)} %refs_14_.1) | copy-start | bytes 1572868
  11.8 5.5 %copy-start.6 = (bf16[1024,256]{1,0:T(8,128)(2,1)S(1)}, bf16[1024,256]{1,0:T(8,128)(2,1)}, u32[]{:S(2)}) copy-start(bf16[1024,256]{1,0:T(8,128)(2,1)} %refs_15_.1) | copy-start | bytes 1572868
  11.8 5.5 %copy-start.8 = (f32[1024]{0:T(1024)S(1)}, f32[1024]{0:T(1024)}, u32[]{:S(2)}) copy-start(f32[1024]{0:T(1024)} %param.20) | copy-start | bytes 12292
  11.8 5.5 %copy-start.10 = (f32[256]{0:T(256)S(1)}, f32[256]{0:T(256)}, u32[]{:S(2)}) copy-start(f32[256]{0:T(256)} %param.17) | copy-start | bytes 3076
  11.8 5.5 %copy-start.11 = (f32[256]{0:T(256)S(1)}, f32[256]{0:T(256)}, u32[]{:S(2)}) copy-start(f32[256]{0:T(256)} %param.18) | copy-start | bytes 3076
  11.9 5.5 %copy-start.12 = (f32[256]{0:T(256)S(1)}, f32[256]{0:T(256)}, u32[]{:S(2)}) copy-start(f32[256]{0:T(256)} %param.22) | copy-start | bytes 3076
  11.9 5.5 %copy-start.13 = (f32[256]{0:T(256)S(1)}, f32[256]{0:T(256)}, u32[]{:S(2)}) copy-start(f32[256]{0:T(256)} %param.23) | copy-start | bytes 3076
  27.1 10.9 %copy-start = (f32[2312,128]{1,0:T(8,128)S(1)}, f32[2312,128]{1,0:T(8,128)}, u32[]{:S(2)}) copy-start(f32[2312,128]{1,0:T(8,128)} %get-tuple-element.64.refs_0_) | copy-start | bytes 3551236
  27.1 7.2 %collective-permute-start.6 = (bf16[1120,256]{1,0:T(8,128)(2,1)S(1)}, bf16[1120,256]{1,0:T(8,128)(2,1)S(1)}, u32[]{:S(2)}, u32[]{:S(2)}) collective-permute-start(bf16[1120,256]{1,0:T(8,128)(2,1)S(1)} %get-tuple-element.66), channel_id=1, source_target_pairs={{0,1},{1,0},{2,3},{3,2},{4,5},{5,4},{6,7},{7,6},{8,9},{9,8},{10,11... | collective-permute-start | bytes 1720328 | tf_op jit(solution)/shard_map/ppermute | solution.py:650
  34.5 8.7 %collective-permute-start.9 = (bf16[256,256]{1,0:T(8,128)(2,1)S(1)}, bf16[256,256]{1,0:T(8,128)(2,1)S(1)}, u32[]{:S(2)}, u32[]{:S(2)}) collective-permute-start(bf16[256,256]{1,0:T(8,128)(2,1)S(1)} %get-tuple-element.74), channel_id=1, source_target_pairs={{0,24},{8,16},{16,8},{24,0},{1,25},{9,17},{17,9},{25,1},{2,26},{10... | collective-permute-start | bytes 393224 | tf_op jit(solution)/shard_map/ppermute | solution.py:650
  36.7 7.4 %collective-permute-start.7 = (bf16[304,256]{1,0:T(8,128)(2,1)S(1)}, bf16[304,256]{1,0:T(8,128)(2,1)S(1)}, u32[]{:S(2)}, u32[]{:S(2)}) collective-permute-start(bf16[304,256]{1,0:T(8,128)(2,1)S(1)} %get-tuple-element.72), channel_id=1, source_target_pairs={{0,8},{8,0},{16,24},{24,16},{1,9},{9,1},{17,25},{25,17},{2,10},{10... | collective-permute-start | bytes 466952 | tf_op jit(solution)/shard_map/ppermute | solution.py:650
  37.0 7.6 %collective-permute-start.8 = (bf16[304,256]{1,0:T(8,128)(2,1)S(1)}, bf16[304,256]{1,0:T(8,128)(2,1)S(1)}, u32[]{:S(2)}, u32[]{:S(2)}) collective-permute-start(bf16[304,256]{1,0:T(8,128)(2,1)S(1)} %get-tuple-element.73), channel_id=1, source_target_pairs={{0,16},{8,24},{16,0},{24,8},{1,17},{9,25},{17,1},{25,9},{2,18},{10... | collective-permute-start | bytes 466952 | tf_op jit(solution)/shard_map/ppermute | solution.py:650
  38.0 2.0 %copy-start.1 = (f32[4256,128]{1,0:T(8,128)S(1)}, f32[4256,128]{1,0:T(8,128)}, u32[]{:S(2)}) copy-start(f32[4256,128]{1,0:T(8,128)} %get-tuple-element.75.refs_1_) | copy-start | bytes 6537220
  44.7 7.5 %collective-permute-start.12 = (bf16[160,256]{1,0:T(8,128)(2,1)S(1)}, bf16[160,256]{1,0:T(8,128)(2,1)S(1)}, u32[]{:S(2)}, u32[]{:S(2)}) collective-permute-start(bf16[160,256]{1,0:T(8,128)(2,1)S(1)} %get-tuple-element.81), channel_id=1, source_target_pairs={{0,6},{1,7},{2,4},{3,5},{4,2},{5,3},{6,0},{7,1},{8,14},{9,15},{10,... | collective-permute-start | bytes 245768 | tf_op jit(solution)/shard_map/ppermute | solution.py:650
  47.1 5.1 %collective-permute-start.10 = (bf16[64,256]{1,0:T(8,128)(2,1)S(1)}, bf16[64,256]{1,0:T(8,128)(2,1)S(1)}, u32[]{:S(2)}, u32[]{:S(2)}) collective-permute-start(bf16[64,256]{1,0:T(8,128)(2,1)S(1)} %get-tuple-element.79), channel_id=1, source_target_pairs={{0,2},{1,3},{2,0},{3,1},{4,6},{5,7},{6,4},{7,5},{8,10},{9,11},{10,... | collective-permute-start | bytes 98312 | tf_op jit(solution)/shard_map/ppermute | solution.py:650
  47.1 5.1 %collective-permute-start.11 = (bf16[64,256]{1,0:T(8,128)(2,1)S(1)}, bf16[64,256]{1,0:T(8,128)(2,1)S(1)}, u32[]{:S(2)}, u32[]{:S(2)}) collective-permute-start(bf16[64,256]{1,0:T(8,128)(2,1)S(1)} %get-tuple-element.80), channel_id=1, source_target_pairs={{0,4},{1,5},{2,6},{3,7},{4,0},{5,1},{6,2},{7,3},{8,12},{9,13},{10,... | collective-permute-start | bytes 98312 | tf_op jit(solution)/shard_map/ppermute | solution.py:650
  49.1 7.6 %copy-start.14 = (f32[1632,128]{1,0:T(8,128)S(1)}, f32[1632,128]{1,0:T(8,128)}, u32[]{:S(2)}) copy-start(f32[1632,128]{1,0:T(8,128)} %get-tuple-element.87.refs_0_) | copy-start | bytes 2506756
  52.3 6.7 %collective-permute-start.15 = (bf16[128,256]{1,0:T(8,128)(2,1)S(1)}, bf16[128,256]{1,0:T(8,128)(2,1)S(1)}, u32[]{:S(2)}, u32[]{:S(2)}) collective-permute-start(bf16[128,256]{1,0:T(8,128)(2,1)S(1)} %shard_map.180.refs_0_), channel_id=1, source_target_pairs={{0,6},{1,7},{2,4},{3,5},{4,2},{5,3},{6,0},{7,1},{8,14},{9,15},{10,... | collective-permute-start | bytes 196616 | tf_op jit(solution)/shard_map/ppermute | solution.py:650
  54.8 6.3 %collective-permute-start.14 = (bf16[128,256]{1,0:T(8,128)(2,1)S(1)}, bf16[128,256]{1,0:T(8,128)(2,1)S(1)}, u32[]{:S(2)}, u32[]{:S(2)}) collective-permute-start(bf16[128,256]{1,0:T(8,128)(2,1)S(1)} %shard_map.180.refs_0_), channel_id=1, source_target_pairs={{0,4},{1,5},{2,6},{3,7},{4,0},{5,1},{6,2},{7,3},{8,12},{9,13},{10,... | collective-permute-start | bytes 196616 | tf_op jit(solution)/shard_map/ppermute | solution.py:650
  55.5 5.6 %collective-permute-start.13 = (bf16[128,256]{1,0:T(8,128)(2,1)S(1)}, bf16[128,256]{1,0:T(8,128)(2,1)S(1)}, u32[]{:S(2)}, u32[]{:S(2)}) collective-permute-start(bf16[128,256]{1,0:T(8,128)(2,1)S(1)} %shard_map.180.refs_0_), channel_id=1, source_target_pairs={{0,2},{1,3},{2,0},{3,1},{4,6},{5,7},{6,4},{7,5},{8,10},{9,11},{10,... | collective-permute-start | bytes 196616 | tf_op jit(solution)/shard_map/ppermute | solution.py:650
  56.9 9.8 %collective-permute-start.16 = (bf16[2,3,128,128]{3,2,1,0:T(8,128)(2,1)S(1)}, bf16[2,3,128,128]{3,2,1,0:T(8,128)(2,1)S(1)}, u32[]{:S(2)}, u32[]{:S(2)}) collective-permute-start(bf16[2,3,128,128]{3,2,1,0:T(8,128)(2,1)S(1)} %get-tuple-element.90), channel_id=1, source_target_pairs={{0,1},{1,0},{2,3},{3,2},{4,5},{5,4},{6,7},{7,6},{8,9},{9,8},{10,11... | collective-permute-start | bytes 589832 | tf_op jit(solution)/shard_map/ppermute | solution.py:650
  57.0 9.7 %collective-permute-start.17 = (bf16[2,3,128,128]{3,2,1,0:T(8,128)(2,1)S(1)}, bf16[2,3,128,128]{3,2,1,0:T(8,128)(2,1)S(1)}, u32[]{:S(2)}, u32[]{:S(2)}) collective-permute-start(bf16[2,3,128,128]{3,2,1,0:T(8,128)(2,1)S(1)} %get-tuple-element.91), channel_id=1, source_target_pairs={{1,2},{3,4},{5,6},{2,1},{4,3},{6,5},{9,10},{11,12},{13,14},{10,9},... | collective-permute-start | bytes 589832 | tf_op jit(solution)/shard_map/ppermute | solution.py:633
  61.1 7.7 %collective-permute-start.20 = (bf16[320,256]{1,0:T(8,128)(2,1)S(1)}, bf16[320,256]{1,0:T(8,128)(2,1)S(1)}, u32[]{:S(2)}, u32[]{:S(2)}) collective-permute-start(bf16[320,256]{1,0:T(8,128)(2,1)S(1)} %shard_map.182.refs_2_.refs_0_), channel_id=1, source_target_pairs={{0,24},{8,16},{16,8},{24,0},{1,25},{9,17},{17,9},{25,1},{2,26},{10... | collective-permute-start | bytes 491528 | tf_op jit(solution)/shard_map/ppermute | solution.py:650
  63.2 7.6 %collective-permute-start.19 = (bf16[320,256]{1,0:T(8,128)(2,1)S(1)}, bf16[320,256]{1,0:T(8,128)(2,1)S(1)}, u32[]{:S(2)}, u32[]{:S(2)}) collective-permute-start(bf16[320,256]{1,0:T(8,128)(2,1)S(1)} %shard_map.182.refs_2_.refs_0_), channel_id=1, source_target_pairs={{0,16},{8,24},{16,0},{24,8},{1,17},{9,25},{17,1},{25,9},{2,18},{10... | collective-permute-start | bytes 491528 | tf_op jit(solution)/shard_map/ppermute | solution.py:650
  63.5 7.2 %collective-permute-start.18 = (bf16[320,256]{1,0:T(8,128)(2,1)S(1)}, bf16[320,256]{1,0:T(8,128)(2,1)S(1)}, u32[]{:S(2)}, u32[]{:S(2)}) collective-permute-start(bf16[320,256]{1,0:T(8,128)(2,1)S(1)} %shard_map.182.refs_2_.refs_0_), channel_id=1, source_target_pairs={{0,8},{8,0},{16,24},{24,16},{1,9},{9,1},{17,25},{25,17},{2,10},{10... | collective-permute-start | bytes 491528 | tf_op jit(solution)/shard_map/ppermute | solution.py:650
  70.8 2.0 %collective-permute-start.21 = (bf16[1088,256]{1,0:T(8,128)(2,1)S(1)}, bf16[1088,256]{1,0:T(8,128)(2,1)S(1)}, u32[]{:S(2)}, u32[]{:S(2)}) collective-permute-start(bf16[1088,256]{1,0:T(8,128)(2,1)S(1)} %shard_map.185.refs_0_), channel_id=1, source_target_pairs={{0,1},{1,0},{2,3},{3,2},{4,5},{5,4},{6,7},{7,6},{8,9},{9,8},{10,11... | collective-permute-start | bytes 1671176 | tf_op jit(solution)/shard_map/ppermute | solution.py:650

commit v4 on v3

--- a/solution.py
+++ b/solution.py
@@ -180,8 +180,8 @@
 
 def forward_kernel(
     band, within, across, got0, got1, got2, got3, cot, taps, gain, shift, bias2, scale, bias1, w1, w2, part, flags,
-    result_out, pad_out, grad_out, mine, other, plain_near, plain_far, rim_out, vecs, bias_out,
-    rim, result, pad, grad, conv, normed, act, pre, gbr, tmp, strip, sems,
+    result_out, pad_out, grad_out, mine, other, plain_near, plain_far, vecs, bias_out,
+    result, pad, grad, conv, normed, act, pre, gbr, tmp, strip, sems,
 ):
     rows, cols, channels = band.shape
     halves = channels // LANES
@@ -322,7 +322,7 @@
 
     bias_out[...] = jnp.zeros_like(bias_out)
     zero = jnp.zeros((1, channels), F32)
-    sums = lax.fori_loop(0, rows // 2, chunk, (zero,) * 5)
+    sums = lax.fori_loop(0, rows // 2, chunk, (zero,) * 5, unroll=True)
     sums = (sums[0], sums[1], sums[2], sums[3] * scale, sums[4])
     vecs[...] = jnp.concatenate(list(sums) + [zero] * 3, axis=0)
 
@@ -331,16 +331,6 @@
     keep_result = pltpu.make_async_copy(result, result_out, sems.at[2])
     keep_result.start()
 
-    def rim_half(h, carry):
-        for k in range(6):
-            acc = spread_row(grad, taps, h, k if k < 3 else rows + k, rows, pitch, groups)
-            for j in range(groups):
-                rim[pl.ds((h * 6 + k) * cpitch + j, SUB, stride=groups), :] = acc[j]
-        return carry
-
-    lax.fori_loop(0, halves, rim_half, 0)
-    keep_rim = pltpu.make_async_copy(rim, rim_out, sems.at[3])
-    keep_rim.start()
     strip[...] = jnp.zeros_like(strip)
     for h in range(halves):
         lane = slice(h * LANES, (h + 1) * LANES)
@@ -385,7 +375,6 @@
     keep_pad.wait()
     keep_grad.wait()
     keep_result.wait()
-    keep_rim.wait()
 
 
 def spread_row(grad, taps, h, o, rows, pitch, groups):
@@ -453,28 +442,31 @@
     some(6, 1)
 
 
-def rims_kernel(rim, got0, got1, got2, got3, flags, within, across, token, total, held):
+def rims_kernel(grad, taps, got0, got1, got2, got3, flags, within, across, token, total, held):
     token[...] = jnp.zeros_like(token)
     halves, _, cols, _ = within.shape
     even = (lax.axis_index("tile") & 1) == 0
-    cpitch = rim.shape[0] // (halves * 6)
+    rows = 8
+    pitch = cols + 2 * LEAD
+    groups = cols // SUB + 1
+    cpitch = groups * SUB
     first, turn_near, turn_far = glued(flags)
     arrived = unpack_columns(first, turn_near, turn_far, (got0, got1, got2, got3))
     for h in range(halves):
         for k in range(6):
-            total[k * cols : (k + 1) * cols, :] = rim[
-                (h * 6 + k) * cpitch : (h * 6 + k) * cpitch + cols, :
-            ]
+            acc = spread_row(grad, taps, h, k if k < 3 else rows + k, rows, pitch, groups)
+            for j in range(groups):
+                total[pl.ds(k * cpitch + j, SUB, stride=groups), :] = acc[j]
         for side in range(2):
             for d in range(3):
                 held[...] = arrived(side, h, d)
                 for k in range(6):
                     o = k if k < 3 else k + 8
-                    at = k * cols + (d if side == 0 else cols - 1 - d)
+                    at = k * cpitch + (d if side == 0 else cols - 1 - d)
                     total[at : at + 1, :] += held[o : o + 1, :]
         for k in range(3):
-            top = total[k * cols : (k + 1) * cols, :].astype(BF16)
-            bottom = total[(k + 3) * cols : (k + 4) * cols, :].astype(BF16)
+            top = total[k * cpitch : k * cpitch + cols, :].astype(BF16)
+            bottom = total[(k + 3) * cpitch : (k + 3) * cpitch + cols, :].astype(BF16)
             within[h, k] = jnp.where(even, bottom, top)
             across[h, k] = jnp.where(even, top, bottom)
 
@@ -724,7 +716,7 @@
         after=(sides[0],),
     )
     part, taps = kept(part), kept(taps)
-    result, pad, grad, mine, other, plain_near, plain_far, rim, vecs, bias_out = call(
+    result, pad, grad, mine, other, plain_near, plain_far, vecs, bias_out = call(
         forward_kernel,
         [
             pltpu.HBM(band.shape, BF16),
@@ -734,12 +726,10 @@
             shape((hidden + 96, channels), BF16),
             shape((48, channels), BF16),
             shape((48, channels), BF16),
-            pltpu.HBM((halves * 6 * (cols + SUB), LANES), F32),
             shape((8, channels), F32),
             shape((1, hidden), F32),
         ],
         [
-            pltpu.VMEM((halves * 6 * (cols + SUB), LANES), F32),
             pltpu.VMEM(band.shape, BF16),
             pltpu.VMEM((halves * ext * wide, LANES), F32),
             pltpu.VMEM((halves * rows * pitch + SUB, LANES), F32),
@@ -750,7 +740,7 @@
             pltpu.VMEM((cells, channels), BF16),
             pltpu.VMEM((2 * cols, channels), F32),
             pltpu.VMEM((12 * 32, LANES), F32),
-            pltpu.SemaphoreType.DMA((4,)),
+            pltpu.SemaphoreType.DMA((3,)),
         ],
         12_000_000_000,
         (
@@ -759,7 +749,7 @@
             flags,
         ),
         limit=20,
-        left=(0, 1, 2, 7),
+        left=(0, 1, 2),
     )
 
     face_masks = list(range(faces - 1, 0, -1))
@@ -828,9 +818,9 @@
     within, across, token = call(
         rims_kernel,
         [shape((halves, 3, cols, LANES), BF16)] * 2 + [sign],
-        [pltpu.VMEM((6 * cols, LANES), F32), pltpu.VMEM((16, LANES), F32)],
+        [pltpu.VMEM((6 * (cols + SUB), LANES), F32), pltpu.VMEM((16, LANES), F32)],
         900_000_000,
-        (rim, *columns, flags),
+        (grad, taps, *columns, flags),
     )
     arrived = row_swap(within, across)
     (pieces,) = call(

time: 74.6 us -> 73.4 us (0.984)
    pallas_call x16, Pallas kernels: 27.9 us -> 27.2 us  [call(): pl.pallas_call(run, out_shape=outs, in_specs=[vmem] * (count - smem) + [s...]
  transfers between devices with their start and end apart: 22 -> 22, of which waited for: 10 -> 10; matrix products, arithmetic and copies ran while one was open for 0% -> 0% of each run, Pallas kernels for 21% -> 22%
where the time goes in v4:
time: 73.4 us; the launch traced here: 73.2 us
  starting transfers between devices  31.4 us (43%)
  Pallas kernels  27.2 us (37%)
  waiting for transfers between devices  12.5 us (17%)
  local copies, waits for them, and re-layouts  1.22 us (2%)
  between operations  0.94 us (1%)
    pallas_call x16, Pallas kernels, call(): pl.pallas_call(run, out_shape=outs, in_specs=[vmem] * (count - smem) + [s...  27.2 us
    ppermute x16, starting transfers between devices, swapped(): lax.ppermute(x, axis, [(i, i ^ mask) for i in range(lax.axis_size(axis))])  22.3 us
    ppermute x16, waiting for transfers between devices, swapped(): lax.ppermute(x, axis, [(i, i ^ mask) for i in range(lax.axis_size(axis))])  11.2 us
    ppermute x4, starting transfers between devices, face_swap(): return lax.ppermute(x, ('face', 'tile'), pairs)  7.76 us
  transfers between devices with their start and end apart: 22, of which 10 were waited for; matrix products, arithmetic and copies ran while one was open for 0% of the time, Pallas kernels for 22%

profile of v4, /device:TPU:0, one launch (start us, length us, event | category | flops | bytes accessed | tf_op | source)
XLA Modules:
  0.0 73.2 jit_solution(4647170946943598889)
XLA Ops:
  0.6 0.0 copy-start.3
  0.6 1.0 %copy-done.3 = bf16[1,8,128,256]{3,2,1,0:T(8,128)(2,1)S(1)} copy-done((bf16[1,8,128,256]{3,2,1,0:T(8,128)(2,1)S(1)}, bf16[1,8,128,256]{3,2,1,0:T(8,128)(2,1)}, u32[]{:S(2)}) %copy-start.3) | copy-done | bytes 524312
  1.7 0.5 collective-permute-start
  2.2 0.7 collective-permute-start.1
  2.9 0.1 copy.19.refs_3_
  3.0 0.3 collective-permute-done.refs_1_
  3.3 0.7 shard_map.172
  4.0 5.7 %collective-permute-start.3 = (bf16[48,256]{1,0:T(8,128)(2,1)S(1)}, bf16[48,256]{1,0:T(8,128)(2,1)S(1)}, u32[]{:S(2)}, u32[]{:S(2)}) collective-permute-start(bf16[48,256]{1,0:T(8,128)(2,1)S(1)} %get-tuple-element.56), channel_id=1, source_target_pairs={{0,15},{1,14},{2,13},{3,12},{4,11},{5,10},{6,9},{7,8},{8,7},{9,6},... | collective-permute-start | bytes 73736 | tf_op jit(solution)/shard_map/ppermute | solution.py:606
  9.7 1.5 %collective-permute-start.4 = (bf16[48,256]{1,0:T(8,128)(2,1)S(1)}, bf16[48,256]{1,0:T(8,128)(2,1)S(1)}, u32[]{:S(2)}, u32[]{:S(2)}) collective-permute-start(bf16[48,256]{1,0:T(8,128)(2,1)S(1)} %get-tuple-element.57), channel_id=1, source_target_pairs={{0,16},{1,17},{2,18},{3,19},{4,20},{5,21},{6,22},{7,23},{8,24},{9,... | collective-permute-start | bytes 73736 | tf_op jit(solution)/shard_map/ppermute | solution.py:606
  11.2 0.5 collective-permute-start.2
  11.8 0.0 copy-start.8
  11.8 0.0 copy-start.10
  11.9 4.1 %shard_map.173 = (f32[2176,128]{1,0:T(8,128)S(1)}, f32[2,50,8,128]{3,2,1,0:T(8,128)S(1)}) custom-call(bf16[8,128,256]{2,1,0:T(8,128)(2,1)S(1)} %bitcast.14, bf16[7,7,256]{2,1,0:T(8,128)(2,1)S(1)} %copy-done.7, f32[1,256]{1,0:T(1,128)S(1)} %bitcast.17, bf16[48,256]{1,0:T(8,128)(2,1)S(1)} %get-tuple-element.55.refs_3_), custom_call_target="tpu_custom_call" | custom-call | flops 4499999744 | bytes 1048576 | tf_op jit(solution)/shard_map/pallas_call | solution.py:35
  16.0 1.3 %collective-permute-done.5.refs_6_ = bf16[48,256]{1,0:T(8,128)(2,1)S(1)} collective-permute-done((bf16[48,256]{1,0:T(8,128)(2,1)S(1)}, bf16[48,256]{1,0:T(8,128)(2,1)S(1)}, u32[]{:S(2)}, u32[]{:S(2)}) %collective-permute-start.5) | collective-permute-done | bytes 24608 | tf_op jit(solution)/shard_map/ppermute | solution.py:606
  17.4 8.1 %shard_map.174 = (bf16[8,128,256]{2,1,0:T(8,128)(2,1)}, f32[4256,128]{1,0:T(8,128)}, f32[2312,128]{1,0:T(8,128)}, f32[1024,256]{1,0:T(8,128)S(1)}, bf16[1120,256...) custom-call(bf16[8,128,256]{2,1,0:T(8,128)(2,1)S(1)} %bitcast.15, ...), custom_call_target="tpu_custom_call" | custom-call | flops 12000000000 | bytes 1048576 | tf_op jit(solution)/shard_map/pallas_call | solution.py:35
  25.5 5.6 %collective-permute-start.6 = (bf16[1120,256]{1,0:T(8,128)(2,1)S(1)}, bf16[1120,256]{1,0:T(8,128)(2,1)S(1)}, u32[]{:S(2)}, u32[]{:S(2)}) collective-permute-start(bf16[1120,256]{1,0:T(8,128)(2,1)S(1)} %get-tuple-element.65), channel_id=1, source_target_pairs={{0,1},{1,0},{2,3},{3,2},{4,5},{5,4},{6,7},{7,6},{8,9},{9,8},{10,11... | collective-permute-start | bytes 1720328 | tf_op jit(solution)/shard_map/ppermute | solution.py:642
  31.1 1.6 %collective-permute-done.6.refs_1_ = bf16[1120,256]{1,0:T(8,128)(2,1)S(1)} collective-permute-done((bf16[1120,256]{1,0:T(8,128)(2,1)S(1)}, bf16[1120,256]{1,0:T(8,128)(2,1)S(1)}, u32[]{:S(2)}, u32[]{:S(2)}) %collective-permute-start.6) | collective-permute-done | bytes 573472 | tf_op jit(solution)/shard_map/ppermute | solution.py:642
  32.7 0.1 shard_map.175
  32.8 2.2 %collective-permute-start.9 = (bf16[256,256]{1,0:T(8,128)(2,1)S(1)}, bf16[256,256]{1,0:T(8,128)(2,1)S(1)}, u32[]{:S(2)}, u32[]{:S(2)}) collective-permute-start(bf16[256,256]{1,0:T(8,128)(2,1)S(1)} %get-tuple-element.73), channel_id=1, source_target_pairs={{0,24},{8,16},{16,8},{24,0},{1,25},{9,17},{17,9},{25,1},{2,26},{10... | collective-permute-start | bytes 393224 | tf_op jit(solution)/shard_map/ppermute | solution.py:642
  35.0 0.3 collective-permute-start.7
  35.3 1.1 %collective-permute-start.8 = (bf16[304,256]{1,0:T(8,128)(2,1)S(1)}, bf16[304,256]{1,0:T(8,128)(2,1)S(1)}, u32[]{:S(2)}, u32[]{:S(2)}) collective-permute-start(bf16[304,256]{1,0:T(8,128)(2,1)S(1)} %get-tuple-element.72), channel_id=1, source_target_pairs={{0,16},{8,24},{16,0},{24,8},{1,17},{9,25},{17,1},{25,9},{2,18},{10... | collective-permute-start | bytes 466952 | tf_op jit(solution)/shard_map/ppermute | solution.py:642
  36.4 2.0 %shard_map.176 = (f32[1088,128]{1,0:T(8,128)S(1)}, f32[8,128]{1,0:T(8,128)S(1)}) custom-call(f32[2312,128]{1,0:T(8,128)S(1)} %copy-done, f32[2,50,8,128]{3,2,1,0:T(8,128)S(1)} %get-tuple-element.59.refs_8_.refs_1_, f32[8,128]{1,0:T(8,128)S(1)} %get-tuple-element.68.refs_2_), custom_call_target="tpu_custom_call" | custom-call | flops 2100000000 | bytes 1048576 | tf_op jit(solution)/shard_map/pallas_call | solution.py:35
  38.4 3.2 %shard_map.177 = (f32[56,128]{1,0:T(8,128)S(1)}, f32[8,128]{1,0:T(8,128)S(1)}) custom-call(f32[2312,128]{1,0:T(8,128)S(1)} %copy-done, f32[4256,128]{1,0:T(8,128)S(1)} %copy-done.1, f32[8,128]{1,0:T(8,128)S(1)} %get-tuple-element.75.refs_2_), custom_call_target="tpu_custom_call" | custom-call | flops 3500000000 | bytes 1048576 | tf_op jit(solution)/shard_map/pallas_call | solution.py:35
  41.7 0.7 collective-permute-done.7.refs_1_
  42.4 0.5 collective-permute-done.8.refs_2_
  42.9 0.1 shard_map.178
  43.0 2.5 %collective-permute-start.12 = (bf16[160,256]{1,0:T(8,128)(2,1)S(1)}, bf16[160,256]{1,0:T(8,128)(2,1)S(1)}, u32[]{:S(2)}, u32[]{:S(2)}) collective-permute-start(bf16[160,256]{1,0:T(8,128)(2,1)S(1)} %get-tuple-element.80), channel_id=1, source_target_pairs={{0,6},{1,7},{2,4},{3,5},{4,2},{5,3},{6,0},{7,1},{8,14},{9,15},{10,... | collective-permute-start | bytes 245768 | tf_op jit(solution)/shard_map/ppermute | solution.py:642
  45.5 2.0 %collective-permute-start.11 = (bf16[64,256]{1,0:T(8,128)(2,1)S(1)}, bf16[64,256]{1,0:T(8,128)(2,1)S(1)}, u32[]{:S(2)}, u32[]{:S(2)}) collective-permute-start(bf16[64,256]{1,0:T(8,128)(2,1)S(1)} %get-tuple-element.79), channel_id=1, source_target_pairs={{0,4},{1,5},{2,6},{3,7},{4,0},{5,1},{6,2},{7,3},{8,12},{9,13},{10,... | collective-permute-start | bytes 98312 | tf_op jit(solution)/shard_map/ppermute | solution.py:642
  47.5 3.1 %shard_map.179 = (f32[56,128]{1,0:T(8,128)S(1)}, f32[8,128]{1,0:T(8,128)}) custom-call(f32[2312,128]{1,0:T(8,128)S(1)} %copy-done, f32[4256,128]{1,0:T(8,128)S(1)} %copy-done.1, f32[8,128]{1,0:T(8,128)S(1)} %get-tuple-element.82.refs_2_), custom_call_target="tpu_custom_call" | custom-call | flops 300000000 | bytes 1048576 | tf_op jit(solution)/shard_map/pallas_call | solution.py:35
  50.6 2.5 %collective-permute-start.15 = (bf16[128,256]{1,0:T(8,128)(2,1)S(1)}, bf16[128,256]{1,0:T(8,128)(2,1)S(1)}, u32[]{:S(2)}, u32[]{:S(2)}) collective-permute-start(bf16[128,256]{1,0:T(8,128)(2,1)S(1)} %shard_map.180.refs_0_), channel_id=1, source_target_pairs={{0,6},{1,7},{2,4},{3,5},{4,2},{5,3},{6,0},{7,1},{8,14},{9,15},{10,... | collective-permute-start | bytes 196616 | tf_op jit(solution)/shard_map/ppermute | solution.py:642
  53.1 0.8 %collective-permute-start.14 = (bf16[128,256]{1,0:T(8,128)(2,1)S(1)}, bf16[128,256]{1,0:T(8,128)(2,1)S(1)}, u32[]{:S(2)}, u32[]{:S(2)}) collective-permute-start(bf16[128,256]{1,0:T(8,128)(2,1)S(1)} %shard_map.180.refs_0_), channel_id=1, source_target_pairs={{0,4},{1,5},{2,6},{3,7},{4,0},{5,1},{6,2},{7,3},{8,12},{9,13},{10,... | collective-permute-start | bytes 196616 | tf_op jit(solution)/shard_map/ppermute | solution.py:642
  53.9 1.2 %collective-permute-start.13 = (bf16[128,256]{1,0:T(8,128)(2,1)S(1)}, bf16[128,256]{1,0:T(8,128)(2,1)S(1)}, u32[]{:S(2)}, u32[]{:S(2)}) collective-permute-start(bf16[128,256]{1,0:T(8,128)(2,1)S(1)} %shard_map.180.refs_0_), channel_id=1, source_target_pairs={{0,2},{1,3},{2,0},{3,1},{4,6},{5,7},{6,4},{7,5},{8,10},{9,11},{10,... | collective-permute-start | bytes 196616 | tf_op jit(solution)/shard_map/ppermute | solution.py:642
  55.1 0.9 %shard_map.181 = (bf16[2,3,128,128]{3,2,1,0:T(8,128)(2,1)S(1)}, bf16[2,3,128,128]{3,2,1,0:T(8,128)(2,1)S(1)}, f32[8,128]{1,0:T(8,128)S(1)}) custom-call(f32[2312,128]{1,0:T(8,128)S(1)} %copy-done, f32[2,50,8,128]{3,2,1,0:T(8,128)S(1)} %get-tuple-element.59.refs_8_.refs_1_, bf16[48,256]{1,0:T(8,128)(2,1)S(1)} %slice.21.refs_2_.refs_4_, ...), custom_call_target="tpu_custom_call" | custom-call | flops 900000000 | bytes 1048576 | tf_op jit(solution)/shard_map/pallas_call | solution.py:35
  56.0 0.1 collective-permute-start.16
  56.0 0.7 collective-permute-start.17
  56.7 0.6 collective-permute-done.15.refs_3_
  57.3 2.2 %collective-permute-done.14.refs_2_ = bf16[128,256]{1,0:T(8,128)(2,1)S(1)} collective-permute-done((bf16[128,256]{1,0:T(8,128)(2,1)S(1)}, bf16[128,256]{1,0:T(8,128)(2,1)S(1)}, u32[]{:S(2)}, u32[]{:S(2)}) %collective-permute-start.14) | collective-permute-done | bytes 65568 | tf_op jit(solution)/shard_map/ppermute | solution.py:642
  59.5 2.1 %collective-permute-start.20 = (bf16[320,256]{1,0:T(8,128)(2,1)S(1)}, bf16[320,256]{1,0:T(8,128)(2,1)S(1)}, u32[]{:S(2)}, u32[]{:S(2)}) collective-permute-start(bf16[320,256]{1,0:T(8,128)(2,1)S(1)} %shard_map.182.refs_2_.refs_0_), channel_id=1, source_target_pairs={{0,24},{8,16},{16,8},{24,0},{1,25},{9,17},{17,9},{25,1},{2,26},{10... | collective-permute-start | bytes 491528 | tf_op jit(solution)/shard_map/ppermute | solution.py:642
  61.6 0.4 collective-permute-start.19
  61.9 1.1 %collective-permute-start.18 = (bf16[320,256]{1,0:T(8,128)(2,1)S(1)}, bf16[320,256]{1,0:T(8,128)(2,1)S(1)}, u32[]{:S(2)}, u32[]{:S(2)}) collective-permute-start(bf16[320,256]{1,0:T(8,128)(2,1)S(1)} %shard_map.182.refs_2_.refs_0_), channel_id=1, source_target_pairs={{0,8},{8,0},{16,24},{24,16},{1,9},{9,1},{17,25},{25,17},{2,10},{10... | collective-permute-start | bytes 491528 | tf_op jit(solution)/shard_map/ppermute | solution.py:642
  63.1 2.0 %shard_map.183 = (f32[1088,128]{1,0:T(8,128)S(1)}, f32[8,128]{1,0:T(8,128)}) custom-call(f32[2312,128]{1,0:T(8,128)S(1)} %copy-done, f32[2,50,8,128]{3,2,1,0:T(8,128)S(1)} %get-tuple-element.59.refs_8_.refs_1_, bf16[320,256]{1,0:T(8,128)(2,1)S(1)} %shard_map.182.refs_2_.refs_0_), custom_call_target="tpu_custom_call" | custom-call | flops 200000000 | bytes 1048576 | tf_op jit(solution)/shard_map/pallas_call | solution.py:35
  65.1 1.1 %shard_map.184 = (bf16[8,128,256]{2,1,0:T(8,128)(2,1)}, f32[8,128]{1,0:T(8,128)S(1)}) custom-call(f32[1088,128]{1,0:T(8,128)S(1)} %get-tuple-element.69.refs_0_, f32[1088,128]{1,0:T(8,128)S(1)} %get-tuple-element.87.refs_1_, bf16[2,3,128,128]{3,2,1,0:T(8,128)(2,1)S(1)} %collective-permute-done.16.refs_2_, ...), custom_call_target="tpu_custom_call" | custom-call | flops 200000000 | bytes 1048576 | tf_op jit(solution)/shard_map/pallas_call | solution.py:35
  66.2 0.9 %collective-permute-done.20.refs_3_ = bf16[320,256]{1,0:T(8,128)(2,1)S(1)} collective-permute-done((bf16[320,256]{1,0:T(8,128)(2,1)S(1)}, bf16[320,256]{1,0:T(8,128)(2,1)S(1)}, u32[]{:S(2)}, u32[]{:S(2)}) %collective-permute-start.20) | collective-permute-done | bytes 163872 | tf_op jit(solution)/shard_map/ppermute | solution.py:642
  67.2 2.4 %collective-permute-done.19.refs_2_ = bf16[320,256]{1,0:T(8,128)(2,1)S(1)} collective-permute-done((bf16[320,256]{1,0:T(8,128)(2,1)S(1)}, bf16[320,256]{1,0:T(8,128)(2,1)S(1)}, u32[]{:S(2)}, u32[]{:S(2)}) %collective-permute-start.19) | collective-permute-done | bytes 163872 | tf_op jit(solution)/shard_map/ppermute | solution.py:642
  69.6 0.0 collective-permute-done.18.refs_1_
  69.6 0.1 collective-permute-start.21
  69.7 1.9 %collective-permute-done.21.refs_1_ = bf16[1088,256]{1,0:T(8,128)(2,1)S(1)} collective-permute-done((bf16[1088,256]{1,0:T(8,128)(2,1)S(1)}, bf16[1088,256]{1,0:T(8,128)(2,1)S(1)}, u32[]{:S(2)}, u32[]{:S(2)}) %collective-permute-start.21) | collective-permute-done | bytes 557088 | tf_op jit(solution)/shard_map/ppermute | solution.py:642
  71.7 1.6 %shard_map.186 = (f32[256,1024]{1,0:T(8,128)}, f32[1024,256]{1,0:T(8,128)}, f32[7,7,256]{2,1,0:T(8,128)}, f32[1,1024]{1,0:T(1,128)}, f32[5,256]{1,0:T(8,128)}) custom-call(bf16[1088,256]{1,0:T(8,128)(2,1)S(1)} %shard_map.185.refs_0_, bf16[1088,256]{1,0:T(8,128)(2,1)S(1)} %collective-permute-done.21.refs_1_), custom_call_target="tpu_custom_call" | custom-call | flops 2000000000 | bytes 1048576 | tf_op jit(solution)/shard_map/pallas_call | solution.py:35
  (47 shorter events, 0.2 us)
Async XLA Ops:
  0.6 1.0 %copy-start.3 = (bf16[1,8,128,256]{3,2,1,0:T(8,128)(2,1)S(1)}, bf16[1,8,128,256]{3,2,1,0:T(8,128)(2,1)}, u32[]{:S(2)}) copy-start(bf16[1,8,128,256]{3,2,1,0:T(8,128)(2,1)} %param.12) | copy-start | bytes 1572868
  1.7 1.2 %copy-start.14 = (s32[4,2,3]{0,1,2:T(2,128)S(1)}, s32[4,2,3]{0,1,2:T(2,128)}, u32[]{:S(2)}) copy-start(s32[4,2,3]{0,1,2:T(2,128)} %param.14) | copy-start | bytes 292
  1.7 1.6 %collective-permute-start = (bf16[3,128,256]{2,1,0:T(8,128)(2,1)S(1)}, bf16[3,128,256]{2,1,0:T(8,128)(2,1)S(1)}, u32[]{:S(2)}, u32[]{:S(2)}) collective-permute-start(bf16[3,128,256]{2,1,0:T(8,128)(2,1)S(1)} %get-tuple-element.52), channel_id=1, source_target_pairs={{0,1},{1,0},{2,3},{3,2},{4,5},{5,4},{6,7},{7,6},{8,9},{9,8},{10,11... | collective-permute-start | bytes 589832 | tf_op jit(solution)/shard_map/ppermute | solution.py:642
  2.2 1.1 %collective-permute-start.1 = (bf16[3,128,256]{2,1,0:T(8,128)(2,1)S(1)}, bf16[3,128,256]{2,1,0:T(8,128)(2,1)S(1)}, u32[]{:S(2)}, u32[]{:S(2)}) collective-permute-start(bf16[3,128,256]{2,1,0:T(8,128)(2,1)S(1)} %get-tuple-element.53), channel_id=1, source_target_pairs={{1,2},{3,4},{5,6},{2,1},{4,3},{6,5},{9,10},{11,12},{13,14},{10,9},... | collective-permute-start | bytes 589832 | tf_op jit(solution)/shard_map/ppermute | solution.py:625
  3.3 8.5 %copy-start.4 = (bf16[1,8,128,256]{3,2,1,0:T(8,128)(2,1)S(1)}, bf16[1,8,128,256]{3,2,1,0:T(8,128)(2,1)}, u32[]{:S(2)}) copy-start(bf16[1,8,128,256]{3,2,1,0:T(8,128)(2,1)} %param.12) | copy-start | bytes 1572868
  3.3 8.5 %copy-start.7 = (bf16[7,7,256]{2,1,0:T(8,128)(2,1)S(1)}, bf16[7,7,256]{2,1,0:T(8,128)(2,1)}, u32[]{:S(2)}) copy-start(bf16[7,7,256]{2,1,0:T(8,128)(2,1)} %refs_1_.1) | copy-start | bytes 75268
  3.3 8.5 %copy-start.9 = (f32[256]{0:T(256)S(1)}, f32[256]{0:T(256)}, u32[]{:S(2)}) copy-start(f32[256]{0:T(256)} %param.16) | copy-start | bytes 3076
  4.0 12.0 %collective-permute-start.3 = (bf16[48,256]{1,0:T(8,128)(2,1)S(1)}, bf16[48,256]{1,0:T(8,128)(2,1)S(1)}, u32[]{:S(2)}, u32[]{:S(2)}) collective-permute-start(bf16[48,256]{1,0:T(8,128)(2,1)S(1)} %get-tuple-element.56), channel_id=1, source_target_pairs={{0,15},{1,14},{2,13},{3,12},{4,11},{5,10},{6,9},{7,8},{8,7},{9,6},... | collective-permute-start | bytes 73736 | tf_op jit(solution)/shard_map/ppermute | solution.py:606
  9.7 6.3 %collective-permute-start.4 = (bf16[48,256]{1,0:T(8,128)(2,1)S(1)}, bf16[48,256]{1,0:T(8,128)(2,1)S(1)}, u32[]{:S(2)}, u32[]{:S(2)}) collective-permute-start(bf16[48,256]{1,0:T(8,128)(2,1)S(1)} %get-tuple-element.57), channel_id=1, source_target_pairs={{0,16},{1,17},{2,18},{3,19},{4,20},{5,21},{6,22},{7,23},{8,24},{9,... | collective-permute-start | bytes 73736 | tf_op jit(solution)/shard_map/ppermute | solution.py:606
  11.2 6.0 %collective-permute-start.5 = (bf16[48,256]{1,0:T(8,128)(2,1)S(1)}, bf16[48,256]{1,0:T(8,128)(2,1)S(1)}, u32[]{:S(2)}, u32[]{:S(2)}) collective-permute-start(bf16[48,256]{1,0:T(8,128)(2,1)S(1)} %get-tuple-element.58), channel_id=1, source_target_pairs={{0,23},{1,22},{2,21},{3,20},{4,19},{5,18},{6,17},{7,16},{8,31},{9,... | collective-permute-start | bytes 73736 | tf_op jit(solution)/shard_map/ppermute | solution.py:606
  11.2 6.0 %collective-permute-start.2 = (bf16[48,256]{1,0:T(8,128)(2,1)S(1)}, bf16[48,256]{1,0:T(8,128)(2,1)S(1)}, u32[]{:S(2)}, u32[]{:S(2)}) collective-permute-start(bf16[48,256]{1,0:T(8,128)(2,1)S(1)} %get-tuple-element.55.refs_3_), channel_id=1, source_target_pairs={{0,8},{1,9},{2,10},{3,11},{4,12},{5,13},{6,14},{7,15},{8,0},{9,1},... | collective-permute-start | bytes 73736 | tf_op jit(solution)/shard_map/ppermute | solution.py:606
  11.8 5.5 %copy-start.2 = (bf16[1,8,128,256]{3,2,1,0:T(8,128)(2,1)S(1)}, bf16[1,8,128,256]{3,2,1,0:T(8,128)(2,1)}, u32[]{:S(2)}) copy-start(bf16[1,8,128,256]{3,2,1,0:T(8,128)(2,1)} %param.13) | copy-start | bytes 1572868
  11.8 5.5 %copy-start.5 = (bf16[256,1024]{1,0:T(8,128)(2,1)S(1)}, bf16[256,1024]{1,0:T(8,128)(2,1)}, u32[]{:S(2)}) copy-start(bf16[256,1024]{1,0:T(8,128)(2,1)} %refs_14_.1) | copy-start | bytes 1572868
  11.8 5.5 %copy-start.6 = (bf16[1024,256]{1,0:T(8,128)(2,1)S(1)}, bf16[1024,256]{1,0:T(8,128)(2,1)}, u32[]{:S(2)}) copy-start(bf16[1024,256]{1,0:T(8,128)(2,1)} %refs_15_.1) | copy-start | bytes 1572868
  11.8 5.5 %copy-start.8 = (f32[1024]{0:T(1024)S(1)}, f32[1024]{0:T(1024)}, u32[]{:S(2)}) copy-start(f32[1024]{0:T(1024)} %param.20) | copy-start | bytes 12292
  11.8 5.5 %copy-start.10 = (f32[256]{0:T(256)S(1)}, f32[256]{0:T(256)}, u32[]{:S(2)}) copy-start(f32[256]{0:T(256)} %param.17) | copy-start | bytes 3076
  11.8 5.5 %copy-start.11 = (f32[256]{0:T(256)S(1)}, f32[256]{0:T(256)}, u32[]{:S(2)}) copy-start(f32[256]{0:T(256)} %param.18) | copy-start | bytes 3076
  11.9 5.5 %copy-start.12 = (f32[256]{0:T(256)S(1)}, f32[256]{0:T(256)}, u32[]{:S(2)}) copy-start(f32[256]{0:T(256)} %param.22) | copy-start | bytes 3076
  11.9 5.5 %copy-start.13 = (f32[256]{0:T(256)S(1)}, f32[256]{0:T(256)}, u32[]{:S(2)}) copy-start(f32[256]{0:T(256)} %param.23) | copy-start | bytes 3076
  25.5 10.9 %copy-start = (f32[2312,128]{1,0:T(8,128)S(1)}, f32[2312,128]{1,0:T(8,128)}, u32[]{:S(2)}) copy-start(f32[2312,128]{1,0:T(8,128)} %get-tuple-element.63.refs_0_) | copy-start | bytes 3551236
  25.5 7.2 %collective-permute-start.6 = (bf16[1120,256]{1,0:T(8,128)(2,1)S(1)}, bf16[1120,256]{1,0:T(8,128)(2,1)S(1)}, u32[]{:S(2)}, u32[]{:S(2)}) collective-permute-start(bf16[1120,256]{1,0:T(8,128)(2,1)S(1)} %get-tuple-element.65), channel_id=1, source_target_pairs={{0,1},{1,0},{2,3},{3,2},{4,5},{5,4},{6,7},{7,6},{8,9},{9,8},{10,11... | collective-permute-start | bytes 1720328 | tf_op jit(solution)/shard_map/ppermute | solution.py:642
  32.8 8.8 %collective-permute-start.9 = (bf16[256,256]{1,0:T(8,128)(2,1)S(1)}, bf16[256,256]{1,0:T(8,128)(2,1)S(1)}, u32[]{:S(2)}, u32[]{:S(2)}) collective-permute-start(bf16[256,256]{1,0:T(8,128)(2,1)S(1)} %get-tuple-element.73), channel_id=1, source_target_pairs={{0,24},{8,16},{16,8},{24,0},{1,25},{9,17},{17,9},{25,1},{2,26},{10... | collective-permute-start | bytes 393224 | tf_op jit(solution)/shard_map/ppermute | solution.py:642
  35.0 7.4 %collective-permute-start.7 = (bf16[304,256]{1,0:T(8,128)(2,1)S(1)}, bf16[304,256]{1,0:T(8,128)(2,1)S(1)}, u32[]{:S(2)}, u32[]{:S(2)}) collective-permute-start(bf16[304,256]{1,0:T(8,128)(2,1)S(1)} %get-tuple-element.71), channel_id=1, source_target_pairs={{0,8},{8,0},{16,24},{24,16},{1,9},{9,1},{17,25},{25,17},{2,10},{10... | collective-permute-start | bytes 466952 | tf_op jit(solution)/shard_map/ppermute | solution.py:642
  35.3 7.6 %collective-permute-start.8 = (bf16[304,256]{1,0:T(8,128)(2,1)S(1)}, bf16[304,256]{1,0:T(8,128)(2,1)S(1)}, u32[]{:S(2)}, u32[]{:S(2)}) collective-permute-start(bf16[304,256]{1,0:T(8,128)(2,1)S(1)} %get-tuple-element.72), channel_id=1, source_target_pairs={{0,16},{8,24},{16,0},{24,8},{1,17},{9,25},{17,1},{25,9},{2,18},{10... | collective-permute-start | bytes 466952 | tf_op jit(solution)/shard_map/ppermute | solution.py:642
  36.4 2.0 %copy-start.1 = (f32[4256,128]{1,0:T(8,128)S(1)}, f32[4256,128]{1,0:T(8,128)}, u32[]{:S(2)}) copy-start(f32[4256,128]{1,0:T(8,128)} %get-tuple-element.74.refs_1_) | copy-start | bytes 6537220
  43.0 7.5 %collective-permute-start.12 = (bf16[160,256]{1,0:T(8,128)(2,1)S(1)}, bf16[160,256]{1,0:T(8,128)(2,1)S(1)}, u32[]{:S(2)}, u32[]{:S(2)}) collective-permute-start(bf16[160,256]{1,0:T(8,128)(2,1)S(1)} %get-tuple-element.80), channel_id=1, source_target_pairs={{0,6},{1,7},{2,4},{3,5},{4,2},{5,3},{6,0},{7,1},{8,14},{9,15},{10,... | collective-permute-start | bytes 245768 | tf_op jit(solution)/shard_map/ppermute | solution.py:642
  45.5 5.1 %collective-permute-start.10 = (bf16[64,256]{1,0:T(8,128)(2,1)S(1)}, bf16[64,256]{1,0:T(8,128)(2,1)S(1)}, u32[]{:S(2)}, u32[]{:S(2)}) collective-permute-start(bf16[64,256]{1,0:T(8,128)(2,1)S(1)} %get-tuple-element.78), channel_id=1, source_target_pairs={{0,2},{1,3},{2,0},{3,1},{4,6},{5,7},{6,4},{7,5},{8,10},{9,11},{10,... | collective-permute-start | bytes 98312 | tf_op jit(solution)/shard_map/ppermute | solution.py:642
  45.5 5.1 %collective-permute-start.11 = (bf16[64,256]{1,0:T(8,128)(2,1)S(1)}, bf16[64,256]{1,0:T(8,128)(2,1)S(1)}, u32[]{:S(2)}, u32[]{:S(2)}) collective-permute-start(bf16[64,256]{1,0:T(8,128)(2,1)S(1)} %get-tuple-element.79), channel_id=1, source_target_pairs={{0,4},{1,5},{2,6},{3,7},{4,0},{5,1},{6,2},{7,3},{8,12},{9,13},{10,... | collective-permute-start | bytes 98312 | tf_op jit(solution)/shard_map/ppermute | solution.py:642
  50.6 6.7 %collective-permute-start.15 = (bf16[128,256]{1,0:T(8,128)(2,1)S(1)}, bf16[128,256]{1,0:T(8,128)(2,1)S(1)}, u32[]{:S(2)}, u32[]{:S(2)}) collective-permute-start(bf16[128,256]{1,0:T(8,128)(2,1)S(1)} %shard_map.180.refs_0_), channel_id=1, source_target_pairs={{0,6},{1,7},{2,4},{3,5},{4,2},{5,3},{6,0},{7,1},{8,14},{9,15},{10,... | collective-permute-start | bytes 196616 | tf_op jit(solution)/shard_map/ppermute | solution.py:642
  53.1 6.3 %collective-permute-start.14 = (bf16[128,256]{1,0:T(8,128)(2,1)S(1)}, bf16[128,256]{1,0:T(8,128)(2,1)S(1)}, u32[]{:S(2)}, u32[]{:S(2)}) collective-permute-start(bf16[128,256]{1,0:T(8,128)(2,1)S(1)} %shard_map.180.refs_0_), channel_id=1, source_target_pairs={{0,4},{1,5},{2,6},{3,7},{4,0},{5,1},{6,2},{7,3},{8,12},{9,13},{10,... | collective-permute-start | bytes 196616 | tf_op jit(solution)/shard_map/ppermute | solution.py:642
  53.9 5.6 %collective-permute-start.13 = (bf16[128,256]{1,0:T(8,128)(2,1)S(1)}, bf16[128,256]{1,0:T(8,128)(2,1)S(1)}, u32[]{:S(2)}, u32[]{:S(2)}) collective-permute-start(bf16[128,256]{1,0:T(8,128)(2,1)S(1)} %shard_map.180.refs_0_), channel_id=1, source_target_pairs={{0,2},{1,3},{2,0},{3,1},{4,6},{5,7},{6,4},{7,5},{8,10},{9,11},{10,... | collective-permute-start | bytes 196616 | tf_op jit(solution)/shard_map/ppermute | solution.py:642
  56.0 9.1 %collective-permute-start.16 = (bf16[2,3,128,128]{3,2,1,0:T(8,128)(2,1)S(1)}, bf16[2,3,128,128]{3,2,1,0:T(8,128)(2,1)S(1)}, u32[]{:S(2)}, u32[]{:S(2)}) collective-permute-start(bf16[2,3,128,128]{3,2,1,0:T(8,128)(2,1)S(1)} %get-tuple-element.88), channel_id=1, source_target_pairs={{0,1},{1,0},{2,3},{3,2},{4,5},{5,4},{6,7},{7,6},{8,9},{9,8},{10,11... | collective-permute-start | bytes 589832 | tf_op jit(solution)/shard_map/ppermute | solution.py:642
  56.0 9.1 %collective-permute-start.17 = (bf16[2,3,128,128]{3,2,1,0:T(8,128)(2,1)S(1)}, bf16[2,3,128,128]{3,2,1,0:T(8,128)(2,1)S(1)}, u32[]{:S(2)}, u32[]{:S(2)}) collective-permute-start(bf16[2,3,128,128]{3,2,1,0:T(8,128)(2,1)S(1)} %get-tuple-element.89), channel_id=1, source_target_pairs={{1,2},{3,4},{5,6},{2,1},{4,3},{6,5},{9,10},{11,12},{13,14},{10,9},... | collective-permute-start | bytes 589832 | tf_op jit(solution)/shard_map/ppermute | solution.py:625
  59.5 7.7 %collective-permute-start.20 = (bf16[320,256]{1,0:T(8,128)(2,1)S(1)}, bf16[320,256]{1,0:T(8,128)(2,1)S(1)}, u32[]{:S(2)}, u32[]{:S(2)}) collective-permute-start(bf16[320,256]{1,0:T(8,128)(2,1)S(1)} %shard_map.182.refs_2_.refs_0_), channel_id=1, source_target_pairs={{0,24},{8,16},{16,8},{24,0},{1,25},{9,17},{17,9},{25,1},{2,26},{10... | collective-permute-start | bytes 491528 | tf_op jit(solution)/shard_map/ppermute | solution.py:642
  61.6 8.0 %collective-permute-start.19 = (bf16[320,256]{1,0:T(8,128)(2,1)S(1)}, bf16[320,256]{1,0:T(8,128)(2,1)S(1)}, u32[]{:S(2)}, u32[]{:S(2)}) collective-permute-start(bf16[320,256]{1,0:T(8,128)(2,1)S(1)} %shard_map.182.refs_2_.refs_0_), channel_id=1, source_target_pairs={{0,16},{8,24},{16,0},{24,8},{1,17},{9,25},{17,1},{25,9},{2,18},{10... | collective-permute-start | bytes 491528 | tf_op jit(solution)/shard_map/ppermute | solution.py:642
  61.9 7.7 %collective-permute-start.18 = (bf16[320,256]{1,0:T(8,128)(2,1)S(1)}, bf16[320,256]{1,0:T(8,128)(2,1)S(1)}, u32[]{:S(2)}, u32[]{:S(2)}) collective-permute-start(bf16[320,256]{1,0:T(8,128)(2,1)S(1)} %shard_map.182.refs_2_.refs_0_), channel_id=1, source_target_pairs={{0,8},{8,0},{16,24},{24,16},{1,9},{9,1},{17,25},{25,17},{2,10},{10... | collective-permute-start | bytes 491528 | tf_op jit(solution)/shard_map/ppermute | solution.py:642
  69.6 2.0 %collective-permute-start.21 = (bf16[1088,256]{1,0:T(8,128)(2,1)S(1)}, bf16[1088,256]{1,0:T(8,128)(2,1)S(1)}, u32[]{:S(2)}, u32[]{:S(2)}) collective-permute-start(bf16[1088,256]{1,0:T(8,128)(2,1)S(1)} %shard_map.185.refs_0_), channel_id=1, source_target_pairs={{0,1},{1,0},{2,3},{3,2},{4,5},{5,4},{6,7},{7,6},{8,9},{9,8},{10,11... | collective-permute-start | bytes 1671176 | tf_op jit(solution)/shard_map/ppermute | solution.py:642

commit v5 on v4

--- a/solution.py
+++ b/solution.py
@@ -291,9 +291,9 @@
                 1.0 + (1.0 - half) * (v * (2 * ROOT_COEF + 6 * ROOT_COEF * CUBIC_COEF * v2))
             )
             d_act = dot(g_branch, w2[hid, :], ((1,), (1,)))
-            g_pre = (d_act * slope).astype(BF16)
-            pre[pl.ds(at, step), hid] = g_pre
-            bias_out[:, hid] += jnp.sum(g_pre.astype(F32), axis=0, keepdims=True)
+            g_pre = d_act * slope
+            pre[pl.ds(at, step), hid] = g_pre.astype(BF16)
+            bias_out[:, hid] += jnp.sum(g_pre, axis=0, keepdims=True)
         branch = dot(act[pl.ds(at, step), :], w2[...], ((1,), (0,))) + bias2
         residual = band[pl.ds(2 * m, 2)].reshape(step, channels).astype(F32)
         result[pl.ds(2 * m, 2)] = (
@@ -753,7 +753,7 @@
     )
 
     face_masks = list(range(faces - 1, 0, -1))
-    chip_masks = list(range(2, tiles, 2))
+    chip_masks = list(range(tiles - 2, 0, -2))
     half, mirror = faces // 2, tiles - 2
     peer = swapped(other, "tile", 1)
     count = hidden // faces

time: 73.4 us -> 73.6 us (level)
  transfers between devices with their start and end apart: 22 -> 22, of which waited for: 10 -> 11; matrix products, arithmetic and copies ran while one was open for 0% -> 0% of each run, Pallas kernels for 22% -> 22%
where the time goes in v5:
time: 73.6 us; the launch traced here: 73.4 us
  starting transfers between devices  31.4 us (43%)
  Pallas kernels  27.1 us (37%)
  waiting for transfers between devices  12.8 us (17%)
  local copies, waits for them, and re-layouts  1.22 us (2%)
  between operations  0.92 us (1%)
    pallas_call x16, Pallas kernels, call(): pl.pallas_call(run, out_shape=outs, in_specs=[vmem] * (count - smem) + [s...  27.1 us
    ppermute x16, starting transfers between devices, swapped(): lax.ppermute(x, axis, [(i, i ^ mask) for i in range(lax.axis_size(axis))])  22.3 us
    ppermute x16, waiting for transfers between devices, swapped(): lax.ppermute(x, axis, [(i, i ^ mask) for i in range(lax.axis_size(axis))])  11.5 us
    ppermute x4, starting transfers between devices, face_swap(): return lax.ppermute(x, ('face', 'tile'), pairs)  7.76 us
  transfers between devices with their start and end apart: 22, of which 11 were waited for; matrix products, arithmetic and copies ran while one was open for 0% of the time, Pallas kernels for 22%

profile of v5, /device:TPU:0, one launch (start us, length us, event | category | flops | bytes accessed | tf_op | source)
XLA Modules:
  0.0 73.4 jit_solution(5187467135058472569)
XLA Ops:
  0.6 0.0 copy-start.3
  0.6 1.0 %copy-done.3 = bf16[1,8,128,256]{3,2,1,0:T(8,128)(2,1)S(1)} copy-done((bf16[1,8,128,256]{3,2,1,0:T(8,128)(2,1)S(1)}, bf16[1,8,128,256]{3,2,1,0:T(8,128)(2,1)}, u32[]{:S(2)}) %copy-start.3) | copy-done | bytes 524312
  1.7 0.5 collective-permute-start
  2.2 0.7 collective-permute-start.1
  2.9 0.1 copy.19.refs_3_
  3.0 0.3 collective-permute-done.refs_1_
  3.3 0.7 shard_map.172
  4.0 5.7 %collective-permute-start.3 = (bf16[48,256]{1,0:T(8,128)(2,1)S(1)}, bf16[48,256]{1,0:T(8,128)(2,1)S(1)}, u32[]{:S(2)}, u32[]{:S(2)}) collective-permute-start(bf16[48,256]{1,0:T(8,128)(2,1)S(1)} %get-tuple-element.56), channel_id=1, source_target_pairs={{0,15},{1,14},{2,13},{3,12},{4,11},{5,10},{6,9},{7,8},{8,7},{9,6},... | collective-permute-start | bytes 73736 | tf_op jit(solution)/shard_map/ppermute | solution.py:606
  9.7 1.5 %collective-permute-start.4 = (bf16[48,256]{1,0:T(8,128)(2,1)S(1)}, bf16[48,256]{1,0:T(8,128)(2,1)S(1)}, u32[]{:S(2)}, u32[]{:S(2)}) collective-permute-start(bf16[48,256]{1,0:T(8,128)(2,1)S(1)} %get-tuple-element.57), channel_id=1, source_target_pairs={{0,16},{1,17},{2,18},{3,19},{4,20},{5,21},{6,22},{7,23},{8,24},{9,... | collective-permute-start | bytes 73736 | tf_op jit(solution)/shard_map/ppermute | solution.py:606
  11.2 0.5 collective-permute-start.2
  11.8 0.0 copy-start.8
  11.8 0.0 copy-start.10
  11.9 0.0 copy-start.13
  11.9 4.1 %shard_map.173 = (f32[2176,128]{1,0:T(8,128)S(1)}, f32[2,50,8,128]{3,2,1,0:T(8,128)S(1)}) custom-call(bf16[8,128,256]{2,1,0:T(8,128)(2,1)S(1)} %bitcast.14, bf16[7,7,256]{2,1,0:T(8,128)(2,1)S(1)} %copy-done.7, f32[1,256]{1,0:T(1,128)S(1)} %bitcast.17, bf16[48,256]{1,0:T(8,128)(2,1)S(1)} %get-tuple-element.55.refs_3_), custom_call_target="tpu_custom_call" | custom-call | flops 4499999744 | bytes 1048576 | tf_op jit(solution)/shard_map/pallas_call | solution.py:35
  16.0 1.3 %collective-permute-done.5.refs_6_ = bf16[48,256]{1,0:T(8,128)(2,1)S(1)} collective-permute-done((bf16[48,256]{1,0:T(8,128)(2,1)S(1)}, bf16[48,256]{1,0:T(8,128)(2,1)S(1)}, u32[]{:S(2)}, u32[]{:S(2)}) %collective-permute-start.5) | collective-permute-done | bytes 24608 | tf_op jit(solution)/shard_map/ppermute | solution.py:606
  17.4 8.0 %shard_map.174 = (bf16[8,128,256]{2,1,0:T(8,128)(2,1)}, f32[4256,128]{1,0:T(8,128)}, f32[2312,128]{1,0:T(8,128)}, f32[1024,256]{1,0:T(8,128)S(1)}, bf16[1120,256...) custom-call(bf16[8,128,256]{2,1,0:T(8,128)(2,1)S(1)} %bitcast.15, ...), custom_call_target="tpu_custom_call" | custom-call | flops 12000000000 | bytes 1048576 | tf_op jit(solution)/shard_map/pallas_call | solution.py:35
  25.4 5.6 %collective-permute-start.6 = (bf16[1120,256]{1,0:T(8,128)(2,1)S(1)}, bf16[1120,256]{1,0:T(8,128)(2,1)S(1)}, u32[]{:S(2)}, u32[]{:S(2)}) collective-permute-start(bf16[1120,256]{1,0:T(8,128)(2,1)S(1)} %get-tuple-element.65), channel_id=1, source_target_pairs={{0,1},{1,0},{2,3},{3,2},{4,5},{5,4},{6,7},{7,6},{8,9},{9,8},{10,11... | collective-permute-start | bytes 1720328 | tf_op jit(solution)/shard_map/ppermute | solution.py:642
  31.0 1.6 %collective-permute-done.6.refs_1_ = bf16[1120,256]{1,0:T(8,128)(2,1)S(1)} collective-permute-done((bf16[1120,256]{1,0:T(8,128)(2,1)S(1)}, bf16[1120,256]{1,0:T(8,128)(2,1)S(1)}, u32[]{:S(2)}, u32[]{:S(2)}) %collective-permute-start.6) | collective-permute-done | bytes 573472 | tf_op jit(solution)/shard_map/ppermute | solution.py:642
  32.6 0.1 shard_map.175
  32.7 2.2 %collective-permute-start.9 = (bf16[256,256]{1,0:T(8,128)(2,1)S(1)}, bf16[256,256]{1,0:T(8,128)(2,1)S(1)}, u32[]{:S(2)}, u32[]{:S(2)}) collective-permute-start(bf16[256,256]{1,0:T(8,128)(2,1)S(1)} %get-tuple-element.73), channel_id=1, source_target_pairs={{0,24},{8,16},{16,8},{24,0},{1,25},{9,17},{17,9},{25,1},{2,26},{10... | collective-permute-start | bytes 393224 | tf_op jit(solution)/shard_map/ppermute | solution.py:642
  34.9 0.3 collective-permute-start.7
  35.2 1.1 %collective-permute-start.8 = (bf16[304,256]{1,0:T(8,128)(2,1)S(1)}, bf16[304,256]{1,0:T(8,128)(2,1)S(1)}, u32[]{:S(2)}, u32[]{:S(2)}) collective-permute-start(bf16[304,256]{1,0:T(8,128)(2,1)S(1)} %get-tuple-element.72), channel_id=1, source_target_pairs={{0,16},{8,24},{16,0},{24,8},{1,17},{9,25},{17,1},{25,9},{2,18},{10... | collective-permute-start | bytes 466952 | tf_op jit(solution)/shard_map/ppermute | solution.py:642
  36.3 2.0 %shard_map.176 = (f32[1088,128]{1,0:T(8,128)S(1)}, f32[8,128]{1,0:T(8,128)S(1)}) custom-call(f32[2312,128]{1,0:T(8,128)S(1)} %copy-done, f32[2,50,8,128]{3,2,1,0:T(8,128)S(1)} %get-tuple-element.59.refs_8_.refs_1_, f32[8,128]{1,0:T(8,128)S(1)} %get-tuple-element.68.refs_2_), custom_call_target="tpu_custom_call" | custom-call | flops 2100000000 | bytes 1048576 | tf_op jit(solution)/shard_map/pallas_call | solution.py:35
  38.3 3.2 %shard_map.177 = (f32[56,128]{1,0:T(8,128)S(1)}, f32[8,128]{1,0:T(8,128)S(1)}) custom-call(f32[2312,128]{1,0:T(8,128)S(1)} %copy-done, f32[4256,128]{1,0:T(8,128)S(1)} %copy-done.1, f32[8,128]{1,0:T(8,128)S(1)} %get-tuple-element.75.refs_2_), custom_call_target="tpu_custom_call" | custom-call | flops 3500000000 | bytes 1048576 | tf_op jit(solution)/shard_map/pallas_call | solution.py:35
  41.6 0.7 collective-permute-done.7.refs_1_
  42.3 0.5 collective-permute-done.8.refs_2_
  42.8 0.1 shard_map.178
  42.9 2.5 %collective-permute-start.10 = (bf16[160,256]{1,0:T(8,128)(2,1)S(1)}, bf16[160,256]{1,0:T(8,128)(2,1)S(1)}, u32[]{:S(2)}, u32[]{:S(2)}) collective-permute-start(bf16[160,256]{1,0:T(8,128)(2,1)S(1)} %get-tuple-element.78), channel_id=1, source_target_pairs={{0,6},{1,7},{2,4},{3,5},{4,2},{5,3},{6,0},{7,1},{8,14},{9,15},{10,... | collective-permute-start | bytes 245768 | tf_op jit(solution)/shard_map/ppermute | solution.py:642
  45.4 2.0 %collective-permute-start.12 = (bf16[64,256]{1,0:T(8,128)(2,1)S(1)}, bf16[64,256]{1,0:T(8,128)(2,1)S(1)}, u32[]{:S(2)}, u32[]{:S(2)}) collective-permute-start(bf16[64,256]{1,0:T(8,128)(2,1)S(1)} %get-tuple-element.80), channel_id=1, source_target_pairs={{0,2},{1,3},{2,0},{3,1},{4,6},{5,7},{6,4},{7,5},{8,10},{9,11},{10,... | collective-permute-start | bytes 98312 | tf_op jit(solution)/shard_map/ppermute | solution.py:642
  47.4 3.1 %shard_map.179 = (f32[56,128]{1,0:T(8,128)S(1)}, f32[8,128]{1,0:T(8,128)}) custom-call(f32[2312,128]{1,0:T(8,128)S(1)} %copy-done, f32[4256,128]{1,0:T(8,128)S(1)} %copy-done.1, f32[8,128]{1,0:T(8,128)S(1)} %get-tuple-element.82.refs_2_), custom_call_target="tpu_custom_call" | custom-call | flops 300000000 | bytes 1048576 | tf_op jit(solution)/shard_map/pallas_call | solution.py:35
  50.5 0.1 collective-permute-done.11.refs_2_
  50.6 2.4 %collective-permute-start.15 = (bf16[128,256]{1,0:T(8,128)(2,1)S(1)}, bf16[128,256]{1,0:T(8,128)(2,1)S(1)}, u32[]{:S(2)}, u32[]{:S(2)}) collective-permute-start(bf16[128,256]{1,0:T(8,128)(2,1)S(1)} %shard_map.180.refs_0_), channel_id=1, source_target_pairs={{0,6},{1,7},{2,4},{3,5},{4,2},{5,3},{6,0},{7,1},{8,14},{9,15},{10,... | collective-permute-start | bytes 196616 | tf_op jit(solution)/shard_map/ppermute | solution.py:642
  53.0 2.0 %collective-permute-start.13 = (bf16[128,256]{1,0:T(8,128)(2,1)S(1)}, bf16[128,256]{1,0:T(8,128)(2,1)S(1)}, u32[]{:S(2)}, u32[]{:S(2)}) collective-permute-start(bf16[128,256]{1,0:T(8,128)(2,1)S(1)} %shard_map.180.refs_0_), channel_id=1, source_target_pairs={{0,2},{1,3},{2,0},{3,1},{4,6},{5,7},{6,4},{7,5},{8,10},{9,11},{10,... | collective-permute-start | bytes 196616 | tf_op jit(solution)/shard_map/ppermute | solution.py:642
  55.1 0.9 %shard_map.181 = (bf16[2,3,128,128]{3,2,1,0:T(8,128)(2,1)S(1)}, bf16[2,3,128,128]{3,2,1,0:T(8,128)(2,1)S(1)}, f32[8,128]{1,0:T(8,128)S(1)}) custom-call(f32[2312,128]{1,0:T(8,128)S(1)} %copy-done, f32[2,50,8,128]{3,2,1,0:T(8,128)S(1)} %get-tuple-element.59.refs_8_.refs_1_, bf16[48,256]{1,0:T(8,128)(2,1)S(1)} %slice.21.refs_2_.refs_4_, ...), custom_call_target="tpu_custom_call" | custom-call | flops 900000000 | bytes 1048576 | tf_op jit(solution)/shard_map/pallas_call | solution.py:35
  55.9 0.1 collective-permute-start.16
  56.0 0.7 collective-permute-start.17
  56.7 0.8 %collective-permute-done.15.refs_3_ = bf16[128,256]{1,0:T(8,128)(2,1)S(1)} collective-permute-done((bf16[128,256]{1,0:T(8,128)(2,1)S(1)}, bf16[128,256]{1,0:T(8,128)(2,1)S(1)}, u32[]{:S(2)}, u32[]{:S(2)}) %collective-permute-start.15) | collective-permute-done | bytes 65568 | tf_op jit(solution)/shard_map/ppermute | solution.py:642
  57.5 1.8 %collective-permute-done.14.refs_2_ = bf16[128,256]{1,0:T(8,128)(2,1)S(1)} collective-permute-done((bf16[128,256]{1,0:T(8,128)(2,1)S(1)}, bf16[128,256]{1,0:T(8,128)(2,1)S(1)}, u32[]{:S(2)}, u32[]{:S(2)}) %collective-permute-start.14) | collective-permute-done | bytes 65568 | tf_op jit(solution)/shard_map/ppermute | solution.py:642
  59.3 2.4 %collective-permute-start.20 = (bf16[320,256]{1,0:T(8,128)(2,1)S(1)}, bf16[320,256]{1,0:T(8,128)(2,1)S(1)}, u32[]{:S(2)}, u32[]{:S(2)}) collective-permute-start(bf16[320,256]{1,0:T(8,128)(2,1)S(1)} %shard_map.182.refs_2_.refs_0_), channel_id=1, source_target_pairs={{0,24},{8,16},{16,8},{24,0},{1,25},{9,17},{17,9},{25,1},{2,26},{10... | collective-permute-start | bytes 491528 | tf_op jit(solution)/shard_map/ppermute | solution.py:642
  61.7 0.3 collective-permute-start.19
  62.0 0.9 %collective-permute-start.18 = (bf16[320,256]{1,0:T(8,128)(2,1)S(1)}, bf16[320,256]{1,0:T(8,128)(2,1)S(1)}, u32[]{:S(2)}, u32[]{:S(2)}) collective-permute-start(bf16[320,256]{1,0:T(8,128)(2,1)S(1)} %shard_map.182.refs_2_.refs_0_), channel_id=1, source_target_pairs={{0,8},{8,0},{16,24},{24,16},{1,9},{9,1},{17,25},{25,17},{2,10},{10... | collective-permute-start | bytes 491528 | tf_op jit(solution)/shard_map/ppermute | solution.py:642
  62.9 2.0 %shard_map.183 = (f32[1088,128]{1,0:T(8,128)S(1)}, f32[8,128]{1,0:T(8,128)}) custom-call(f32[2312,128]{1,0:T(8,128)S(1)} %copy-done, f32[2,50,8,128]{3,2,1,0:T(8,128)S(1)} %get-tuple-element.59.refs_8_.refs_1_, bf16[320,256]{1,0:T(8,128)(2,1)S(1)} %shard_map.182.refs_2_.refs_0_), custom_call_target="tpu_custom_call" | custom-call | flops 200000000 | bytes 1048576 | tf_op jit(solution)/shard_map/pallas_call | solution.py:35
  64.9 1.1 %shard_map.184 = (bf16[8,128,256]{2,1,0:T(8,128)(2,1)}, f32[8,128]{1,0:T(8,128)S(1)}) custom-call(f32[1088,128]{1,0:T(8,128)S(1)} %get-tuple-element.69.refs_0_, f32[1088,128]{1,0:T(8,128)S(1)} %get-tuple-element.87.refs_1_, bf16[2,3,128,128]{3,2,1,0:T(8,128)(2,1)S(1)} %collective-permute-done.16.refs_2_, ...), custom_call_target="tpu_custom_call" | custom-call | flops 200000000 | bytes 1048576 | tf_op jit(solution)/shard_map/pallas_call | solution.py:35
  66.1 1.3 %collective-permute-done.20.refs_3_ = bf16[320,256]{1,0:T(8,128)(2,1)S(1)} collective-permute-done((bf16[320,256]{1,0:T(8,128)(2,1)S(1)}, bf16[320,256]{1,0:T(8,128)(2,1)S(1)}, u32[]{:S(2)}, u32[]{:S(2)}) %collective-permute-start.20) | collective-permute-done | bytes 163872 | tf_op jit(solution)/shard_map/ppermute | solution.py:642
  67.4 2.4 %collective-permute-done.19.refs_2_ = bf16[320,256]{1,0:T(8,128)(2,1)S(1)} collective-permute-done((bf16[320,256]{1,0:T(8,128)(2,1)S(1)}, bf16[320,256]{1,0:T(8,128)(2,1)S(1)}, u32[]{:S(2)}, u32[]{:S(2)}) %collective-permute-start.19) | collective-permute-done | bytes 163872 | tf_op jit(solution)/shard_map/ppermute | solution.py:642
  69.8 0.1 collective-permute-start.21
  69.9 1.9 %collective-permute-done.21.refs_1_ = bf16[1088,256]{1,0:T(8,128)(2,1)S(1)} collective-permute-done((bf16[1088,256]{1,0:T(8,128)(2,1)S(1)}, bf16[1088,256]{1,0:T(8,128)(2,1)S(1)}, u32[]{:S(2)}, u32[]{:S(2)}) %collective-permute-start.21) | collective-permute-done | bytes 557088 | tf_op jit(solution)/shard_map/ppermute | solution.py:642
  71.8 1.6 %shard_map.186 = (f32[256,1024]{1,0:T(8,128)}, f32[1024,256]{1,0:T(8,128)}, f32[7,7,256]{2,1,0:T(8,128)}, f32[1,1024]{1,0:T(1,128)}, f32[5,256]{1,0:T(8,128)}) custom-call(bf16[1088,256]{1,0:T(8,128)(2,1)S(1)} %shard_map.185.refs_0_, bf16[1088,256]{1,0:T(8,128)(2,1)S(1)} %collective-permute-done.21.refs_1_), custom_call_target="tpu_custom_call" | custom-call | flops 2000000000 | bytes 1048576 | tf_op jit(solution)/shard_map/pallas_call | solution.py:35
  (47 shorter events, 0.2 us)
Async XLA Ops:
  0.6 1.0 %copy-start.3 = (bf16[1,8,128,256]{3,2,1,0:T(8,128)(2,1)S(1)}, bf16[1,8,128,256]{3,2,1,0:T(8,128)(2,1)}, u32[]{:S(2)}) copy-start(bf16[1,8,128,256]{3,2,1,0:T(8,128)(2,1)} %param.12) | copy-start | bytes 1572868
  1.7 1.2 %copy-start.14 = (s32[4,2,3]{0,1,2:T(2,128)S(1)}, s32[4,2,3]{0,1,2:T(2,128)}, u32[]{:S(2)}) copy-start(s32[4,2,3]{0,1,2:T(2,128)} %param.14) | copy-start | bytes 292
  1.7 1.6 %collective-permute-start = (bf16[3,128,256]{2,1,0:T(8,128)(2,1)S(1)}, bf16[3,128,256]{2,1,0:T(8,128)(2,1)S(1)}, u32[]{:S(2)}, u32[]{:S(2)}) collective-permute-start(bf16[3,128,256]{2,1,0:T(8,128)(2,1)S(1)} %get-tuple-element.52), channel_id=1, source_target_pairs={{0,1},{1,0},{2,3},{3,2},{4,5},{5,4},{6,7},{7,6},{8,9},{9,8},{10,11... | collective-permute-start | bytes 589832 | tf_op jit(solution)/shard_map/ppermute | solution.py:642
  2.2 1.1 %collective-permute-start.1 = (bf16[3,128,256]{2,1,0:T(8,128)(2,1)S(1)}, bf16[3,128,256]{2,1,0:T(8,128)(2,1)S(1)}, u32[]{:S(2)}, u32[]{:S(2)}) collective-permute-start(bf16[3,128,256]{2,1,0:T(8,128)(2,1)S(1)} %get-tuple-element.53), channel_id=1, source_target_pairs={{1,2},{3,4},{5,6},{2,1},{4,3},{6,5},{9,10},{11,12},{13,14},{10,9},... | collective-permute-start | bytes 589832 | tf_op jit(solution)/shard_map/ppermute | solution.py:625
  3.3 8.5 %copy-start.4 = (bf16[1,8,128,256]{3,2,1,0:T(8,128)(2,1)S(1)}, bf16[1,8,128,256]{3,2,1,0:T(8,128)(2,1)}, u32[]{:S(2)}) copy-start(bf16[1,8,128,256]{3,2,1,0:T(8,128)(2,1)} %param.12) | copy-start | bytes 1572868
  3.3 8.5 %copy-start.7 = (bf16[7,7,256]{2,1,0:T(8,128)(2,1)S(1)}, bf16[7,7,256]{2,1,0:T(8,128)(2,1)}, u32[]{:S(2)}) copy-start(bf16[7,7,256]{2,1,0:T(8,128)(2,1)} %refs_1_.1) | copy-start | bytes 75268
  3.3 8.5 %copy-start.9 = (f32[256]{0:T(256)S(1)}, f32[256]{0:T(256)}, u32[]{:S(2)}) copy-start(f32[256]{0:T(256)} %param.16) | copy-start | bytes 3076
  4.0 12.0 %collective-permute-start.3 = (bf16[48,256]{1,0:T(8,128)(2,1)S(1)}, bf16[48,256]{1,0:T(8,128)(2,1)S(1)}, u32[]{:S(2)}, u32[]{:S(2)}) collective-permute-start(bf16[48,256]{1,0:T(8,128)(2,1)S(1)} %get-tuple-element.56), channel_id=1, source_target_pairs={{0,15},{1,14},{2,13},{3,12},{4,11},{5,10},{6,9},{7,8},{8,7},{9,6},... | collective-permute-start | bytes 73736 | tf_op jit(solution)/shard_map/ppermute | solution.py:606
  9.7 6.3 %collective-permute-start.4 = (bf16[48,256]{1,0:T(8,128)(2,1)S(1)}, bf16[48,256]{1,0:T(8,128)(2,1)S(1)}, u32[]{:S(2)}, u32[]{:S(2)}) collective-permute-start(bf16[48,256]{1,0:T(8,128)(2,1)S(1)} %get-tuple-element.57), channel_id=1, source_target_pairs={{0,16},{1,17},{2,18},{3,19},{4,20},{5,21},{6,22},{7,23},{8,24},{9,... | collective-permute-start | bytes 73736 | tf_op jit(solution)/shard_map/ppermute | solution.py:606
  11.2 6.0 %collective-permute-start.5 = (bf16[48,256]{1,0:T(8,128)(2,1)S(1)}, bf16[48,256]{1,0:T(8,128)(2,1)S(1)}, u32[]{:S(2)}, u32[]{:S(2)}) collective-permute-start(bf16[48,256]{1,0:T(8,128)(2,1)S(1)} %get-tuple-element.58), channel_id=1, source_target_pairs={{0,23},{1,22},{2,21},{3,20},{4,19},{5,18},{6,17},{7,16},{8,31},{9,... | collective-permute-start | bytes 73736 | tf_op jit(solution)/shard_map/ppermute | solution.py:606
  11.2 6.0 %collective-permute-start.2 = (bf16[48,256]{1,0:T(8,128)(2,1)S(1)}, bf16[48,256]{1,0:T(8,128)(2,1)S(1)}, u32[]{:S(2)}, u32[]{:S(2)}) collective-permute-start(bf16[48,256]{1,0:T(8,128)(2,1)S(1)} %get-tuple-element.55.refs_3_), channel_id=1, source_target_pairs={{0,8},{1,9},{2,10},{3,11},{4,12},{5,13},{6,14},{7,15},{8,0},{9,1},... | collective-permute-start | bytes 73736 | tf_op jit(solution)/shard_map/ppermute | solution.py:606
  11.8 5.5 %copy-start.2 = (bf16[1,8,128,256]{3,2,1,0:T(8,128)(2,1)S(1)}, bf16[1,8,128,256]{3,2,1,0:T(8,128)(2,1)}, u32[]{:S(2)}) copy-start(bf16[1,8,128,256]{3,2,1,0:T(8,128)(2,1)} %param.13) | copy-start | bytes 1572868
  11.8 5.5 %copy-start.5 = (bf16[256,1024]{1,0:T(8,128)(2,1)S(1)}, bf16[256,1024]{1,0:T(8,128)(2,1)}, u32[]{:S(2)}) copy-start(bf16[256,1024]{1,0:T(8,128)(2,1)} %refs_14_.1) | copy-start | bytes 1572868
  11.8 5.5 %copy-start.6 = (bf16[1024,256]{1,0:T(8,128)(2,1)S(1)}, bf16[1024,256]{1,0:T(8,128)(2,1)}, u32[]{:S(2)}) copy-start(bf16[1024,256]{1,0:T(8,128)(2,1)} %refs_15_.1) | copy-start | bytes 1572868
  11.8 5.5 %copy-start.8 = (f32[1024]{0:T(1024)S(1)}, f32[1024]{0:T(1024)}, u32[]{:S(2)}) copy-start(f32[1024]{0:T(1024)} %param.20) | copy-start | bytes 12292
  11.8 5.5 %copy-start.10 = (f32[256]{0:T(256)S(1)}, f32[256]{0:T(256)}, u32[]{:S(2)}) copy-start(f32[256]{0:T(256)} %param.17) | copy-start | bytes 3076
  11.8 5.5 %copy-start.11 = (f32[256]{0:T(256)S(1)}, f32[256]{0:T(256)}, u32[]{:S(2)}) copy-start(f32[256]{0:T(256)} %param.18) | copy-start | bytes 3076
  11.9 5.5 %copy-start.12 = (f32[256]{0:T(256)S(1)}, f32[256]{0:T(256)}, u32[]{:S(2)}) copy-start(f32[256]{0:T(256)} %param.22) | copy-start | bytes 3076
  11.9 5.5 %copy-start.13 = (f32[256]{0:T(256)S(1)}, f32[256]{0:T(256)}, u32[]{:S(2)}) copy-start(f32[256]{0:T(256)} %param.23) | copy-start | bytes 3076
  25.4 10.9 %copy-start = (f32[2312,128]{1,0:T(8,128)S(1)}, f32[2312,128]{1,0:T(8,128)}, u32[]{:S(2)}) copy-start(f32[2312,128]{1,0:T(8,128)} %get-tuple-element.63.refs_0_) | copy-start | bytes 3551236
  25.4 7.2 %collective-permute-start.6 = (bf16[1120,256]{1,0:T(8,128)(2,1)S(1)}, bf16[1120,256]{1,0:T(8,128)(2,1)S(1)}, u32[]{:S(2)}, u32[]{:S(2)}) collective-permute-start(bf16[1120,256]{1,0:T(8,128)(2,1)S(1)} %get-tuple-element.65), channel_id=1, source_target_pairs={{0,1},{1,0},{2,3},{3,2},{4,5},{5,4},{6,7},{7,6},{8,9},{9,8},{10,11... | collective-permute-start | bytes 1720328 | tf_op jit(solution)/shard_map/ppermute | solution.py:642
  32.7 8.8 %collective-permute-start.9 = (bf16[256,256]{1,0:T(8,128)(2,1)S(1)}, bf16[256,256]{1,0:T(8,128)(2,1)S(1)}, u32[]{:S(2)}, u32[]{:S(2)}) collective-permute-start(bf16[256,256]{1,0:T(8,128)(2,1)S(1)} %get-tuple-element.73), channel_id=1, source_target_pairs={{0,24},{8,16},{16,8},{24,0},{1,25},{9,17},{17,9},{25,1},{2,26},{10... | collective-permute-start | bytes 393224 | tf_op jit(solution)/shard_map/ppermute | solution.py:642
  34.9 7.4 %collective-permute-start.7 = (bf16[304,256]{1,0:T(8,128)(2,1)S(1)}, bf16[304,256]{1,0:T(8,128)(2,1)S(1)}, u32[]{:S(2)}, u32[]{:S(2)}) collective-permute-start(bf16[304,256]{1,0:T(8,128)(2,1)S(1)} %get-tuple-element.71), channel_id=1, source_target_pairs={{0,8},{8,0},{16,24},{24,16},{1,9},{9,1},{17,25},{25,17},{2,10},{10... | collective-permute-start | bytes 466952 | tf_op jit(solution)/shard_map/ppermute | solution.py:642
  35.2 7.6 %collective-permute-start.8 = (bf16[304,256]{1,0:T(8,128)(2,1)S(1)}, bf16[304,256]{1,0:T(8,128)(2,1)S(1)}, u32[]{:S(2)}, u32[]{:S(2)}) collective-permute-start(bf16[304,256]{1,0:T(8,128)(2,1)S(1)} %get-tuple-element.72), channel_id=1, source_target_pairs={{0,16},{8,24},{16,0},{24,8},{1,17},{9,25},{17,1},{25,9},{2,18},{10... | collective-permute-start | bytes 466952 | tf_op jit(solution)/shard_map/ppermute | solution.py:642
  36.3 2.0 %copy-start.1 = (f32[4256,128]{1,0:T(8,128)S(1)}, f32[4256,128]{1,0:T(8,128)}, u32[]{:S(2)}) copy-start(f32[4256,128]{1,0:T(8,128)} %get-tuple-element.74.refs_1_) | copy-start | bytes 6537220
  42.9 7.5 %collective-permute-start.10 = (bf16[160,256]{1,0:T(8,128)(2,1)S(1)}, bf16[160,256]{1,0:T(8,128)(2,1)S(1)}, u32[]{:S(2)}, u32[]{:S(2)}) collective-permute-start(bf16[160,256]{1,0:T(8,128)(2,1)S(1)} %get-tuple-element.78), channel_id=1, source_target_pairs={{0,6},{1,7},{2,4},{3,5},{4,2},{5,3},{6,0},{7,1},{8,14},{9,15},{10,... | collective-permute-start | bytes 245768 | tf_op jit(solution)/shard_map/ppermute | solution.py:642
  45.4 5.1 %collective-permute-start.11 = (bf16[64,256]{1,0:T(8,128)(2,1)S(1)}, bf16[64,256]{1,0:T(8,128)(2,1)S(1)}, u32[]{:S(2)}, u32[]{:S(2)}) collective-permute-start(bf16[64,256]{1,0:T(8,128)(2,1)S(1)} %get-tuple-element.79), channel_id=1, source_target_pairs={{0,4},{1,5},{2,6},{3,7},{4,0},{5,1},{6,2},{7,3},{8,12},{9,13},{10,... | collective-permute-start | bytes 98312 | tf_op jit(solution)/shard_map/ppermute | solution.py:642
  45.4 5.1 %collective-permute-start.12 = (bf16[64,256]{1,0:T(8,128)(2,1)S(1)}, bf16[64,256]{1,0:T(8,128)(2,1)S(1)}, u32[]{:S(2)}, u32[]{:S(2)}) collective-permute-start(bf16[64,256]{1,0:T(8,128)(2,1)S(1)} %get-tuple-element.80), channel_id=1, source_target_pairs={{0,2},{1,3},{2,0},{3,1},{4,6},{5,7},{6,4},{7,5},{8,10},{9,11},{10,... | collective-permute-start | bytes 98312 | tf_op jit(solution)/shard_map/ppermute | solution.py:642
  50.6 6.9 %collective-permute-start.15 = (bf16[128,256]{1,0:T(8,128)(2,1)S(1)}, bf16[128,256]{1,0:T(8,128)(2,1)S(1)}, u32[]{:S(2)}, u32[]{:S(2)}) collective-permute-start(bf16[128,256]{1,0:T(8,128)(2,1)S(1)} %shard_map.180.refs_0_), channel_id=1, source_target_pairs={{0,6},{1,7},{2,4},{3,5},{4,2},{5,3},{6,0},{7,1},{8,14},{9,15},{10,... | collective-permute-start | bytes 196616 | tf_op jit(solution)/shard_map/ppermute | solution.py:642
  53.0 6.3 %collective-permute-start.14 = (bf16[128,256]{1,0:T(8,128)(2,1)S(1)}, bf16[128,256]{1,0:T(8,128)(2,1)S(1)}, u32[]{:S(2)}, u32[]{:S(2)}) collective-permute-start(bf16[128,256]{1,0:T(8,128)(2,1)S(1)} %shard_map.180.refs_0_), channel_id=1, source_target_pairs={{0,4},{1,5},{2,6},{3,7},{4,0},{5,1},{6,2},{7,3},{8,12},{9,13},{10,... | collective-permute-start | bytes 196616 | tf_op jit(solution)/shard_map/ppermute | solution.py:642
  53.0 6.3 %collective-permute-start.13 = (bf16[128,256]{1,0:T(8,128)(2,1)S(1)}, bf16[128,256]{1,0:T(8,128)(2,1)S(1)}, u32[]{:S(2)}, u32[]{:S(2)}) collective-permute-start(bf16[128,256]{1,0:T(8,128)(2,1)S(1)} %shard_map.180.refs_0_), channel_id=1, source_target_pairs={{0,2},{1,3},{2,0},{3,1},{4,6},{5,7},{6,4},{7,5},{8,10},{9,11},{10,... | collective-permute-start | bytes 196616 | tf_op jit(solution)/shard_map/ppermute | solution.py:642
  55.9 9.0 %collective-permute-start.16 = (bf16[2,3,128,128]{3,2,1,0:T(8,128)(2,1)S(1)}, bf16[2,3,128,128]{3,2,1,0:T(8,128)(2,1)S(1)}, u32[]{:S(2)}, u32[]{:S(2)}) collective-permute-start(bf16[2,3,128,128]{3,2,1,0:T(8,128)(2,1)S(1)} %get-tuple-element.88), channel_id=1, source_target_pairs={{0,1},{1,0},{2,3},{3,2},{4,5},{5,4},{6,7},{7,6},{8,9},{9,8},{10,11... | collective-permute-start | bytes 589832 | tf_op jit(solution)/shard_map/ppermute | solution.py:642
  56.0 8.9 %collective-permute-start.17 = (bf16[2,3,128,128]{3,2,1,0:T(8,128)(2,1)S(1)}, bf16[2,3,128,128]{3,2,1,0:T(8,128)(2,1)S(1)}, u32[]{:S(2)}, u32[]{:S(2)}) collective-permute-start(bf16[2,3,128,128]{3,2,1,0:T(8,128)(2,1)S(1)} %get-tuple-element.89), channel_id=1, source_target_pairs={{1,2},{3,4},{5,6},{2,1},{4,3},{6,5},{9,10},{11,12},{13,14},{10,9},... | collective-permute-start | bytes 589832 | tf_op jit(solution)/shard_map/ppermute | solution.py:625
  59.3 8.1 %collective-permute-start.20 = (bf16[320,256]{1,0:T(8,128)(2,1)S(1)}, bf16[320,256]{1,0:T(8,128)(2,1)S(1)}, u32[]{:S(2)}, u32[]{:S(2)}) collective-permute-start(bf16[320,256]{1,0:T(8,128)(2,1)S(1)} %shard_map.182.refs_2_.refs_0_), channel_id=1, source_target_pairs={{0,24},{8,16},{16,8},{24,0},{1,25},{9,17},{17,9},{25,1},{2,26},{10... | collective-permute-start | bytes 491528 | tf_op jit(solution)/shard_map/ppermute | solution.py:642
  61.7 8.0 %collective-permute-start.19 = (bf16[320,256]{1,0:T(8,128)(2,1)S(1)}, bf16[320,256]{1,0:T(8,128)(2,1)S(1)}, u32[]{:S(2)}, u32[]{:S(2)}) collective-permute-start(bf16[320,256]{1,0:T(8,128)(2,1)S(1)} %shard_map.182.refs_2_.refs_0_), channel_id=1, source_target_pairs={{0,16},{8,24},{16,0},{24,8},{1,17},{9,25},{17,1},{25,9},{2,18},{10... | collective-permute-start | bytes 491528 | tf_op jit(solution)/shard_map/ppermute | solution.py:642
  62.0 7.7 %collective-permute-start.18 = (bf16[320,256]{1,0:T(8,128)(2,1)S(1)}, bf16[320,256]{1,0:T(8,128)(2,1)S(1)}, u32[]{:S(2)}, u32[]{:S(2)}) collective-permute-start(bf16[320,256]{1,0:T(8,128)(2,1)S(1)} %shard_map.182.refs_2_.refs_0_), channel_id=1, source_target_pairs={{0,8},{8,0},{16,24},{24,16},{1,9},{9,1},{17,25},{25,17},{2,10},{10... | collective-permute-start | bytes 491528 | tf_op jit(solution)/shard_map/ppermute | solution.py:642
  69.8 2.0 %collective-permute-start.21 = (bf16[1088,256]{1,0:T(8,128)(2,1)S(1)}, bf16[1088,256]{1,0:T(8,128)(2,1)S(1)}, u32[]{:S(2)}, u32[]{:S(2)}) collective-permute-start(bf16[1088,256]{1,0:T(8,128)(2,1)S(1)} %shard_map.185.refs_0_), channel_id=1, source_target_pairs={{0,1},{1,0},{2,3},{3,2},{4,5},{5,4},{6,7},{7,6},{8,9},{9,8},{10,11... | collective-permute-start | bytes 1671176 | tf_op jit(solution)/shard_map/ppermute | solution.py:642
